TPU v7x, 32 devices: a whole 2x2x4 slice. The times are simulated.
32 devices in a mesh: tok: 8 (over z, y), store: 4 (over x, core).
Axes of the slice: x: 2, y: 2, z: 4, core: 2. Of those that a mesh axis runs over, the one named last changes fastest.
Arguments:
- activations: bfloat16 [8, 256, 14336], P('store', 'tok'), may hold values from -6 to 6
- out_grads: bfloat16 [8, 256, 4096], P('store', 'tok'), may hold values from -6 to 6
- validity: int32 [8, 256], P('store', 'tok'), may hold values 0 or 1
- proj_in: bfloat16 [14336, 64], P('tok'), may hold values from -0.046875 to 0.046875
- proj_out: bfloat16 [4096, 64], P('tok'), may hold values from -0.09375 to 0.09375
- precond: bfloat16 [4096, 4096], P(('tok', 'store')), may hold values from -0.05 to 2.05, as said below
- queries: bfloat16 [256, 4096], P('store'), may hold values from -0.09375 to 0.09375
- store_rows: float32 [4096, 4096], P(('tok', 'store')), may hold values from -6 to 6
- plan: int32 [4, 32], P(None, ('tok', 'store')), may hold values 0 or 1
Outputs:
- scores: float32 [256, 4096], P(None, ('tok', 'store'))
- precond_docs: float32 [8, 4096], P('store', 'tok')
- doc_scores: float32 [256, 8], P('store')
Inputs may be any that keep to these rules, and one draw needn't show every extreme that they name: `precond`: symmetric positive definite. `validity`: 1 marks a real token. `plan`: 1 where the query block is scored against the store block.
All inputs are finite; a program needn't handle non-finite values. No bound on the sum of `validity` on one device may be relied on, other than what follows from the above.
Results may differ from a plain program's by a relative error of at most 0.0049.
Values may be sent and summed in bfloat16 or wider, within the bound.
No kernel may reach another device: no remote copies, remote signals or barrier semaphores. Data moves between devices by JAX's collectives and lax.ppermute only.
A program may use at most 64 MiB of HBM per device.

v0:
```python
import math

import jax
import jax.numpy as jnp
from jax import lax
from jax.sharding import PartitionSpec as P


def local(activations, out_grads, validity, proj_in, proj_out, precond, queries, store_rows, plan):
    tok_count = lax.axis_size("tok")
    store_count = lax.axis_size("store")
    doc_local = activations.shape[0]
    len_local = activations.shape[1]
    flat_acts = activations.reshape(doc_local * len_local, activations.shape[2])
    flat_grads = out_grads.reshape(doc_local * len_local, out_grads.shape[2])
    left_acc = jnp.dot(
        flat_acts,
        lax.all_gather(proj_in, "tok", axis=0, tiled=True),
        preferred_element_type=jnp.float32,
    )
    right_acc = jnp.dot(
        flat_grads,
        lax.all_gather(proj_out, "tok", axis=0, tiled=True),
        preferred_element_type=jnp.float32,
    )
    left_proj = left_acc.astype(jnp.bfloat16).reshape(doc_local, len_local, -1)
    right_proj = right_acc.astype(jnp.bfloat16).reshape(doc_local, len_local, -1)
    masked = right_proj.astype(jnp.float32) * validity.astype(jnp.float32)[:, :, None]
    norm_scale = 1.0 / math.sqrt(len_local * tok_count)
    partial_value = (
        jnp.einsum(
            "dpo,dpi->doi", masked, left_proj.astype(jnp.float32), precision=lax.Precision.HIGHEST
        ).reshape(doc_local, -1)
        * norm_scale
    )
    k_total = partial_value.shape[1]
    block_rows = precond.shape[0]
    blocks = partial_value.reshape(doc_local, tok_count, store_count, block_rows)
    moved = lax.all_to_all(
        lax.all_to_all(blocks, "tok", split_axis=1, concat_axis=1, tiled=True),
        "store",
        split_axis=2,
        concat_axis=0,
        tiled=True,
    )
    grad_block = jnp.sum(moved, axis=1).reshape(-1, block_rows).astype(jnp.bfloat16)
    partial_pre = jnp.dot(grad_block, precond, preferred_element_type=jnp.float32)
    full_pre = lax.psum(partial_pre, ("tok", "store"))
    cols_tok = k_total // tok_count
    precond_docs = lax.dynamic_slice(
        full_pre,
        (lax.axis_index("store") * doc_local, lax.axis_index("tok") * cols_tok),
        (doc_local, cols_tok),
    )
    doc_scores = lax.dot_general(
        queries.astype(jnp.float32),
        full_pre,
        (((1,), (1,)), ((), ())),
        precision=lax.Precision.HIGHEST,
    )
    query_dev = queries.shape[0]
    row_weights = plan.astype(jnp.float32)[:, 0]
    segment = lax.all_gather(queries, "store", axis=0, tiled=True)
    raw_scores = lax.dot_general(
        segment.astype(jnp.float32),
        store_rows,
        (((1,), (1,)), ((), ())),
        precision=lax.Precision.HIGHEST,
    )
    owners = lax.iota(jnp.int32, segment.shape[0]) // query_dev
    onehot = (owners[:, None] == lax.iota(jnp.int32, store_count)[None, :]).astype(jnp.float32)
    scores = raw_scores * jnp.dot(onehot, row_weights, precision=lax.Precision.HIGHEST)[:, None]
    return (scores, precond_docs, doc_scores)


def solution(mesh):
    return jax.shard_map(
        local,
        mesh=mesh,
        in_specs=(
            P("store", "tok", None),
            P("store", "tok", None),
            P("store", "tok"),
            P("tok", None),
            P("tok", None),
            P(("tok", "store"), None),
            P("store", None),
            P(("tok", "store"), None),
            P(None, ("tok", "store")),
        ),
        out_specs=(P(None, ("tok", "store")), P("store", "tok"), P("store", None)),
        check_vma=False,
    )
```

profile of v0, /device:TPU:0, one launch (start us, length us, event | category | flops | bytes accessed | tf_op | source)
XLA Modules:
  0.0 222.6 jit_solution(4785290300403083312)
XLA Ops:
  7.2 0.0 copy-start
  7.2 0.0 all-gather.5.cloned.1.call-start
  7.2 0.7 all-gather.5.cloned.1.call-update
  7.9 0.0 all-gather.3.cloned.1.call-start
  8.0 0.7 all-gather.3.cloned.1.call-update
  8.7 0.7 convert_element_type.35
  9.3 33.7 %all_gather.10 = bf16[4096,64]{0,1:T(8,128)(2,1)S(1)} all-gather(bf16[512,64]{0,1:T(8,128)(2,1)} %param.13), channel_id=1, replica_groups=mesh['tok'=8,'store'=4] {'tok'}, dimensions={0}, use_global_device_ids=true | all-gather | bytes 589824 | tf_op jit(solution)/shard_map/all_gather | solution.py:23
  43.0 1.3 convolution_convert_fusion.1
  44.3 0.0 copy-start.3
  44.3 16.6 %all-gather.5.cloned.1.call-done = bf16[14336,64]{0,1:T(8,128)(2,1)} async-done(((bf16[1792,64]{0,1:T(8,128)(2,1)}), bf16[14336,64]{0,1:T(8,128)(2,1)}) %all-gather.5.cloned.1.call-update) | async-done | bytes 1835024 | tf_op jit(solution)/shard_map/all_gather | solution.py:18
  61.0 2.8 %convolution_convert_fusion = bf16[64,64]{1,0:T(8,128)(2,1)S(1)} fusion(bf16[64,14336]{1,0:T(8,128)(2,1)} %bitcast.24, bf16[14336,64]{0,1:T(8,128)(2,1)} %all-gather.5.cloned.1.call-done), kind=kOutput, calls=%fused_computation.2 | convolution fusion | flops 117444608 | bytes 3678208 | tf_op jit(solution)/shard_map/dot_general | solution.py:16
  63.7 0.3 convolution_multiply_fusion.1
  64.0 0.1 mul.38
  64.1 0.6 copy.12
  64.7 3.8 %all-to-all-start = ((f32[2,8,4,128]{3,2,0,1:T(4,128)}), f32[2,8,4,128]{3,2,0,1:T(4,128)S(1)}, u32[]{:S(2)}, u32[]{:S(2)}) async-start(f32[2,8,4,128]{3,2,0,1:T(4,128)} %copy.12), calls=%async_computation | async-start | bytes 65536 | tf_op jit(solution)/shard_map/all_to_all | solution.py:40
  68.5 6.7 %all-to-all-done = f32[2,8,4,128]{3,2,0,1:T(4,128)S(1)} async-done(((f32[2,8,4,128]{3,2,0,1:T(4,128)}), f32[2,8,4,128]{3,2,0,1:T(4,128)S(1)}, u32[]{:S(2)}, u32[]{:S(2)}) %all-to-all-start) | async-done | bytes 32800 | tf_op jit(solution)/shard_map/all_to_all | solution.py:40
  75.2 0.6 copy.13
  75.8 3.3 %all-to-all-start.1 = ((f32[2,8,4,128]{3,1,0,2:T(8,128)}), f32[2,8,4,128]{3,1,0,2:T(8,128)S(1)}, u32[]{:S(2)}, u32[]{:S(2)}) async-start(f32[2,8,4,128]{3,1,0,2:T(8,128)} %copy.13), calls=%async_computation.1 | async-start | bytes 65536 | tf_op jit(solution)/shard_map/all_to_all | solution.py:39
  79.1 0.0 all-reduce.2.cloned.1.call-start
  79.2 0.0 copy-done.3
  79.2 0.2 fusion
  79.4 3.8 %all-to-all-done.1 = f32[2,8,4,128]{3,1,0,2:T(8,128)S(1)} async-done(((f32[2,8,4,128]{3,1,0,2:T(8,128)}), f32[2,8,4,128]{3,1,0,2:T(8,128)S(1)}, u32[]{:S(2)}, u32[]{:S(2)}) %all-to-all-start.1) | async-done | bytes 32800 | tf_op jit(solution)/shard_map/all_to_all | solution.py:39
  83.2 0.0 copy-done.2
  83.2 0.9 fusion.5
  84.1 0.0 all-reduce.2.cloned.1.call-update
  84.1 0.5 all-gather.3.cloned.1.call-done
  84.6 0.0 copy-done
  84.6 4.1 %convolution_multiply_fusion = f32[256,128]{1,0:T(8,128)} fusion(bf16[256,4096]{1,0:T(8,128)(2,1)} %all-gather.3.cloned.1.call-done, f32[128,4096]{1,0:T(8,128)S(1)} %copy-done, f32[256]{0:T(256)S(1)} %bitcast.30), kind=kOutput, calls=%fused_computation | convolution fusion | flops 1610645504 | bytes 4326400 | tf_op jit(solution)/shard_map/dot_general | solution.py:64
  88.8 123.9 %all-reduce.2.cloned.1.call-done = f32[8,4096]{1,0:T(8,128)} async-done(((f32[8,4096]{1,0:T(8,128)}), f32[8,4096]{1,0:T(8,128)}) %all-reduce.2.cloned.1.call-update) | async-done | bytes 131088 | tf_op jit(solution)/shard_map/psum | solution.py:48
  212.6 0.0 copy-done.1
  212.6 2.0 convolution_bitcast_fusion
  214.7 1.4 dynamic_slice.3
  (6 shorter events, 0.0 us)
Async XLA Ops:
  7.2 77.4 %copy-start = (f32[128,4096]{1,0:T(8,128)S(1)}, f32[128,4096]{1,0:T(8,128)}, u32[]{:S(2)}) copy-start(f32[128,4096]{1,0:T(8,128)} %param.16) | copy-start | bytes 6291460
  7.2 53.8 %all-gather.5.cloned.1.call-start = ((), (), s32[]{:S(2)}) async-start(), calls=%async_computation.3 | async-start | bytes 2064384 | tf_op jit(solution)/shard_map/all_gather | solution.py:18
  7.9 76.7 %all-gather.3.cloned.1.call-start = ((), (), s32[]{:S(2)}) async-start(), calls=%async_computation.2 | async-start | bytes 2621440 | tf_op jit(solution)/shard_map/all_gather | solution.py:63
  44.3 34.8 %copy-start.3 = (s32[4,1]{0,1:T(1,128)S(1)}, s32[4,1]{0,1:T(1,128)}, u32[]{:S(2)}) copy-start(s32[4,1]{0,1:T(1,128)} %param.17) | copy-start | bytes 52
  61.0 22.2 %copy-start.2 = (bf16[128,4096]{1,0:T(8,128)(2,1)S(1)}, bf16[128,4096]{1,0:T(8,128)(2,1)}, u32[]{:S(2)}) copy-start(bf16[128,4096]{1,0:T(8,128)(2,1)} %param.14) | copy-start | bytes 3145732
  64.7 10.5 %all-to-all-start = ((f32[2,8,4,128]{3,2,0,1:T(4,128)}), f32[2,8,4,128]{3,2,0,1:T(4,128)S(1)}, u32[]{:S(2)}, u32[]{:S(2)}) async-start(f32[2,8,4,128]{3,2,0,1:T(4,128)} %copy.12), calls=%async_computation | async-start | bytes 65536 | tf_op jit(solution)/shard_map/all_to_all | solution.py:40
  75.8 7.3 %all-to-all-start.1 = ((f32[2,8,4,128]{3,1,0,2:T(8,128)}), f32[2,8,4,128]{3,1,0,2:T(8,128)S(1)}, u32[]{:S(2)}, u32[]{:S(2)}) async-start(f32[2,8,4,128]{3,1,0,2:T(8,128)} %copy.13), calls=%async_computation.1 | async-start | bytes 65536 | tf_op jit(solution)/shard_map/all_to_all | solution.py:39
  79.1 133.5 %all-reduce.2.cloned.1.call-start = ((), (), s32[]{:S(2)}) async-start(), calls=%async_computation.4 | async-start | bytes 262144 | tf_op jit(solution)/shard_map/psum | solution.py:48
  84.6 128.0 %copy-start.1 = (bf16[64,4096]{1,0:T(8,128)(2,1)S(1)}, bf16[64,4096]{1,0:T(8,128)(2,1)}, u32[]{:S(2)}) copy-start(bf16[64,4096]{1,0:T(8,128)(2,1)} %param.15) | copy-start | bytes 1572868
Sparse Core Ops, SparseCore 0:
  10.2 50.7 all-gather.4
  62.5 22.0 all-gather.2
  90.1 122.4 all-reduce.1
where the time goes:
time: 223 us
  waiting for transfers between devices  153 us (69%)
  blocking collectives  33.7 us (15%)
  between operations  13.8 us (6%)
  matrix products  11.6 us (5%)
  starting transfers between devices  7.16 us (3%)
  local copies, waits for them, and re-layouts  2.75 us (1%)
    psum x1, waiting for transfers between devices, local(): full_pre = lax.psum(partial_pre, ('tok', 'store'))  124 us
    all_gather x1, blocking collectives, local(): lax.all_gather(proj_out, 'tok', axis=0, tiled=True)  33.7 us
    all_gather x1, waiting for transfers between devices, local(): lax.all_gather(proj_in, 'tok', axis=0, tiled=True)  16.6 us
    all_to_all x1, waiting for transfers between devices, local(): lax.all_to_all(blocks, 'tok', split_axis=1, concat_axis=1, tiled=True)  6.68 us
  transfers between devices with their start and end apart: 5, of which 5 were waited for; matrix products, arithmetic and copies ran while one was open for 5% of the time, Pallas kernels for 0%

commit v1 on v0

v1 whole, which is shorter than its diff:
```python
import math

import jax
import jax.numpy as jnp
from jax import lax
from jax.sharding import PartitionSpec as P

AXES = ("tok", "store")
BF16 = jnp.bfloat16
F32 = jnp.float32


def local(activations, out_grads, validity, proj_in, proj_out, precond, queries, store_rows, plan):
    nt = lax.axis_size("tok")
    ns = lax.axis_size("store")
    nx = ns // 2
    t = lax.axis_index("tok")
    s = lax.axis_index("store")
    core = s % 2
    x = s // 2
    docs, toks = activations.shape[:2]
    feat = proj_in.shape[1]
    n_tok = docs * toks
    z_offs = list(range(0, nt, 2))
    x_offs = list(range(0, ns, 2))

    def send(value, dt, ds):
        perm = [
            (i * ns + j, (i ^ dt) * ns + (j ^ ds)) for i in range(nt) for j in range(ns)
        ]
        return lax.ppermute(value, AXES, perm)

    def piece(w):
        rows, cols = w.shape[0] // 2, feat // nx
        return lax.dynamic_slice(w, (core * rows, x * cols), (rows, cols)).T

    k_in, k_out = proj_in.shape[0] // 2, proj_out.shape[0] // 2
    mine = jnp.concatenate([piece(proj_in), piece(proj_out)], axis=1)
    z_blocks = jnp.stack([mine] + [send(mine, o, 0) for o in z_offs[1:]])

    def halves(a, k):
        view = a.reshape(n_tok, nt, 2, k)
        own = lax.dynamic_slice(view, (0, 0, core, 0), (n_tok, nt, 1, k))[:, :, 0]
        other = lax.dynamic_slice(view, (0, 0, 1 - core, 0), (n_tok, nt, 1, k))[:, :, 0]
        return jnp.concatenate([own, send(other, 0, 1)], axis=0)

    acts = halves(activations, k_in)
    grads = halves(out_grads, k_out)

    blocks = {}
    for dy in (0, 1):
        for dx in x_offs:
            got = z_blocks if (dy, dx) == (0, 0) else send(z_blocks, dy, dx)
            for n, dz in enumerate(z_offs):
                blocks[dz + dy, dx] = got[n]

    left = right = 0.0
    for dt in range(nt):
        act = lax.dynamic_index_in_dim(acts, t ^ dt, 1, keepdims=False)
        grad = lax.dynamic_index_in_dim(grads, t ^ dt, 1, keepdims=False)
        w = jnp.stack([blocks[dt, dx] for dx in x_offs])
        w = jnp.take(w, x ^ jnp.arange(nx), axis=0).reshape(feat, k_in + k_out)
        nt_dims = (((1,), (1,)), ((), ()))
        left = left + lax.dot_general(act, w[:, :k_in], nt_dims, preferred_element_type=F32)
        right = right + lax.dot_general(grad, w[:, k_in:], nt_dims, preferred_element_type=F32)
    both = jnp.concatenate([left, right], axis=1)
    both = (both[:n_tok] + send(both[n_tok:], 0, 1)).astype(BF16)
    mask = validity.reshape(n_tok, 1).astype(BF16)
    left = both[:, :feat].reshape(docs, toks, feat)
    right = (both[:, feat:] * mask).reshape(docs, toks, -1)
    part = jnp.einsum("dpo,dpi->odi", right, left, preferred_element_type=F32)
    part = part.reshape(part.shape[0], docs * feat)

    terms = [part] + [send(part, o, 0) for o in z_offs[1:]]
    while len(terms) > 1:
        terms = [terms[i] + terms[i + 1] for i in range(0, len(terms), 2)]
    total = terms[0]
    total = total + send(total, 1, 0)
    norm = 1.0 / math.sqrt(toks * nt)
    grad_docs = (total * norm).astype(BF16)

    def rows_of(g):
        return g.reshape(-1, docs, feat).transpose(1, 0, 2).reshape(docs, -1)

    own = rows_of(grad_docs)
    g_x = jnp.concatenate([own] + [send(own, 0, o) for o in x_offs[1:]])
    g_core = send(g_x, 0, 1)

    p_pair = jnp.concatenate([precond, send(precond, 0, 1)])
    cols = p_pair.shape[0]
    nt_dims = (((1,), (1,)), ((), ()))
    pre = lax.dot_general(g_x, p_pair, nt_dims, preferred_element_type=F32).reshape(nx, docs, cols)
    pieces = [pre[0]] + [send(pre[n], 0, o) for n, o in enumerate(x_offs) if n]

    def in_place(parts):
        both = jnp.stack(parts).reshape(nx, parts[0].shape[0], 2, cols // 2)
        both = jnp.take(both, x ^ jnp.arange(nx), axis=0)
        both = jnp.take(both, core ^ jnp.arange(2), axis=2)
        return both.transpose(1, 0, 2, 3).reshape(parts[0].shape[0], -1)

    precond_docs = in_place(pieces)

    q_x = [queries] + [send(queries, 0, o) for o in x_offs[1:]]
    q_mine = jnp.concatenate(q_x)
    qp = lax.dot_general(q_mine, p_pair, nt_dims, preferred_element_type=F32).astype(BF16)
    qp = qp.reshape(nx, queries.shape[0], cols)
    qp = in_place([qp[0]] + [send(qp[n], 0, o) for n, o in enumerate(x_offs) if n])
    qp_z = jnp.stack([qp] + [send(qp, o, 0) for o in z_offs[1:]])
    qp_all = jnp.stack([qp_z, send(qp_z, 1, 0)], axis=1).reshape(nt, *qp.shape)
    qp_all = jnp.take(qp_all, t ^ jnp.arange(nt), axis=0).transpose(1, 0, 2)
    qp_all = qp_all.reshape(queries.shape[0], -1)
    g_all = jnp.stack([g_x.reshape(nx, docs, -1), g_core.reshape(nx, docs, -1)], axis=1)
    g_all = jnp.take(g_all.reshape(ns, docs, -1), s ^ jnp.arange(ns), axis=0)
    g_all = g_all.reshape(ns * docs, -1)
    doc_scores = lax.dot_general(qp_all, g_all, nt_dims, preferred_element_type=F32)

    q_core = send(q_mine, 0, 1)
    q_all = jnp.concatenate([q_mine.reshape(nx, 1, *queries.shape), q_core.reshape(nx, 1, *queries.shape)], axis=1)
    q_all = q_all.reshape(-1, queries.shape[1])
    high = store_rows.astype(BF16)
    low = (store_rows - high.astype(F32)).astype(BF16)
    raw = lax.dot_general(q_all, high, nt_dims, preferred_element_type=F32)
    raw = raw + lax.dot_general(q_all, low, nt_dims, preferred_element_type=F32)
    order = s ^ jnp.arange(ns)
    raw = jnp.take(raw.reshape(ns, -1, raw.shape[1]), order, axis=0)
    scores = raw * plan.astype(F32)[:, :, None]
    return scores.reshape(-1, raw.shape[2]), precond_docs, doc_scores


def solution(mesh):
    return jax.shard_map(
        local,
        mesh=mesh,
        in_specs=(
            P("store", "tok", None),
            P("store", "tok", None),
            P("store", "tok"),
            P("tok", None),
            P("tok", None),
            P(("tok", "store"), None),
            P("store", None),
            P(("tok", "store"), None),
            P(None, ("tok", "store")),
        ),
        out_specs=(P(None, ("tok", "store")), P("store", "tok"), P("store", None)),
        check_vma=False,
    )
```

time: 223 us -> 147 us (0.66)
  waiting for transfers between devices: 153 us -> 27.7 us
  local copies, waits for them, and re-layouts: 2.75 us -> 49.4 us
  blocking collectives: 33.7 us -> 0 us
  other arithmetic: 0.7 us -> 31.5 us
  starting transfers between devices: 7.16 us -> 25.8 us
  between operations: 13.8 us -> 1.24 us
    psum x1 -> x0, waiting for transfers between devices: 124 us -> none  [local(): full_pre = lax.psum(partial_pre, ('tok', 'store'))]
    all_gather x1 -> x0, blocking collectives: 33.7 us -> none  [local(): lax.all_gather(proj_out, 'tok', axis=0, tiled=True)]
    ppermute x0 -> x24, waiting for transfers between devices: none -> 27.7 us  [send(): return lax.ppermute(value, AXES, perm)]
    ppermute x0 -> x24, starting transfers between devices: none -> 25.8 us  [send(): return lax.ppermute(value, AXES, perm)]
    gather x0 -> x15, local copies, waits for them, and re-layouts: none -> 20.6 us  [the longest x8 16.4 us: local(): w = jnp.take(w, x ^ jnp.arange(nx), axis=0).reshape(feat, k_in + k_out)]
    concatenate x0 -> x7, other arithmetic: none -> 17.7 us  [the longest x4 15.4 us: halves(): return jnp.concatenate([own, send(other, 0, 1)], axis=0)]
    all_gather x2 -> x0, waiting for transfers between devices: 17.1 us -> none  [the longest x1 16.6 us: local(): lax.all_gather(proj_in, 'tok', axis=0, tiled=True)]
    all_to_all x2 -> x0, waiting for transfers between devices: 10.5 us -> none  [the longest x1 6.68 us: local(): lax.all_to_all(blocks, 'tok', split_axis=1, concat_axis=1, tiled=True)]
  transfers between devices with their start and end apart: 5 -> 24, of which waited for: 5 -> 9; matrix products, arithmetic and copies ran while one was open for 5% -> 57% of each run, Pallas kernels for 0% -> 0%
where the time goes in v1:
time: 147 us; the launch traced here: 146 us
  local copies, waits for them, and re-layouts  49.4 us (34%)
  other arithmetic  31.5 us (21%)
  waiting for transfers between devices  27.7 us (19%)
  starting transfers between devices  25.8 us (18%)
  matrix products  10.5 us (7%)
    ppermute x24, waiting for transfers between devices, send(): return lax.ppermute(value, AXES, perm)  27.7 us
    ppermute x24, starting transfers between devices, send(): return lax.ppermute(value, AXES, perm)  25.8 us
    gather x8, local copies, waits for them, and re-layouts, local(): w = jnp.take(w, x ^ jnp.arange(nx), axis=0).reshape(feat, k_in + k_out)  16.4 us
    concatenate x4, other arithmetic, halves(): return jnp.concatenate([own, send(other, 0, 1)], axis=0)  15.4 us
    dynamic_slice x2, local copies, waits for them, and re-layouts, halves(): lax.dynamic_slice(view, (0, 0, 1 - core, 0), (n_tok, nt, 1, k))[:, :, 0]  7.46 us
    unnamed x38, local copies, waits for them, and re-layouts  7.4 us
    reshape x2, local copies, waits for them, and re-layouts, halves(): view = a.reshape(n_tok, nt, 2, k)  6.01 us
    another operation x4, other arithmetic, local(): w = jnp.stack([blocks[dt, dx] for dx in x_offs])  5.88 us
  transfers between devices with their start and end apart: 24, of which 9 were waited for; matrix products, arithmetic and copies ran while one was open for 57% of the time, Pallas kernels for 0%

profile of v1, /device:TPU:0, one launch (start us, length us, event | category | flops | bytes accessed | tf_op | source)
XLA Modules:
  0.0 146.1 jit_solution(7909182533211308854)
XLA Ops:
  3.0 3.0 %collective-permute-start.3 = (bf16[32,1152]{1,0:T(8,128)(2,1)}, bf16[32,1152]{1,0:T(8,128)(2,1)}, u32[]{:S(2)}, u32[]{:S(2)}) collective-permute-start(bf16[32,1152]{1,0:T(8,128)(2,1)} %get-tuple-element.39), channel_id=1, source_target_pairs={{0,8},{1,9},{2,10},{3,11},{4,12},{5,13},{6,14},{7,15},{8,0},{9,1},... | collective-permute-start | bytes 221192 | tf_op jit(solution)/shard_map/ppermute | solution.py:31
  6.0 2.6 %collective-permute-start.4 = (bf16[32,1152]{1,0:T(8,128)(2,1)}, bf16[32,1152]{1,0:T(8,128)(2,1)}, u32[]{:S(2)}, u32[]{:S(2)}) collective-permute-start(bf16[32,1152]{1,0:T(8,128)(2,1)} %get-tuple-element.39), channel_id=1, source_target_pairs={{0,16},{1,17},{2,18},{3,19},{4,20},{5,21},{6,22},{7,23},{8,24},{9,... | collective-permute-start | bytes 221192 | tf_op jit(solution)/shard_map/ppermute | solution.py:31
  10.0 1.9 %constant_dynamic-slice_fusion = (bf16[64,8,1,256]{3,2,1,0:T(2,128)(2,1)S(1)}, bf16[64,8,1,256]{3,2,1,0:T(2,128)(2,1)}) fusion(bf16[64,8,2,256]{3,2,1,0:T(2,128)(2,1)S(1)} %reshape.245, s32[]{:T(128)S(6)} %select_n.197, s32[]{:T(128)S(6)} %select_n.196), kind=kLoop, calls=%fused_computation.175 | loop fusion | bytes 1048584 | tf_op jit(solution)/shard_map/dynamic_slice | solution.py:44
  12.7 1.7 %collective-permute-start = (bf16[64,4096]{1,0:T(8,128)(2,1)}, bf16[64,4096]{1,0:T(8,128)(2,1)}, u32[]{:S(2)}, u32[]{:S(2)}) collective-permute-start(bf16[64,4096]{1,0:T(8,128)(2,1)} %param.17), channel_id=1, source_target_pairs={{0,2},{1,3},{2,0},{3,1},{4,6},{5,7},{6,4},{7,5},{8,10},{9,11},{10,... | collective-permute-start | bytes 1572872 | tf_op jit(solution)/shard_map/ppermute | solution.py:31
  14.9 1.9 %constant_dynamic-update-slice_fusion.1 = bf16[128,4096]{1,0:T(8,128)(2,1)} fusion(bf16[64,4096]{1,0:T(8,128)(2,1)} %param.17), kind=kLoop, calls=%fused_computation.180 | loop fusion | bytes 1048576
  16.8 4.6 %reshape.236 = bf16[64,8,2,896]{3,2,1,0:T(2,128)(2,1)S(1)} reshape(bf16[2,32,14336]{2,1,0:T(8,128)(2,1)} %param.11) | data formatting | bytes 3670016 | tf_op jit(solution)/shard_map/reshape | solution.py:42
  21.4 5.6 %constant_dynamic-slice_fusion.2 = (bf16[64,8,1,896]{3,2,1,0:T(2,128)(2,1)}, bf16[64,8,1,896]{3,2,1,0:T(2,128)(2,1)}) fusion(bf16[64,8,2,896]{3,2,1,0:T(2,128)(2,1)S(1)} %reshape.236, s32[]{:T(128)S(6)} %select_n.197, s32[]{:T(128)S(6)} %select_n.196), kind=kLoop, calls=%fused_computation.177 | loop fusion | bytes 3670024 | tf_op jit(solution)/shard_map/dynamic_slice | solution.py:44
  29.4 2.7 %copy.131 = bf16[64,8,1,896]{3,1,2,0:T(8,128)(2,1)} copy(bf16[64,8,1,896]{3,2,1,0:T(2,128)(2,1)} %get-tuple-element.12) | data formatting | bytes 1835008
  32.9 1.8 %pad_maximum_fusion.2 = bf16[4,32,1152]{2,1,0:T(8,128)(2,1)} fusion(bf16[1,32,1152]{2,1,0:T(8,128)(2,1)} %bitcast.12, bf16[1,32,1152]{2,1,0:T(8,128)(2,1)} %bitcast.11, bf16[1,32,1152]{2,1,0:T(8,128)(2,1)} %bitcast.10, bf16[1,32,1152]{2,1,0:T(8,128)(2,1)} %get-tuple-element.38), kind=kLoop, calls=%fused_computation.80 | loop fusion | flops 442368 | bytes 589824 | tf_op jit(solution)/shard_map/stack | solution.py:39
  36.4 2.0 %fusion.35 = (bf16[128,1,256]{2,1,0:T(2,128)(2,1)}, bf16[128,1,256]{2,1,0:T(2,128)(2,1)}) fusion(s32[]{:T(128)S(6)} %select_n.207, bf16[64,8,256]{2,1,0:T(8,128)(2,1)S(1)} %bitcast.133, bf16[64,8,256]{2,1,0:T(8,128)(2,1)} %collective-permute-done.9, s32[]{:T(128)S(6)} %select_n.206), kind=kLoop, calls=%fused_computation.124 | loop fusion | flops 262144 | bytes 655368 | tf_op jit(solution)/shard_map/concatenate | solution.py:45
  38.4 3.2 %fusion.28 = (bf16[128,1,256]{2,1,0:T(2,128)(2,1)}, bf16[128,1,256]{2,1,0:T(2,128)(2,1)}, bf16[128,1,256]{2,1,0:T(2,128)(2,1)}, bf16[128,1,256]{2,1,0:T(2,128)(2...) fusion(s32[]{:T(128)S(6)} %select_n.208, bf16[64,8,256]{2,1,0:T(8,128)(2,1)S(1)} %bitcast.134, ...), kind=kLoop, calls=%fused_computation.117 | loop fusion | flops 786432 | bytes 917528 | tf_op jit(solution)/shard_map/concatenate | solution.py:45
  41.7 8.7 %collective-permute-done.7 = bf16[4,32,1152]{2,1,0:T(8,128)(2,1)S(1)} collective-permute-done((bf16[4,32,1152]{2,1,0:T(8,128)(2,1)}, bf16[4,32,1152]{2,1,0:T(8,128)(2,1)S(1)}, u32[]{:S(2)}, u32[]{:S(2)}) %collective-permute-start.7) | collective-permute-done | bytes 294944 | tf_op jit(solution)/shard_map/ppermute | solution.py:31
  54.2 2.1 %gather_fusion.8 = bf16[2,32,1152]{2,1,0:T(8,128)(2,1)} fusion(bf16[2,32,1152]{2,1,0:T(8,128)(2,1)} %get-tuple-element.58, s32[1024]{0:T(1024)S(1)} %pad_clamp_fusion.3), kind=kCustom, calls=%fused_computation.1.clone | custom fusion | bytes 294920 | tf_op jit(solution)/shard_map/jit(_take)/gather | solution.py:62
  56.4 1.7 %pad_maximum_fusion.9 = (bf16[2,32,1152]{2,1,0:T(8,128)(2,1)}, bf16[2,32,1152]{2,1,0:T(8,128)(2,1)}) fusion(bf16[1,32,1152]{2,1,0:T(8,128)(2,1)} %get-tuple-element.29, bf16[1,32,1152]{2,1,0:T(8,128)(2,1)} %get-tuple-element.25, bf16[1,32,1152]{2,1,0:T(8,128)(2,1)} %get-tuple-element.28, bf16[1,32,1152]{2,1,0:T(8,128)(2,1)S(1)} %get-tuple-element.24), kind=kLoop, calls=%fused_computation.106 | loop fusion | flops 147456 | bytes 589824 | tf_op jit(solution)/shard_map/stack | solution.py:61
  58.1 2.1 %gather_fusion.12 = bf16[2,32,1152]{2,1,0:T(8,128)(2,1)} fusion(bf16[2,32,1152]{2,1,0:T(8,128)(2,1)} %get-tuple-element.60, s32[1024]{0:T(1024)S(1)} %pad_clamp_fusion.3), kind=kCustom, calls=%fused_computation.5.clone | custom fusion | bytes 294920 | tf_op jit(solution)/shard_map/jit(_take)/gather | solution.py:62
  60.2 2.1 %gather_fusion.14 = bf16[2,32,1152]{2,1,0:T(8,128)(2,1)} fusion(bf16[2,32,1152]{2,1,0:T(8,128)(2,1)} %get-tuple-element.61, s32[1024]{0:T(1024)S(1)} %pad_clamp_fusion.3), kind=kCustom, calls=%fused_computation.7.clone | custom fusion | bytes 294920 | tf_op jit(solution)/shard_map/jit(_take)/gather | solution.py:62
  62.4 1.6 %fusion.80 = (bf16[1,32,1152]{2,1,0:T(8,128)(2,1)S(1)}, bf16[1,32,1152]{2,1,0:T(8,128)(2,1)S(1)}, bf16[1,32,1152]{2,1,0:T(8,128)(2,1)S(1)}, bf16[1,32,1152]{2,1,0:T(8,128)(2,1)}) fusion(bf16[4,32,1152]{2,1,0:T(8,128)(2,1)} %collective-permute-done.6), kind=kLoop, calls=%fused_computation.213 | loop fusion | bytes 589824 | tf_op jit(solution)/shard_map/slice | solution.py:55
  64.0 1.7 %pad_maximum_fusion.8 = (bf16[2,32,1152]{2,1,0:T(8,128)(2,1)}, bf16[2,32,1152]{2,1,0:T(8,128)(2,1)}) fusion(bf16[1,32,1152]{2,1,0:T(8,128)(2,1)S(1)} %get-tuple-element.33, bf16[1,32,1152]{2,1,0:T(8,128)(2,1)} %bitcast.11, bf16[1,32,1152]{2,1,0:T(8,128)(2,1)S(1)} %get-tuple-element.32, bf16[1,32,1152]{2,1,0:T(8,128)(2,1)} %bitcast.12), kind=kLoop, calls=%fused_computation.105 | loop fusion | flops 147456 | bytes 589824 | tf_op jit(solution)/shard_map/stack | solution.py:61
  65.7 2.1 %gather_fusion.11 = bf16[2,32,1152]{2,1,0:T(8,128)(2,1)} fusion(bf16[2,32,1152]{2,1,0:T(8,128)(2,1)} %get-tuple-element.64, s32[1024]{0:T(1024)S(1)} %pad_clamp_fusion.3), kind=kCustom, calls=%fused_computation.4.clone | custom fusion | bytes 294920 | tf_op jit(solution)/shard_map/jit(_take)/gather | solution.py:62
  67.8 2.1 %gather_fusion.13 = bf16[2,32,1152]{2,1,0:T(8,128)(2,1)} fusion(bf16[2,32,1152]{2,1,0:T(8,128)(2,1)} %get-tuple-element.65, s32[1024]{0:T(1024)S(1)} %pad_clamp_fusion.3), kind=kCustom, calls=%fused_computation.6.clone | custom fusion | bytes 294920 | tf_op jit(solution)/shard_map/jit(_take)/gather | solution.py:62
  70.0 1.7 %pad_maximum_fusion.4 = (bf16[2,32,1152]{2,1,0:T(8,128)(2,1)}, bf16[2,32,1152]{2,1,0:T(8,128)(2,1)}) fusion(bf16[1,32,1152]{2,1,0:T(8,128)(2,1)} %get-tuple-element.35, bf16[1,32,1152]{2,1,0:T(8,128)(2,1)S(1)} %copy-done.6, bf16[1,32,1152]{2,1,0:T(8,128)(2,1)S(1)} %get-tuple-element.34, bf16[1,32,1152]{2,1,0:T(8,128)(2,1)} %bitcast.10), kind=kLoop, calls=%fused_computation.101 | loop fusion | flops 147456 | bytes 589824 | tf_op jit(solution)/shard_map/stack | solution.py:61
  71.7 2.1 %gather_fusion.7 = bf16[2,32,1152]{2,1,0:T(8,128)(2,1)} fusion(bf16[2,32,1152]{2,1,0:T(8,128)(2,1)} %get-tuple-element.62, s32[1024]{0:T(1024)S(1)} %pad_clamp_fusion.3), kind=kCustom, calls=%fused_computation.clone | custom fusion | bytes 294920 | tf_op jit(solution)/shard_map/jit(_take)/gather | solution.py:62
  73.8 2.1 %gather_fusion.9 = bf16[2,32,1152]{2,1,0:T(8,128)(2,1)} fusion(bf16[2,32,1152]{2,1,0:T(8,128)(2,1)} %get-tuple-element.63, s32[1024]{0:T(1024)S(1)} %pad_clamp_fusion.3), kind=kCustom, calls=%fused_computation.2.clone | custom fusion | bytes 294920 | tf_op jit(solution)/shard_map/jit(_take)/gather | solution.py:62
  82.4 7.8 %fusion.3 = (bf16[128,1,896]{2,1,0:T(2,128)(2,1)S(1)}, bf16[128,1,896]{2,1,0:T(2,128)(2,1)S(1)}, bf16[128,1,896]{2,1,0:T(2,128)(2,1)S(1)}, bf16[128,1,896]{2,1,0...) fusion(s32[]{:T(128)S(6)} %select_n.208, bf16[64,8,896]{2,1,0:T(8,128)(2,1)S(1)} %bitcast.130, ...), kind=kLoop, calls=%fused_computation.72 | loop fusion | flops 2752512 | bytes 3211288 | tf_op jit(solution)/shard_map/concatenate | solution.py:45
  91.3 2.4 %fusion.10 = (bf16[128,1,896]{2,1,0:T(2,128)(2,1)S(1)}, bf16[128,1,896]{2,1,0:T(2,128)(2,1)S(1)}) fusion(s32[]{:T(128)S(6)} %select_n.207, bf16[64,8,896]{2,1,0:T(8,128)(2,1)S(1)} %bitcast.131, bf16[64,8,896]{2,1,0:T(8,128)(2,1)} %collective-permute-done.2, s32[]{:T(128)S(6)} %select_n.206), kind=kLoop, calls=%fused_computation.79 | loop fusion | flops 917504 | bytes 2293768 | tf_op jit(solution)/shard_map/concatenate | solution.py:45
  98.0 3.5 %collective-permute-start.12 = (f32[64,128]{1,0:T(8,128)S(1)}, f32[64,128]{1,0:T(8,128)S(1)}, u32[]{:S(2)}, u32[]{:S(2)}) collective-permute-start(f32[64,128]{1,0:T(8,128)S(1)} %copy.28), channel_id=1, source_target_pairs={{0,16},{1,17},{2,18},{3,19},{4,20},{5,21},{6,22},{7,23},{8,24},{9,... | collective-permute-start | bytes 98312 | tf_op jit(solution)/shard_map/ppermute | solution.py:31
  101.5 2.5 %collective-permute-done.12 = f32[64,128]{1,0:T(8,128)S(1)} collective-permute-done((f32[64,128]{1,0:T(8,128)S(1)}, f32[64,128]{1,0:T(8,128)S(1)}, u32[]{:S(2)}, u32[]{:S(2)}) %collective-permute-start.12) | collective-permute-done | bytes 32800 | tf_op jit(solution)/shard_map/ppermute | solution.py:31
  104.0 3.2 %collective-permute-done.13 = f32[64,128]{1,0:T(8,128)S(1)} collective-permute-done((f32[64,128]{1,0:T(8,128)S(1)}, f32[64,128]{1,0:T(8,128)S(1)}, u32[]{:S(2)}, u32[]{:S(2)}) %collective-permute-start.13) | collective-permute-done | bytes 32800 | tf_op jit(solution)/shard_map/ppermute | solution.py:31
  109.1 2.1 %collective-permute-done.14 = f32[64,128]{1,0:T(8,128)S(1)} collective-permute-done((f32[64,128]{1,0:T(8,128)S(1)}, f32[64,128]{1,0:T(8,128)S(1)}, u32[]{:S(2)}, u32[]{:S(2)}) %collective-permute-start.14) | collective-permute-done | bytes 32800 | tf_op jit(solution)/shard_map/ppermute | solution.py:31
  126.2 3.5 %collective-permute-start.21 = (bf16[64,512]{1,0:T(8,128)(2,1)S(1)}, bf16[64,512]{1,0:T(8,128)(2,1)S(1)}, u32[]{:S(2)}, u32[]{:S(2)}) collective-permute-start(bf16[64,512]{1,0:T(8,128)(2,1)S(1)} %reshape.252), channel_id=1, source_target_pairs={{0,24},{1,25},{2,26},{3,27},{4,28},{5,29},{6,30},{7,31},{8,16},{9,... | collective-permute-start | bytes 196616 | tf_op jit(solution)/shard_map/ppermute | solution.py:31
  130.5 2.6 %collective-permute-done.20 = bf16[64,512]{1,0:T(8,128)(2,1)S(1)} collective-permute-done((bf16[64,512]{1,0:T(8,128)(2,1)S(1)}, bf16[64,512]{1,0:T(8,128)(2,1)S(1)}, u32[]{:S(2)}, u32[]{:S(2)}) %collective-permute-start.20) | collective-permute-done | bytes 65568 | tf_op jit(solution)/shard_map/ppermute | solution.py:31
  134.9 4.7 %collective-permute-done.22 = bf16[4,64,512]{2,1,0:T(8,128)(2,1)S(1)} collective-permute-done((bf16[4,64,512]{2,1,0:T(8,128)(2,1)S(1)}, bf16[4,64,512]{2,1,0:T(8,128)(2,1)S(1)}, u32[]{:S(2)}, u32[]{:S(2)}) %collective-permute-start.22) | collective-permute-done | bytes 262176 | tf_op jit(solution)/shard_map/ppermute | solution.py:31
  (176 shorter events, 51.4 us)
Async XLA Ops:
  3.0 29.3 %collective-permute-start.3 = (bf16[32,1152]{1,0:T(8,128)(2,1)}, bf16[32,1152]{1,0:T(8,128)(2,1)}, u32[]{:S(2)}, u32[]{:S(2)}) collective-permute-start(bf16[32,1152]{1,0:T(8,128)(2,1)} %get-tuple-element.39), channel_id=1, source_target_pairs={{0,8},{1,9},{2,10},{3,11},{4,12},{5,13},{6,14},{7,15},{8,0},{9,1},... | collective-permute-start | bytes 221192 | tf_op jit(solution)/shard_map/ppermute | solution.py:31
  6.0 26.6 %collective-permute-start.4 = (bf16[32,1152]{1,0:T(8,128)(2,1)}, bf16[32,1152]{1,0:T(8,128)(2,1)}, u32[]{:S(2)}, u32[]{:S(2)}) collective-permute-start(bf16[32,1152]{1,0:T(8,128)(2,1)} %get-tuple-element.39), channel_id=1, source_target_pairs={{0,16},{1,17},{2,18},{3,19},{4,20},{5,21},{6,22},{7,23},{8,24},{9,... | collective-permute-start | bytes 221192 | tf_op jit(solution)/shard_map/ppermute | solution.py:31
  8.6 24.3 %collective-permute-start.5 = (bf16[32,1152]{1,0:T(8,128)(2,1)}, bf16[32,1152]{1,0:T(8,128)(2,1)}, u32[]{:S(2)}, u32[]{:S(2)}) collective-permute-start(bf16[32,1152]{1,0:T(8,128)(2,1)} %get-tuple-element.39), channel_id=1, source_target_pairs={{0,24},{1,25},{2,26},{3,27},{4,28},{5,29},{6,30},{7,31},{8,16},{9,... | collective-permute-start | bytes 221192 | tf_op jit(solution)/shard_map/ppermute | solution.py:31
  12.7 23.5 %collective-permute-start.9 = (bf16[64,8,256]{2,1,0:T(8,128)(2,1)}, bf16[64,8,256]{2,1,0:T(8,128)(2,1)}, u32[]{:S(2)}, u32[]{:S(2)}) collective-permute-start(bf16[64,8,256]{2,1,0:T(8,128)(2,1)} %bitcast.126), channel_id=1, source_target_pairs={{0,1},{1,0},{2,3},{3,2},{4,5},{5,4},{6,7},{7,6},{8,9},{9,8},{10,11... | collective-permute-start | bytes 786440 | tf_op jit(solution)/shard_map/ppermute | solution.py:31
  12.7 100.3 %collective-permute-start = (bf16[64,4096]{1,0:T(8,128)(2,1)}, bf16[64,4096]{1,0:T(8,128)(2,1)}, u32[]{:S(2)}, u32[]{:S(2)}) collective-permute-start(bf16[64,4096]{1,0:T(8,128)(2,1)} %param.17), channel_id=1, source_target_pairs={{0,2},{1,3},{2,0},{3,1},{4,6},{5,7},{6,4},{7,5},{8,10},{9,11},{10,... | collective-permute-start | bytes 1572872 | tf_op jit(solution)/shard_map/ppermute | solution.py:31
  21.4 5.6 %copy-start.5 = (bf16[128,4096]{1,0:T(8,128)(2,1)S(1)}, bf16[128,4096]{1,0:T(8,128)(2,1)}, u32[]{:S(2)}) copy-start(bf16[128,4096]{1,0:T(8,128)(2,1)} %param.16) | copy-start | bytes 3145732
  29.4 2.8 %copy-start.4 = (bf16[64,8,1,256]{3,2,1,0:T(2,128)(2,1)S(1)}, bf16[64,8,1,256]{3,2,1,0:T(2,128)(2,1)}, u32[]{:S(2)}) copy-start(bf16[64,8,1,256]{3,2,1,0:T(2,128)(2,1)} %get-tuple-element.23) | copy-start | bytes 786436
  32.3 83.0 %collective-permute-start.16 = (bf16[128,4096]{1,0:T(8,128)(2,1)}, bf16[128,4096]{1,0:T(8,128)(2,1)}, u32[]{:S(2)}, u32[]{:S(2)}) collective-permute-start(bf16[128,4096]{1,0:T(8,128)(2,1)} %param.16), channel_id=1, source_target_pairs={{0,1},{1,0},{2,3},{3,2},{4,5},{5,4},{6,7},{7,6},{8,9},{9,8},{10,11... | collective-permute-start | bytes 3145736 | tf_op jit(solution)/shard_map/ppermute | solution.py:31
  32.6 49.8 %collective-permute-start.2 = (bf16[64,8,896]{2,1,0:T(8,128)(2,1)}, bf16[64,8,896]{2,1,0:T(8,128)(2,1)}, u32[]{:S(2)}, u32[]{:S(2)}) collective-permute-start(bf16[64,8,896]{2,1,0:T(8,128)(2,1)} %bitcast.137), channel_id=1, source_target_pairs={{0,1},{1,0},{2,3},{3,2},{4,5},{5,4},{6,7},{7,6},{8,9},{9,8},{10,11... | collective-permute-start | bytes 2752520 | tf_op jit(solution)/shard_map/ppermute | solution.py:31
  34.7 15.7 %collective-permute-start.7 = (bf16[4,32,1152]{2,1,0:T(8,128)(2,1)}, bf16[4,32,1152]{2,1,0:T(8,128)(2,1)S(1)}, u32[]{:S(2)}, u32[]{:S(2)}) collective-permute-start(bf16[4,32,1152]{2,1,0:T(8,128)(2,1)} %pad_maximum_fusion.2), channel_id=1, source_target_pairs={{0,4},{1,5},{2,6},{3,7},{4,0},{5,1},{6,2},{7,3},{8,12},{9,13},{10,... | collective-permute-start | bytes 884744 | tf_op jit(solution)/shard_map/ppermute | solution.py:31
  36.2 15.1 %collective-permute-start.8 = (bf16[4,32,1152]{2,1,0:T(8,128)(2,1)}, bf16[4,32,1152]{2,1,0:T(8,128)(2,1)S(1)}, u32[]{:S(2)}, u32[]{:S(2)}) collective-permute-start(bf16[4,32,1152]{2,1,0:T(8,128)(2,1)} %pad_maximum_fusion.2), channel_id=1, source_target_pairs={{0,6},{1,7},{2,4},{3,5},{4,2},{5,3},{6,0},{7,1},{8,14},{9,15},{10,... | collective-permute-start | bytes 884744 | tf_op jit(solution)/shard_map/ppermute | solution.py:31
  50.3 12.0 %collective-permute-start.6 = (bf16[4,32,1152]{2,1,0:T(8,128)(2,1)}, bf16[4,32,1152]{2,1,0:T(8,128)(2,1)}, u32[]{:S(2)}, u32[]{:S(2)}) collective-permute-start(bf16[4,32,1152]{2,1,0:T(8,128)(2,1)} %pad_maximum_fusion.2), channel_id=1, source_target_pairs={{0,2},{1,3},{2,0},{3,1},{4,6},{5,7},{6,4},{7,5},{8,10},{9,11},{10,... | collective-permute-start | bytes 884744 | tf_op jit(solution)/shard_map/ppermute | solution.py:31
  52.0 18.0 %copy-start.6 = (bf16[1,32,1152]{2,1,0:T(8,128)(2,1)S(1)}, bf16[1,32,1152]{2,1,0:T(8,128)(2,1)}, u32[]{:S(2)}) copy-start(bf16[1,32,1152]{2,1,0:T(8,128)(2,1)} %get-tuple-element.38) | copy-start | bytes 221188
  91.2 3.8 %copy-start.13 = (s32[2]{0:T(128)S(1)}, s32[2]{0:T(128)}, u32[]{:S(2)}) copy-start(s32[2]{0:T(128)} %fusion.72) | copy-start | bytes 28
  91.2 3.8 %copy-start.14 = (s32[2,32]{1,0:T(2,128)S(1)}, s32[2,32]{1,0:T(2,128)}, u32[]{:S(2)}) copy-start(s32[2,32]{1,0:T(2,128)} %param.13) | copy-start | bytes 772
  91.3 17.7 %copy-start.12 = (f32[4]{0:T(128)S(1)}, f32[4]{0:T(128)}, u32[]{:S(2)}) copy-start(f32[4]{0:T(128)} %convert_bitcast_fusion) | copy-start | bytes 52
  93.7 19.3 %copy-start.3 = (bf16[128,4096]{1,0:T(8,128)(2,1)S(1)}, bf16[128,4096]{1,0:T(8,128)(2,1)}, u32[]{:S(2)}) copy-start(bf16[128,4096]{1,0:T(8,128)(2,1)} %constant_dynamic-update-slice_fusion.1) | copy-start | bytes 3145732
  95.1 1.5 %collective-permute-start.10 = (f32[64,128]{0,1:T(8,128)}, f32[64,128]{0,1:T(8,128)S(1)}, u32[]{:S(2)}, u32[]{:S(2)}) collective-permute-start(f32[64,128]{0,1:T(8,128)} %pad_maximum_fusion.13), channel_id=1, source_target_pairs={{0,1},{1,0},{2,3},{3,2},{4,5},{5,4},{6,7},{7,6},{8,9},{9,8},{10,11... | collective-permute-start | bytes 98312 | tf_op jit(solution)/shard_map/ppermute | solution.py:31
  97.0 4.5 %collective-permute-start.11 = (f32[64,128]{1,0:T(8,128)S(1)}, f32[64,128]{1,0:T(8,128)S(1)}, u32[]{:S(2)}, u32[]{:S(2)}) collective-permute-start(f32[64,128]{1,0:T(8,128)S(1)} %copy.28), channel_id=1, source_target_pairs={{0,8},{1,9},{2,10},{3,11},{4,12},{5,13},{6,14},{7,15},{8,0},{9,1},... | collective-permute-start | bytes 98312 | tf_op jit(solution)/shard_map/ppermute | solution.py:31
  98.0 6.0 %collective-permute-start.12 = (f32[64,128]{1,0:T(8,128)S(1)}, f32[64,128]{1,0:T(8,128)S(1)}, u32[]{:S(2)}, u32[]{:S(2)}) collective-permute-start(f32[64,128]{1,0:T(8,128)S(1)} %copy.28), channel_id=1, source_target_pairs={{0,16},{1,17},{2,18},{3,19},{4,20},{5,21},{6,22},{7,23},{8,24},{9,... | collective-permute-start | bytes 98312 | tf_op jit(solution)/shard_map/ppermute | solution.py:31
  101.5 5.7 %collective-permute-start.13 = (f32[64,128]{1,0:T(8,128)S(1)}, f32[64,128]{1,0:T(8,128)S(1)}, u32[]{:S(2)}, u32[]{:S(2)}) collective-permute-start(f32[64,128]{1,0:T(8,128)S(1)} %copy.28), channel_id=1, source_target_pairs={{0,24},{1,25},{2,26},{3,27},{4,28},{5,29},{6,30},{7,31},{8,16},{9,... | collective-permute-start | bytes 98312 | tf_op jit(solution)/shard_map/ppermute | solution.py:31
  107.2 4.0 %collective-permute-start.14 = (f32[64,128]{1,0:T(8,128)S(1)}, f32[64,128]{1,0:T(8,128)S(1)}, u32[]{:S(2)}, u32[]{:S(2)}) collective-permute-start(f32[64,128]{1,0:T(8,128)S(1)} %add_add_fusion), channel_id=1, source_target_pairs={{0,4},{1,5},{2,6},{3,7},{4,0},{5,1},{6,2},{7,3},{8,12},{9,13},{10,... | collective-permute-start | bytes 98312 | tf_op jit(solution)/shard_map/ppermute | solution.py:31
  111.4 3.8 %collective-permute-start.15 = (bf16[2,4096]{1,0:T(2,128)(2,1)S(1)}, bf16[2,4096]{1,0:T(2,128)(2,1)S(1)}, u32[]{:S(2)}, u32[]{:S(2)}) collective-permute-start(bf16[2,4096]{1,0:T(2,128)(2,1)S(1)} %reshape.250), channel_id=1, source_target_pairs={{0,2},{1,3},{2,0},{3,1},{4,6},{5,7},{6,4},{7,5},{8,10},{9,11},{10,... | collective-permute-start | bytes 49160 | tf_op jit(solution)/shard_map/ppermute | solution.py:31
  114.0 27.4 %collective-permute-start.1 = (bf16[128,4096]{1,0:T(8,128)(2,1)S(1)}, bf16[128,4096]{1,0:T(8,128)(2,1)}, u32[]{:S(2)}, u32[]{:S(2)}) collective-permute-start(bf16[128,4096]{1,0:T(8,128)(2,1)S(1)} %constant_dynamic-update-slice_fusion), channel_id=1, source_target_pairs={{0,1},{1,0},{2,3},{3,2},{4,5},{5,4},{6,7},{7,6},{8,9},{9,8},{10,11... | collective-permute-start | bytes 3145736 | tf_op jit(solution)/shard_map/ppermute | solution.py:31
  115.2 8.5 %collective-permute-start.23 = (bf16[4,4096]{1,0:T(4,128)(2,1)S(1)}, bf16[4,4096]{1,0:T(4,128)(2,1)S(1)}, u32[]{:S(2)}, u32[]{:S(2)}) collective-permute-start(bf16[4,4096]{1,0:T(4,128)(2,1)S(1)} %pad_maximum_fusion.16), channel_id=1, source_target_pairs={{0,1},{1,0},{2,3},{3,2},{4,5},{5,4},{6,7},{7,6},{8,9},{9,8},{10,11... | collective-permute-start | bytes 98312 | tf_op jit(solution)/shard_map/ppermute | solution.py:31
  116.6 6.4 %copy-start.11 = (pred[2]{0:T(512)(128)(4,1)S(1)}, pred[2]{0:T(512)(128)(4,1)}, u32[]{:S(2)}) copy-start(pred[2]{0:T(512)(128)(4,1)} %get-tuple-element.55) | copy-start | bytes 10
  118.1 3.6 %collective-permute-start.17 = (f32[2,256]{1,0:T(2,128)S(1)}, f32[2,256]{1,0:T(2,128)S(1)}, u32[]{:S(2)}, u32[]{:S(2)}) collective-permute-start(f32[2,256]{1,0:T(2,128)S(1)} %get-tuple-element.45), channel_id=1, source_target_pairs={{0,2},{1,3},{2,0},{3,1},{4,6},{5,7},{6,4},{7,5},{8,10},{9,11},{10,... | collective-permute-start | bytes 6152 | tf_op jit(solution)/shard_map/ppermute | solution.py:31
  119.7 4.1 %collective-permute-start.18 = (bf16[64,256]{1,0:T(8,128)(2,1)S(1)}, bf16[64,256]{1,0:T(8,128)(2,1)S(1)}, u32[]{:S(2)}, u32[]{:S(2)}) collective-permute-start(bf16[64,256]{1,0:T(8,128)(2,1)S(1)} %get-tuple-element.41), channel_id=1, source_target_pairs={{0,2},{1,3},{2,0},{3,1},{4,6},{5,7},{6,4},{7,5},{8,10},{9,11},{10,... | collective-permute-start | bytes 98312 | tf_op jit(solution)/shard_map/ppermute | solution.py:31
  125.2 5.3 %collective-permute-start.19 = (bf16[64,512]{1,0:T(8,128)(2,1)S(1)}, bf16[64,512]{1,0:T(8,128)(2,1)S(1)}, u32[]{:S(2)}, u32[]{:S(2)}) collective-permute-start(bf16[64,512]{1,0:T(8,128)(2,1)S(1)} %reshape.252), channel_id=1, source_target_pairs={{0,8},{1,9},{2,10},{3,11},{4,12},{5,13},{6,14},{7,15},{8,0},{9,1},... | collective-permute-start | bytes 196616 | tf_op jit(solution)/shard_map/ppermute | solution.py:31
  125.3 7.8 %collective-permute-start.20 = (bf16[64,512]{1,0:T(8,128)(2,1)S(1)}, bf16[64,512]{1,0:T(8,128)(2,1)S(1)}, u32[]{:S(2)}, u32[]{:S(2)}) collective-permute-start(bf16[64,512]{1,0:T(8,128)(2,1)S(1)} %reshape.252), channel_id=1, source_target_pairs={{0,16},{1,17},{2,18},{3,19},{4,20},{5,21},{6,22},{7,23},{8,24},{9,... | collective-permute-start | bytes 196616 | tf_op jit(solution)/shard_map/ppermute | solution.py:31
  126.2 6.9 %collective-permute-start.21 = (bf16[64,512]{1,0:T(8,128)(2,1)S(1)}, bf16[64,512]{1,0:T(8,128)(2,1)S(1)}, u32[]{:S(2)}, u32[]{:S(2)}) collective-permute-start(bf16[64,512]{1,0:T(8,128)(2,1)S(1)} %reshape.252), channel_id=1, source_target_pairs={{0,24},{1,25},{2,26},{3,27},{4,28},{5,29},{6,30},{7,31},{8,16},{9,... | collective-permute-start | bytes 196616 | tf_op jit(solution)/shard_map/ppermute | solution.py:31
  133.1 6.4 %collective-permute-start.22 = (bf16[4,64,512]{2,1,0:T(8,128)(2,1)S(1)}, bf16[4,64,512]{2,1,0:T(8,128)(2,1)S(1)}, u32[]{:S(2)}, u32[]{:S(2)}) collective-permute-start(bf16[4,64,512]{2,1,0:T(8,128)(2,1)S(1)} %get-tuple-element.37), channel_id=1, source_target_pairs={{0,4},{1,5},{2,6},{3,7},{4,0},{5,1},{6,2},{7,3},{8,12},{9,13},{10,... | collective-permute-start | bytes 786440 | tf_op jit(solution)/shard_map/ppermute | solution.py:31
  (8 other events, 13.4 us)

commit v2 on v1

--- a/solution.py
+++ b/solution.py
@@ -3,14 +3,18 @@
 import jax
 import jax.numpy as jnp
 from jax import lax
+from jax.experimental import pallas as pl
+from jax.experimental.pallas import tpu as pltpu
 from jax.sharding import PartitionSpec as P
 
 AXES = ("tok", "store")
 BF16 = jnp.bfloat16
 F32 = jnp.float32
-
-
-def local(activations, out_grads, validity, proj_in, proj_out, precond, queries, store_rows, plan):
+LANES = 128
+VMEM_LIMIT = 48 * 1024 * 1024
+
+
+def plain(activations, out_grads, validity, proj_in, proj_out, precond, queries, store_rows, plan):
     nt = lax.axis_size("tok")
     ns = lax.axis_size("store")
     nx = ns // 2
@@ -125,6 +129,295 @@
     raw = jnp.take(raw.reshape(ns, -1, raw.shape[1]), order, axis=0)
     scores = raw * plan.astype(F32)[:, :, None]
     return scores.reshape(-1, raw.shape[2]), precond_docs, doc_scores
+
+
+def place():
+    t, s = lax.axis_index("tok"), lax.axis_index("store")
+    return t, s, s // 2, s % 2
+
+
+def dot_nt(a, b):
+    return lax.dot_general(a, b, (((1,), (1,)), ((), ())), preferred_element_type=F32)
+
+
+def call(body, out, *args, scratch=(), flops=0):
+    moved = sum(a.size * a.dtype.itemsize for a in args)
+    return pl.pallas_call(
+        body,
+        out_shape=out,
+        scratch_shapes=scratch,
+        compiler_params=pltpu.CompilerParams(vmem_limit_bytes=VMEM_LIMIT),
+        cost_estimate=pl.CostEstimate(flops=flops, bytes_accessed=moved, transcendentals=0),
+    )(*args)
+
+
+def shape(dims, dtype):
+    return jax.ShapeDtypeStruct(dims, dtype)
+
+
+def pack(nx, w_in, w_out):
+    feat = w_in.shape[1]
+    share = feat // nx
+    k_in, k_out = w_in.shape[0] // 2, w_out.shape[0] // 2
+
+    def body(in_ref, out_ref, piece_ref):
+        _, _, x, core = place()
+        row = lax.broadcasted_iota(jnp.int32, (share, feat), 0) + x * share
+        col = lax.broadcasted_iota(jnp.int32, (share, feat), 1)
+        pick_in = (col == row).astype(BF16)
+        pick_out = (col == (row % (feat // 2)) * 2 + row // (feat // 2)).astype(BF16)
+        piece_ref[:, :k_in] = dot_nt(pick_in, in_ref[pl.ds(core * k_in, k_in), :]).astype(BF16)
+        piece_ref[:, k_in:] = dot_nt(pick_out, out_ref[pl.ds(core * k_out, k_out), :]).astype(BF16)
+
+    return call(body, shape((share, k_in + k_out), BF16), w_in, w_out)
+
+
+def split(nt, acts, grads, k_in, k_out):
+    def body(act_ref, grad_ref, half_ref):
+        _, _, _, core = place()
+        for ref, k, base in ((act_ref, k_in, 0), (grad_ref, k_out, nt * k_in)):
+            for i in range(nt):
+                at = pl.multiple_of(i * 2 * k + (1 - core) * k, LANES)
+                half_ref[:, base + i * k : base + (i + 1) * k] = ref[:, pl.ds(at, k)]
+
+    return call(body, shape((acts.shape[0], nt * (k_in + k_out)), BF16), acts, grads)
+
+
+def project(nt, nx, acts, grads, theirs, blocks, k_in, k_out):
+    n_tok = acts.shape[0]
+    share = blocks[0][0].shape[1]
+    feat = share * nx
+    flat = [b for row in blocks for b in row]
+
+    def body(act_ref, grad_ref, theirs_ref, *refs):
+        block_refs, (mine_ref, other_ref, w_ref) = refs[: len(flat)], refs[len(flat) :]
+        t, _, x, core = place()
+        left = jnp.zeros((2 * n_tok, feat), F32)
+        right = jnp.zeros((feat, 2 * n_tok), F32)
+        for dt in range(nt):
+            slot = dt * feat
+            for dx in range(nx):
+                at = pl.multiple_of(slot + (x ^ dx) * share, share)
+                w_ref[pl.ds(at, share), :] = block_refs[(dt % 2) * nx + dx][dt // 2]
+            i = t ^ dt
+
+            def inputs(ref, k, base):
+                own = ref[:, pl.ds(pl.multiple_of((2 * i + core) * k, LANES), k)]
+                got = theirs_ref[:, pl.ds(pl.multiple_of(base + i * k, LANES), k)]
+                return jnp.concatenate([own, got], axis=0)
+
+            w = w_ref[slot : slot + feat, :]
+            left += dot_nt(inputs(act_ref, k_in, 0), w[:, :k_in])
+            right += dot_nt(w[:, k_in:], inputs(grad_ref, k_out, nt * k_in))
+        mine_ref[...] = jnp.concatenate([right[:, :n_tok], left[:n_tok]], axis=1)
+        other_ref[...] = jnp.concatenate([right[:, n_tok:], left[n_tok:]], axis=1)
+
+    out = shape((feat, n_tok + feat), F32)
+    return call(
+        body,
+        (out, out),
+        acts,
+        grads,
+        theirs,
+        *flat,
+        scratch=[pltpu.VMEM((nt * feat, k_in + k_out), BF16)],
+    )
+
+
+def outer(mine, got, validity):
+    docs, toks = validity.shape
+    feat = mine.shape[0]
+    half = feat // 2
+
+    def body(mine_ref, got_ref, valid_ref, out_ref):
+        both = (mine_ref[...] + got_ref[...]).astype(BF16)
+        for d in range(docs):
+            mask = valid_ref[d : d + 1, :].astype(F32).astype(BF16)
+            right = both[:, d * toks : (d + 1) * toks] * mask
+            left = both[d * toks : (d + 1) * toks, docs * toks :]
+            parts = [
+                jnp.dot(right[n * half : (n + 1) * half], left, preferred_element_type=F32) for n in (0, 1)
+            ]
+            out_ref[d * half : (d + 1) * half, :] = jnp.concatenate(parts, axis=1)
+
+    return call(body, shape((docs * half, 2 * feat), F32), mine, got, validity)
+
+
+def rows_from(ref, n, half):
+    parts = [ref[pl.ds(j, n, stride=half), :] for j in range(half)]
+    return jnp.concatenate(parts, axis=1).astype(BF16)
+
+
+def precondition(grads, p_own, p_got, docs):
+    nx = len(grads)
+    high = grads[0].shape[0]
+    cols = p_own.shape[0]
+
+    def body(*refs):
+        g_refs, (own_ref, got_ref), outs, wide = refs[:nx], refs[nx : nx + 2], refs[nx + 2 : -1], refs[-1]
+        _, _, _, core = place()
+        for n in range(nx):
+            wide[n * high : (n + 1) * high, :] = g_refs[n][...].astype(F32)
+        rows = rows_from(wide, nx * docs, high // docs)
+        for p_ref, c in ((own_ref, core), (got_ref, 1 - core)):
+            res = dot_nt(rows, p_ref[...])
+            for n in range(nx):
+                outs[n][:, pl.ds(pl.multiple_of(c * cols, LANES), cols)] = res[n * docs : (n + 1) * docs]
+
+    return call(
+        body,
+        tuple(shape((docs, 2 * cols), F32) for _ in grads),
+        *grads,
+        p_own,
+        p_got,
+        scratch=[pltpu.VMEM((nx * high, LANES), F32)],
+    )
+
+
+def query_products(queries, p_own, p_got):
+    nx = len(queries)
+    n_q = queries[0].shape[0]
+    cols = p_own.shape[0]
+
+    def body(*refs):
+        q_refs, (own_ref, got_ref), outs = refs[:nx], refs[nx : nx + 2], refs[nx + 2 :]
+        _, _, _, core = place()
+        for p_ref, c in ((own_ref, core), (got_ref, 1 - core)):
+            at = pl.ds(pl.multiple_of(c * cols, LANES), cols)
+            for n in range(nx):
+                outs[n][:, at] = dot_nt(q_refs[n][...], p_ref[...]).astype(BF16)
+
+    return call(body, tuple(shape((n_q, 2 * cols), BF16) for _ in queries), *queries, p_own, p_got)
+
+
+def line_up(near, far):
+    half, nx, n_q, cols = near.shape
+
+    def body(near_ref, far_ref, out_ref):
+        t, _, x, _ = place()
+        for dy, ref in enumerate((near_ref, far_ref)):
+            for n in range(half):
+                for dx in range(nx):
+                    at = ((t ^ (2 * n + dy)) * nx + (x ^ dx)) * cols
+                    out_ref[:, pl.ds(pl.multiple_of(at, LANES), cols)] = ref[n, dx]
+
+    return call(body, shape((n_q, 2 * half * nx * cols), BF16), near, far)
+
+
+def score_docs(products, grads, grads_got, docs):
+    nx = len(grads)
+    high = grads[0].shape[0]
+
+    def body(prod_ref, *refs):
+        g_refs, got_ref, out_ref, wide = refs[:nx], refs[nx], refs[nx + 1], refs[nx + 2]
+        _, s, _, _ = place()
+        for n in range(nx):
+            for c, g in ((0, g_refs[n][...]), (1, got_ref[n])):
+                wide[pl.ds(pl.multiple_of((s ^ (2 * n + c)) * high, high), high), :] = g.astype(F32)
+        rows = rows_from(wide, 2 * nx * docs, high // docs)
+        out_ref[...] = dot_nt(prod_ref[...], rows)
+
+    return call(
+        body,
+        shape((products.shape[0], 2 * nx * docs), F32),
+        products,
+        *grads,
+        grads_got,
+        scratch=[pltpu.VMEM((2 * nx * high, LANES), F32)],
+    )
+
+
+def score_rows(queries, store_rows, plan):
+    ns = len(queries)
+    n_q, width = queries[0].shape
+    n_rows = store_rows.shape[0]
+    step = 4 * LANES
+
+    def body(*refs):
+        q_refs, (rows_ref, plan_ref, out_ref, q_all) = refs[:ns], refs[ns:]
+        _, s, _, _ = place()
+        for n in range(ns):
+            q_all[pl.ds(pl.multiple_of((s ^ n) * n_q, n_q), n_q), :] = q_refs[n][...]
+        total = jnp.zeros((ns * n_q, n_rows), F32)
+        for k in range(0, width, step):
+            rows = rows_ref[:, k : k + step]
+            high = rows.astype(BF16)
+            low = (rows - high.astype(F32)).astype(BF16)
+            q = q_all[:, k : k + step]
+            total += dot_nt(q, high) + dot_nt(q, low)
+        for n in range(ns):
+            weight = plan_ref[n : n + 1, :].astype(F32)
+            out_ref[n * n_q : (n + 1) * n_q, :] = total[n * n_q : (n + 1) * n_q] * weight
+
+    return call(
+        body,
+        shape((ns * n_q, n_rows), F32),
+        *queries,
+        store_rows,
+        plan,
+        scratch=[pltpu.VMEM((ns * n_q, width), BF16)],
+        flops=4 * ns * n_q * width * n_rows,
+    )
+
+
+def tiled(activations, out_grads, validity, proj_in, proj_out, precond, queries, store_rows, plan):
+    nt = lax.axis_size("tok")
+    ns = lax.axis_size("store")
+    nx = ns // 2
+    docs, toks = activations.shape[:2]
+    z_offs = list(range(0, nt, 2))
+    x_offs = list(range(0, ns, 2))
+
+    def send(value, dt, ds):
+        perm = [(i * ns + j, (i ^ dt) * ns + (j ^ ds)) for i in range(nt) for j in range(ns)]
+        return lax.ppermute(value, AXES, perm)
+
+    k_in, k_out = proj_in.shape[0] // 2, proj_out.shape[0] // 2
+    acts = activations.reshape(docs * toks, -1)
+    grads = out_grads.reshape(docs * toks, -1)
+
+    q_x = [queries] + [send(queries, 0, o) for o in x_offs[1:]]
+    mine = pack(nx, proj_in, proj_out)
+    near = jnp.stack([mine] + [send(mine, o, 0) for o in z_offs[1:]])
+    theirs = send(split(nt, acts, grads, k_in, k_out), 0, 1)
+    blocks = [[near if (dy, dx) == (0, 0) else send(near, dy, dx) for dx in x_offs] for dy in (0, 1)]
+    p_got = send(precond, 0, 1)
+    q_core = [send(q, 0, 1) for q in q_x]
+
+    own, other = project(nt, nx, acts, grads, theirs, blocks, k_in, k_out)
+    part = outer(own, send(other, 0, 1), validity)
+
+    terms = [part] + [send(part, o, 0) for o in z_offs[1:]]
+    while len(terms) > 1:
+        terms = [terms[i] + terms[i + 1] for i in range(0, len(terms), 2)]
+    total = terms[0]
+    total = total + send(total, 1, 0)
+    g_own = (total * (1.0 / math.sqrt(toks * nt))).astype(BF16)
+    g_x = [g_own] + [send(g_own, 0, o) for o in x_offs[1:]]
+
+    pre = precondition(g_x, precond, p_got, docs)
+    pre = jnp.stack([pre[0]] + [send(pre[n], 0, o) for n, o in enumerate(x_offs) if n])
+    x = lax.axis_index("store") // 2
+    if nx == 2:
+        pre = jnp.where(x == 0, pre, pre[::-1])
+    else:
+        pre = jnp.take(pre, x ^ jnp.arange(nx), axis=0)
+    precond_docs = pre.transpose(1, 0, 2).reshape(docs, -1)
+
+    qp = query_products(q_x, precond, p_got)
+    qp = jnp.stack([qp[0]] + [send(qp[n], 0, o) for n, o in enumerate(x_offs) if n])
+    qp = jnp.stack([qp] + [send(qp, o, 0) for o in z_offs[1:]])
+    products = line_up(qp, send(qp, 1, 0))
+    doc_scores = score_docs(products, g_x, send(jnp.stack(g_x), 0, 1), docs)
+
+    scores = score_rows([q for pair in zip(q_x, q_core) for q in pair], store_rows, plan)
+    return scores, precond_docs, doc_scores
+
+
+def local(*args):
+    rows_in, rows_out = args[3].shape[0], args[4].shape[0]
+    whole_tiles = all(n % (2 * LANES) == 0 for n in (rows_in, rows_out)) and args[5].shape[0] % LANES == 0
+    return (tiled if whole_tiles else plain)(*args)
 
 
 def solution(mesh):

time: 147 us -> 83.5 us (0.57)
  local copies, waits for them, and re-layouts: 49.4 us -> 11 us
  other arithmetic: 31.5 us -> 0.72 us
  Pallas kernels: 0 us -> 12.3 us
  matrix products: 10.5 us -> 0 us
  waiting for transfers between devices: 27.7 us -> 31.2 us
    gather x15 -> x0, local copies, waits for them, and re-layouts: 20.6 us -> none  [the longest x8 16.4 us: local(): w = jnp.take(w, x ^ jnp.arange(nx), axis=0).reshape(feat, k_in + k_out)]
    concatenate x7 -> x0, other arithmetic: 17.7 us -> none  [the longest x4 15.4 us: halves(): return jnp.concatenate([own, send(other, 0, 1)], axis=0)]
    pallas_call x0 -> x9, Pallas kernels: none -> 12.3 us  [call(): pl.pallas_call(body, out_shape=out, scratch_shapes=scratch, compiler_para...]
    dot_general x22 -> x0, matrix products: 10.5 us -> none  [the longest x8 4.85 us: local(): lax.dot_general(grad, w[:, k_in:], nt_dims, preferred_element_type=F32)]
    another operation x11 -> x5, other arithmetic: 8.52 us -> 0.1 us  [the longest x1 0.05 us: tiled(): near = jnp.stack([mine] + [send(mine, o, 0) for o in z_offs[1:]])]
    dynamic_slice x2 -> x0, local copies, waits for them, and re-layouts: 7.46 us -> none  [halves(): lax.dynamic_slice(view, (0, 0, 1 - core, 0), (n_tok, nt, 1, k))[:, :, 0]]
    reshape x8 -> x0, local copies, waits for them, and re-layouts: 6.94 us -> none  [the longest x2 6.01 us: halves(): view = a.reshape(n_tok, nt, 2, k)]
    unnamed x38 -> x26, local copies, waits for them, and re-layouts: 7.4 us -> 11 us
  transfers between devices with their start and end apart: 24 -> 24, of which waited for: 9 -> 8; matrix products, arithmetic and copies ran while one was open for 57% -> 5% of each run, Pallas kernels for 0% -> 13%
where the time goes in v2:
time: 83.5 us; the launch traced here: 82.9 us
  waiting for transfers between devices  31.2 us (37%)
  starting transfers between devices  26.9 us (32%)
  Pallas kernels  12.3 us (15%)
  local copies, waits for them, and re-layouts  11 us (13%)
    ppermute x24, waiting for transfers between devices, send(): return lax.ppermute(value, AXES, perm)  31.2 us
    ppermute x24, starting transfers between devices, send(): return lax.ppermute(value, AXES, perm)  26.9 us
    pallas_call x9, Pallas kernels, call(): pl.pallas_call(body, out_shape=out, scratch_shapes=scratch, compiler_para...  12.3 us
    unnamed x26, local copies, waits for them, and re-layouts  11 us
  transfers between devices with their start and end apart: 24, of which 8 were waited for; matrix products, arithmetic and copies ran while one was open for 5% of the time, Pallas kernels for 13%

profile of v2, /device:TPU:0, one launch (start us, length us, event | category | flops | bytes accessed | tf_op | source)
XLA Modules:
  0.0 82.9 jit_solution(16208114581973528802)
XLA Ops:
  0.6 1.5 %copy-done = bf16[2,32,14336]{2,1,0:T(8,128)(2,1)S(1)} copy-done((bf16[2,32,14336]{2,1,0:T(8,128)(2,1)S(1)}, bf16[2,32,14336]{2,1,0:T(8,128)(2,1)}, u32[]{:S(2)}) %copy-start) | copy-done | bytes 1835032
  2.1 1.0 %copy-done.3 = bf16[2,32,4096]{2,1,0:T(8,128)(2,1)S(1)} copy-done((bf16[2,32,4096]{2,1,0:T(8,128)(2,1)S(1)}, bf16[2,32,4096]{2,1,0:T(8,128)(2,1)}, u32[]{:S(2)}) %copy-start.3) | copy-done | bytes 524312
  3.2 1.2 %shard_map.113 = bf16[64,9216]{1,0:T(8,128)(2,1)} custom-call(bf16[64,14336]{1,0:T(8,128)(2,1)S(1)} %bitcast.20, bf16[64,4096]{1,0:T(8,128)(2,1)S(1)} %bitcast.22), custom_call_target="tpu_custom_call" | custom-call | bytes 2359296 | tf_op jit(solution)/shard_map/pallas_call | solution.py:145
  4.8 2.0 %copy.13.in_ref = bf16[1792,64]{1,0:T(8,128)(2,1)} copy(bf16[1792,64]{0,1:T(8,128)(2,1)} %param.12) | data formatting | bytes 458752 | tf_op args[3]
  6.8 1.0 %copy.14.out_ref = bf16[512,64]{1,0:T(8,128)(2,1)S(1)} copy(bf16[512,64]{0,1:T(8,128)(2,1)} %param.13) | data formatting | bytes 131072 | tf_op args[4]
  7.8 1.0 %copy-done.8 = bf16[1792,64]{1,0:T(8,128)(2,1)S(1)} copy-done((bf16[1792,64]{1,0:T(8,128)(2,1)S(1)}, bf16[1792,64]{1,0:T(8,128)(2,1)}, u32[]{:S(2)}) %copy-start.8) | copy-done | bytes 229400
  9.0 4.7 %collective-permute-start.6 = (bf16[32,1152]{1,0:T(8,128)(2,1)S(1)}, bf16[32,1152]{1,0:T(8,128)(2,1)S(1)}, u32[]{:S(2)}, u32[]{:S(2)}) collective-permute-start(bf16[32,1152]{1,0:T(8,128)(2,1)S(1)} %shard_map.114), channel_id=1, source_target_pairs={{0,24},{1,25},{2,26},{3,27},{4,28},{5,29},{6,30},{7,31},{8,16},{9,... | collective-permute-start | bytes 221192 | tf_op jit(solution)/shard_map/ppermute | solution.py:373
  14.4 1.6 %collective-permute-start.1 = (bf16[64,4096]{1,0:T(8,128)(2,1)}, bf16[64,4096]{1,0:T(8,128)(2,1)}, u32[]{:S(2)}, u32[]{:S(2)}) collective-permute-start(bf16[64,4096]{1,0:T(8,128)(2,1)} %refs_0_.3), channel_id=1, source_target_pairs={{0,2},{1,3},{2,0},{3,1},{4,6},{5,7},{6,4},{7,5},{8,10},{9,11},{10,... | collective-permute-start | bytes 1572872 | tf_op jit(solution)/shard_map/ppermute | solution.py:373
  16.0 0.9 %collective-permute-done.6 = bf16[32,1152]{1,0:T(8,128)(2,1)S(1)} collective-permute-done((bf16[32,1152]{1,0:T(8,128)(2,1)S(1)}, bf16[32,1152]{1,0:T(8,128)(2,1)S(1)}, u32[]{:S(2)}, u32[]{:S(2)}) %collective-permute-start.6) | collective-permute-done | bytes 73760 | tf_op jit(solution)/shard_map/ppermute | solution.py:373
  16.9 3.5 %collective-permute-done.5 = bf16[32,1152]{1,0:T(8,128)(2,1)S(1)} collective-permute-done((bf16[32,1152]{1,0:T(8,128)(2,1)S(1)}, bf16[32,1152]{1,0:T(8,128)(2,1)S(1)}, u32[]{:S(2)}, u32[]{:S(2)}) %collective-permute-start.5) | collective-permute-done | bytes 73760 | tf_op jit(solution)/shard_map/ppermute | solution.py:373
  20.5 1.6 %collective-permute-start.7 = (bf16[4,32,1152]{2,1,0:T(8,128)(2,1)S(1)}, bf16[4,32,1152]{2,1,0:T(8,128)(2,1)S(1)}, u32[]{:S(2)}, u32[]{:S(2)}) collective-permute-start(bf16[4,32,1152]{2,1,0:T(8,128)(2,1)S(1)} %pad_maximum_fusion.refs_0_), channel_id=1, source_target_pairs={{0,2},{1,3},{2,0},{3,1},{4,6},{5,7},{6,4},{7,5},{8,10},{9,11},{10,... | collective-permute-start | bytes 884744 | tf_op jit(solution)/shard_map/ppermute | solution.py:373
  22.0 1.5 %collective-permute-start.8 = (bf16[4,32,1152]{2,1,0:T(8,128)(2,1)S(1)}, bf16[4,32,1152]{2,1,0:T(8,128)(2,1)S(1)}, u32[]{:S(2)}, u32[]{:S(2)}) collective-permute-start(bf16[4,32,1152]{2,1,0:T(8,128)(2,1)S(1)} %pad_maximum_fusion.refs_0_), channel_id=1, source_target_pairs={{0,4},{1,5},{2,6},{3,7},{4,0},{5,1},{6,2},{7,3},{8,12},{9,13},{10,... | collective-permute-start | bytes 884744 | tf_op jit(solution)/shard_map/ppermute | solution.py:373
  23.6 11.0 %collective-permute-done.7.refs_1_ = bf16[4,32,1152]{2,1,0:T(8,128)(2,1)S(1)} collective-permute-done((bf16[4,32,1152]{2,1,0:T(8,128)(2,1)S(1)}, bf16[4,32,1152]{2,1,0:T(8,128)(2,1)S(1)}, u32[]{:S(2)}, u32[]{:S(2)}) %collective-permute-start.7) | collective-permute-done | bytes 294944 | tf_op jit(solution)/shard_map/ppermute | solution.py:373
  35.0 2.4 %collective-permute-start.9 = (bf16[4,32,1152]{2,1,0:T(8,128)(2,1)S(1)}, bf16[4,32,1152]{2,1,0:T(8,128)(2,1)S(1)}, u32[]{:S(2)}, u32[]{:S(2)}) collective-permute-start(bf16[4,32,1152]{2,1,0:T(8,128)(2,1)S(1)} %pad_maximum_fusion.refs_0_), channel_id=1, source_target_pairs={{0,6},{1,7},{2,4},{3,5},{4,2},{5,3},{6,0},{7,1},{8,14},{9,15},{10,... | collective-permute-start | bytes 884744 | tf_op jit(solution)/shard_map/ppermute | solution.py:373
  37.5 7.4 %collective-permute-done.9.refs_3_ = bf16[4,32,1152]{2,1,0:T(8,128)(2,1)S(1)} collective-permute-done((bf16[4,32,1152]{2,1,0:T(8,128)(2,1)S(1)}, bf16[4,32,1152]{2,1,0:T(8,128)(2,1)S(1)}, u32[]{:S(2)}, u32[]{:S(2)}) %collective-permute-start.9) | collective-permute-done | bytes 294944 | tf_op jit(solution)/shard_map/ppermute | solution.py:373
  44.9 2.2 %shard_map.115 = (f32[64,128]{1,0:T(8,128)S(1)}, f32[64,128]{1,0:T(8,128)S(1)}) custom-call(bf16[64,14336]{1,0:T(8,128)(2,1)S(1)} %bitcast.21, bf16[64,4096]{1,0:T(8,128)(2,1)S(1)} %bitcast.23, bf16[64,9216]{1,0:T(8,128)(2,1)} %collective-permute-done.3.theirs_ref, bf16[4,32,1152]{2,1,0:T(8,128)(2,1)S(1)} %pad_maximum_fusion.refs_0_, ...), custom_call_target="tpu_custom_call" | custom-call | bytes 4718592 | tf_op jit(solution)/shard_map/pallas_call | solution.py:145
  47.3 1.0 %copy-done.6 = bf16[64,4096]{1,0:T(8,128)(2,1)S(1)} copy-done((bf16[64,4096]{1,0:T(8,128)(2,1)S(1)}, bf16[64,4096]{1,0:T(8,128)(2,1)}, u32[]{:S(2)}) %copy-start.6) | copy-done | bytes 524312
  48.3 2.9 %shard_map.118 = (bf16[64,256]{1,0:T(8,128)(2,1)S(1)}, bf16[64,256]{1,0:T(8,128)(2,1)S(1)}) custom-call(bf16[64,4096]{1,0:T(8,128)(2,1)S(1)} %copy-done.6, bf16[64,4096]{1,0:T(8,128)(2,1)} %collective-permute-done.1.refs_2_.refs_1_, bf16[128,4096]{1,0:T(8,128)(2,1)S(1)} %copy-done.2, bf16[128,4096]{1,0:T(8,128)(2,1)} %collective-permute-done.16.refs_3_), custom_call_target="tpu_custom_call" | custom-call | bytes 3145728 | tf_op jit(solution)/shard_map/pallas_call | solution.py:145
  51.3 1.6 %collective-permute-start.18 = (bf16[64,256]{1,0:T(8,128)(2,1)S(1)}, bf16[64,256]{1,0:T(8,128)(2,1)S(1)}, u32[]{:S(2)}, u32[]{:S(2)}) collective-permute-start(bf16[64,256]{1,0:T(8,128)(2,1)S(1)} %get-tuple-element.14), channel_id=1, source_target_pairs={{0,2},{1,3},{2,0},{3,1},{4,6},{5,7},{6,4},{7,5},{8,10},{9,11},{10,... | collective-permute-start | bytes 98312 | tf_op jit(solution)/shard_map/ppermute | solution.py:373
  53.2 2.3 %collective-permute-start.12 = (f32[64,128]{1,0:T(8,128)S(1)}, f32[64,128]{1,0:T(8,128)S(1)}, u32[]{:S(2)}, u32[]{:S(2)}) collective-permute-start(f32[64,128]{1,0:T(8,128)S(1)} %shard_map.116), channel_id=1, source_target_pairs={{0,16},{1,17},{2,18},{3,19},{4,20},{5,21},{6,22},{7,23},{8,24},{9,... | collective-permute-start | bytes 98312 | tf_op jit(solution)/shard_map/ppermute | solution.py:373
  55.5 1.4 %collective-permute-start.13 = (f32[64,128]{1,0:T(8,128)S(1)}, f32[64,128]{1,0:T(8,128)S(1)}, u32[]{:S(2)}, u32[]{:S(2)}) collective-permute-start(f32[64,128]{1,0:T(8,128)S(1)} %shard_map.116), channel_id=1, source_target_pairs={{0,24},{1,25},{2,26},{3,27},{4,28},{5,29},{6,30},{7,31},{8,16},{9,... | collective-permute-start | bytes 98312 | tf_op jit(solution)/shard_map/ppermute | solution.py:373
  57.2 1.6 %copy-done.5 = f32[128,4096]{1,0:T(8,128)S(1)} copy-done((f32[128,4096]{1,0:T(8,128)S(1)}, f32[128,4096]{1,0:T(8,128)}, u32[]{:S(2)}) %copy-start.5) | copy-done | bytes 2097176
  58.8 1.0 %copy-done.7 = bf16[64,4096]{1,0:T(8,128)(2,1)S(1)} copy-done((bf16[64,4096]{1,0:T(8,128)(2,1)S(1)}, bf16[64,4096]{1,0:T(8,128)(2,1)}, u32[]{:S(2)}) %copy-start.7) | copy-done | bytes 524312
  59.9 3.4 %shard_map.112 = f32[256,128]{1,0:T(8,128)} custom-call(bf16[64,4096]{1,0:T(8,128)(2,1)S(1)} %copy-done.7, bf16[64,4096]{1,0:T(8,128)(2,1)} %collective-permute-done.refs_1_, bf16[64,4096]{1,0:T(8,128)(2,1)} %collective-permute-done.1.refs_2_.refs_1_, bf16[64,4096]{1,0:T(8,128)(2,1)} %collective-permute-done.2.refs_3_, f32[128,4096]{1,0:T(8,128)S(1)} %copy-done.5, ...), custom_call_target="tpu_custom_call" | custom-call | flops 536870912 | bytes 4194320 | tf_op jit(solution)/shard_map/pallas_call | solution.py:145
  63.3 1.6 %collective-permute-start.14 = (f32[64,128]{1,0:T(8,128)S(1)}, f32[64,128]{1,0:T(8,128)S(1)}, u32[]{:S(2)}, u32[]{:S(2)}) collective-permute-start(f32[64,128]{1,0:T(8,128)S(1)} %add_add_fusion), channel_id=1, source_target_pairs={{0,4},{1,5},{2,6},{3,7},{4,0},{5,1},{6,2},{7,3},{8,12},{9,13},{10,... | collective-permute-start | bytes 98312 | tf_op jit(solution)/shard_map/ppermute | solution.py:373
  64.9 3.0 %collective-permute-start.21 = (bf16[2,64,256]{2,1,0:T(8,128)(2,1)S(1)}, bf16[2,64,256]{2,1,0:T(8,128)(2,1)S(1)}, u32[]{:S(2)}, u32[]{:S(2)}) collective-permute-start(bf16[2,64,256]{2,1,0:T(8,128)(2,1)S(1)} %get-tuple-element.19), channel_id=1, source_target_pairs={{0,24},{1,25},{2,26},{3,27},{4,28},{5,29},{6,30},{7,31},{8,16},{9,... | collective-permute-start | bytes 196616 | tf_op jit(solution)/shard_map/ppermute | solution.py:373
  68.2 1.2 %collective-permute-start.19 = (bf16[2,64,256]{2,1,0:T(8,128)(2,1)S(1)}, bf16[2,64,256]{2,1,0:T(8,128)(2,1)S(1)}, u32[]{:S(2)}, u32[]{:S(2)}) collective-permute-start(bf16[2,64,256]{2,1,0:T(8,128)(2,1)S(1)} %get-tuple-element.19), channel_id=1, source_target_pairs={{0,8},{1,9},{2,10},{3,11},{4,12},{5,13},{6,14},{7,15},{8,0},{9,1},... | collective-permute-start | bytes 196616 | tf_op jit(solution)/shard_map/ppermute | solution.py:373
  70.0 1.4 %collective-permute-done.21 = bf16[2,64,256]{2,1,0:T(8,128)(2,1)S(1)} collective-permute-done((bf16[2,64,256]{2,1,0:T(8,128)(2,1)S(1)}, bf16[2,64,256]{2,1,0:T(8,128)(2,1)S(1)}, u32[]{:S(2)}, u32[]{:S(2)}) %collective-permute-start.21) | collective-permute-done | bytes 65568 | tf_op jit(solution)/shard_map/ppermute | solution.py:373
  71.4 2.5 %collective-permute-done.20 = bf16[2,64,256]{2,1,0:T(8,128)(2,1)S(1)} collective-permute-done((bf16[2,64,256]{2,1,0:T(8,128)(2,1)S(1)}, bf16[2,64,256]{2,1,0:T(8,128)(2,1)S(1)}, u32[]{:S(2)}, u32[]{:S(2)}) %collective-permute-start.20) | collective-permute-done | bytes 65568 | tf_op jit(solution)/shard_map/ppermute | solution.py:373
  74.5 1.9 %shard_map.117 = (f32[2,256]{1,0:T(2,128)S(1)}, f32[2,256]{1,0:T(2,128)S(1)}) custom-call(bf16[64,128]{1,0:T(8,128)(2,1)S(1)} %multiply_convert_fusion.refs_0_, bf16[64,128]{1,0:T(8,128)(2,1)S(1)} %collective-permute-done.15.refs_1_, bf16[128,4096]{1,0:T(8,128)(2,1)S(1)} %copy-done.2, bf16[128,4096]{1,0:T(8,128)(2,1)} %collective-permute-done.16.refs_3_), custom_call_target="tpu_custom_call" | custom-call | bytes 2129920 | tf_op jit(solution)/shard_map/pallas_call | solution.py:145
  76.9 3.0 %collective-permute-done.17 = f32[2,256]{1,0:T(2,128)S(1)} collective-permute-done((f32[2,256]{1,0:T(2,128)S(1)}, f32[2,256]{1,0:T(2,128)S(1)}, u32[]{:S(2)}, u32[]{:S(2)}) %collective-permute-start.17) | collective-permute-done | bytes 2080 | tf_op jit(solution)/shard_map/ppermute | solution.py:373
  80.6 1.3 %collective-permute-done.22.far_ref = bf16[4,2,64,256]{3,2,1,0:T(8,128)(2,1)S(1)} collective-permute-done((bf16[4,2,64,256]{3,2,1,0:T(8,128)(2,1)S(1)}, bf16[4,2,64,256]{3,2,1,0:T(8,128)(2,1)S(1)}, u32[]{:S(2)}, u32[]{:S(2)}) %collective-permute-start.22) | collective-permute-done | bytes 262176 | tf_op jit(solution)/shard_map/ppermute | solution.py:373
  (59 shorter events, 6.4 us)
Async XLA Ops:
  0.6 1.5 %copy-start = (bf16[2,32,14336]{2,1,0:T(8,128)(2,1)S(1)}, bf16[2,32,14336]{2,1,0:T(8,128)(2,1)}, u32[]{:S(2)}) copy-start(bf16[2,32,14336]{2,1,0:T(8,128)(2,1)} %param.9) | copy-start | bytes 5505028
  3.2 13.7 %copy-start.2 = (bf16[128,4096]{1,0:T(8,128)(2,1)S(1)}, bf16[128,4096]{1,0:T(8,128)(2,1)}, u32[]{:S(2)}) copy-start(bf16[128,4096]{1,0:T(8,128)(2,1)} %refs_2_.3) | copy-start | bytes 3145732
  3.2 41.8 %copy-start.4 = (bf16[2,32,4096]{2,1,0:T(8,128)(2,1)S(1)}, bf16[2,32,4096]{2,1,0:T(8,128)(2,1)}, u32[]{:S(2)}) copy-start(bf16[2,32,4096]{2,1,0:T(8,128)(2,1)} %param.10) | copy-start | bytes 1572868
  4.3 40.6 %copy-start.1 = (bf16[2,32,14336]{2,1,0:T(8,128)(2,1)S(1)}, bf16[2,32,14336]{2,1,0:T(8,128)(2,1)}, u32[]{:S(2)}) copy-start(bf16[2,32,14336]{2,1,0:T(8,128)(2,1)} %param.9) | copy-start | bytes 5505028
  4.3 40.6 %collective-permute-start.3 = (bf16[64,9216]{1,0:T(8,128)(2,1)}, bf16[64,9216]{1,0:T(8,128)(2,1)}, u32[]{:S(2)}, u32[]{:S(2)}) collective-permute-start(bf16[64,9216]{1,0:T(8,128)(2,1)} %shard_map.113), channel_id=1, source_target_pairs={{0,1},{1,0},{2,3},{3,2},{4,5},{5,4},{6,7},{7,6},{8,9},{9,8},{10,11... | collective-permute-start | bytes 3538952 | tf_op jit(solution)/shard_map/ppermute | solution.py:373
  9.0 7.9 %collective-permute-start.6 = (bf16[32,1152]{1,0:T(8,128)(2,1)S(1)}, bf16[32,1152]{1,0:T(8,128)(2,1)S(1)}, u32[]{:S(2)}, u32[]{:S(2)}) collective-permute-start(bf16[32,1152]{1,0:T(8,128)(2,1)S(1)} %shard_map.114), channel_id=1, source_target_pairs={{0,24},{1,25},{2,26},{3,27},{4,28},{5,29},{6,30},{7,31},{8,16},{9,... | collective-permute-start | bytes 221192 | tf_op jit(solution)/shard_map/ppermute | solution.py:373
  13.7 6.7 %collective-permute-start.5 = (bf16[32,1152]{1,0:T(8,128)(2,1)S(1)}, bf16[32,1152]{1,0:T(8,128)(2,1)S(1)}, u32[]{:S(2)}, u32[]{:S(2)}) collective-permute-start(bf16[32,1152]{1,0:T(8,128)(2,1)S(1)} %shard_map.114), channel_id=1, source_target_pairs={{0,16},{1,17},{2,18},{3,19},{4,20},{5,21},{6,22},{7,23},{8,24},{9,... | collective-permute-start | bytes 221192 | tf_op jit(solution)/shard_map/ppermute | solution.py:373
  13.7 6.7 %collective-permute-start.4 = (bf16[32,1152]{1,0:T(8,128)(2,1)S(1)}, bf16[32,1152]{1,0:T(8,128)(2,1)S(1)}, u32[]{:S(2)}, u32[]{:S(2)}) collective-permute-start(bf16[32,1152]{1,0:T(8,128)(2,1)S(1)} %shard_map.114), channel_id=1, source_target_pairs={{0,8},{1,9},{2,10},{3,11},{4,12},{5,13},{6,14},{7,15},{8,0},{9,1},... | collective-permute-start | bytes 221192 | tf_op jit(solution)/shard_map/ppermute | solution.py:373
  14.4 20.2 %collective-permute-start.1 = (bf16[64,4096]{1,0:T(8,128)(2,1)}, bf16[64,4096]{1,0:T(8,128)(2,1)}, u32[]{:S(2)}, u32[]{:S(2)}) collective-permute-start(bf16[64,4096]{1,0:T(8,128)(2,1)} %refs_0_.3), channel_id=1, source_target_pairs={{0,2},{1,3},{2,0},{3,1},{4,6},{5,7},{6,4},{7,5},{8,10},{9,11},{10,... | collective-permute-start | bytes 1572872 | tf_op jit(solution)/shard_map/ppermute | solution.py:373
  16.9 30.4 %collective-permute-start.16 = (bf16[128,4096]{1,0:T(8,128)(2,1)S(1)}, bf16[128,4096]{1,0:T(8,128)(2,1)}, u32[]{:S(2)}, u32[]{:S(2)}) collective-permute-start(bf16[128,4096]{1,0:T(8,128)(2,1)S(1)} %copy-done.2), channel_id=1, source_target_pairs={{0,1},{1,0},{2,3},{3,2},{4,5},{5,4},{6,7},{7,6},{8,9},{9,8},{10,11... | collective-permute-start | bytes 3145736 | tf_op jit(solution)/shard_map/ppermute | solution.py:373
  20.5 26.7 %copy-start.10 = (s32[4,1]{0,1:T(1,128)S(1)}, s32[4,1]{0,1:T(1,128)}, u32[]{:S(2)}) copy-start(s32[4,1]{0,1:T(1,128)} %param.17) | copy-start | bytes 52
  20.5 14.1 %collective-permute-start.7 = (bf16[4,32,1152]{2,1,0:T(8,128)(2,1)S(1)}, bf16[4,32,1152]{2,1,0:T(8,128)(2,1)S(1)}, u32[]{:S(2)}, u32[]{:S(2)}) collective-permute-start(bf16[4,32,1152]{2,1,0:T(8,128)(2,1)S(1)} %pad_maximum_fusion.refs_0_), channel_id=1, source_target_pairs={{0,2},{1,3},{2,0},{3,1},{4,6},{5,7},{6,4},{7,5},{8,10},{9,11},{10,... | collective-permute-start | bytes 884744 | tf_op jit(solution)/shard_map/ppermute | solution.py:373
  22.0 13.0 %collective-permute-start.8 = (bf16[4,32,1152]{2,1,0:T(8,128)(2,1)S(1)}, bf16[4,32,1152]{2,1,0:T(8,128)(2,1)S(1)}, u32[]{:S(2)}, u32[]{:S(2)}) collective-permute-start(bf16[4,32,1152]{2,1,0:T(8,128)(2,1)S(1)} %pad_maximum_fusion.refs_0_), channel_id=1, source_target_pairs={{0,4},{1,5},{2,6},{3,7},{4,0},{5,1},{6,2},{7,3},{8,12},{9,13},{10,... | collective-permute-start | bytes 884744 | tf_op jit(solution)/shard_map/ppermute | solution.py:373
  34.5 22.4 %collective-permute-start = (bf16[64,4096]{1,0:T(8,128)(2,1)}, bf16[64,4096]{1,0:T(8,128)(2,1)}, u32[]{:S(2)}, u32[]{:S(2)}) collective-permute-start(bf16[64,4096]{1,0:T(8,128)(2,1)} %refs_0_.3), channel_id=1, source_target_pairs={{0,1},{1,0},{2,3},{3,2},{4,5},{5,4},{6,7},{7,6},{8,9},{9,8},{10,11... | collective-permute-start | bytes 1572872 | tf_op jit(solution)/shard_map/ppermute | solution.py:373
  34.5 22.7 %collective-permute-start.2 = (bf16[64,4096]{1,0:T(8,128)(2,1)}, bf16[64,4096]{1,0:T(8,128)(2,1)}, u32[]{:S(2)}, u32[]{:S(2)}) collective-permute-start(bf16[64,4096]{1,0:T(8,128)(2,1)} %collective-permute-done.1.refs_2_.refs_1_), channel_id=1, source_target_pairs={{0,1},{1,0},{2,3},{3,2},{4,5},{5,4},{6,7},{7,6},{8,9},{9,8},{10,11... | collective-permute-start | bytes 1572872 | tf_op jit(solution)/shard_map/ppermute | solution.py:373
  35.0 9.9 %collective-permute-start.9 = (bf16[4,32,1152]{2,1,0:T(8,128)(2,1)S(1)}, bf16[4,32,1152]{2,1,0:T(8,128)(2,1)S(1)}, u32[]{:S(2)}, u32[]{:S(2)}) collective-permute-start(bf16[4,32,1152]{2,1,0:T(8,128)(2,1)S(1)} %pad_maximum_fusion.refs_0_), channel_id=1, source_target_pairs={{0,6},{1,7},{2,4},{3,5},{4,2},{5,3},{6,0},{7,1},{8,14},{9,15},{10,... | collective-permute-start | bytes 884744 | tf_op jit(solution)/shard_map/ppermute | solution.py:373
  47.1 5.7 %copy-start.9 = (s32[2,32]{1,0:T(2,128)S(1)}, s32[2,32]{1,0:T(2,128)}, u32[]{:S(2)}) copy-start(s32[2,32]{1,0:T(2,128)} %valid_ref.1) | copy-start | bytes 772
  47.1 5.7 %collective-permute-start.10 = (f32[64,128]{1,0:T(8,128)S(1)}, f32[64,128]{1,0:T(8,128)S(1)}, u32[]{:S(2)}, u32[]{:S(2)}) collective-permute-start(f32[64,128]{1,0:T(8,128)S(1)} %get-tuple-element.10), channel_id=1, source_target_pairs={{0,1},{1,0},{2,3},{3,2},{4,5},{5,4},{6,7},{7,6},{8,9},{9,8},{10,11... | collective-permute-start | bytes 98312 | tf_op jit(solution)/shard_map/ppermute | solution.py:373
  47.3 1.0 %copy-start.6 = (bf16[64,4096]{1,0:T(8,128)(2,1)S(1)}, bf16[64,4096]{1,0:T(8,128)(2,1)}, u32[]{:S(2)}) copy-start(bf16[64,4096]{1,0:T(8,128)(2,1)} %refs_0_.3) | copy-start | bytes 1572868
  51.3 13.6 %collective-permute-start.18 = (bf16[64,256]{1,0:T(8,128)(2,1)S(1)}, bf16[64,256]{1,0:T(8,128)(2,1)S(1)}, u32[]{:S(2)}, u32[]{:S(2)}) collective-permute-start(bf16[64,256]{1,0:T(8,128)(2,1)S(1)} %get-tuple-element.14), channel_id=1, source_target_pairs={{0,2},{1,3},{2,0},{3,1},{4,6},{5,7},{6,4},{7,5},{8,10},{9,11},{10,... | collective-permute-start | bytes 98312 | tf_op jit(solution)/shard_map/ppermute | solution.py:373
  53.2 10.1 %collective-permute-start.12 = (f32[64,128]{1,0:T(8,128)S(1)}, f32[64,128]{1,0:T(8,128)S(1)}, u32[]{:S(2)}, u32[]{:S(2)}) collective-permute-start(f32[64,128]{1,0:T(8,128)S(1)} %shard_map.116), channel_id=1, source_target_pairs={{0,16},{1,17},{2,18},{3,19},{4,20},{5,21},{6,22},{7,23},{8,24},{9,... | collective-permute-start | bytes 98312 | tf_op jit(solution)/shard_map/ppermute | solution.py:373
  55.5 7.8 %collective-permute-start.13 = (f32[64,128]{1,0:T(8,128)S(1)}, f32[64,128]{1,0:T(8,128)S(1)}, u32[]{:S(2)}, u32[]{:S(2)}) collective-permute-start(f32[64,128]{1,0:T(8,128)S(1)} %shard_map.116), channel_id=1, source_target_pairs={{0,24},{1,25},{2,26},{3,27},{4,28},{5,29},{6,30},{7,31},{8,16},{9,... | collective-permute-start | bytes 98312 | tf_op jit(solution)/shard_map/ppermute | solution.py:373
  56.9 6.3 %collective-permute-start.11 = (f32[64,128]{1,0:T(8,128)S(1)}, f32[64,128]{1,0:T(8,128)S(1)}, u32[]{:S(2)}, u32[]{:S(2)}) collective-permute-start(f32[64,128]{1,0:T(8,128)S(1)} %shard_map.116), channel_id=1, source_target_pairs={{0,8},{1,9},{2,10},{3,11},{4,12},{5,13},{6,14},{7,15},{8,0},{9,1},... | collective-permute-start | bytes 98312 | tf_op jit(solution)/shard_map/ppermute | solution.py:373
  57.2 1.6 %copy-start.5 = (f32[128,4096]{1,0:T(8,128)S(1)}, f32[128,4096]{1,0:T(8,128)}, u32[]{:S(2)}) copy-start(f32[128,4096]{1,0:T(8,128)} %refs_4_.1) | copy-start | bytes 6291460
  63.3 6.1 %collective-permute-start.14 = (f32[64,128]{1,0:T(8,128)S(1)}, f32[64,128]{1,0:T(8,128)S(1)}, u32[]{:S(2)}, u32[]{:S(2)}) collective-permute-start(f32[64,128]{1,0:T(8,128)S(1)} %add_add_fusion), channel_id=1, source_target_pairs={{0,4},{1,5},{2,6},{3,7},{4,0},{5,1},{6,2},{7,3},{8,12},{9,13},{10,... | collective-permute-start | bytes 98312 | tf_op jit(solution)/shard_map/ppermute | solution.py:373
  64.9 6.5 %collective-permute-start.21 = (bf16[2,64,256]{2,1,0:T(8,128)(2,1)S(1)}, bf16[2,64,256]{2,1,0:T(8,128)(2,1)S(1)}, u32[]{:S(2)}, u32[]{:S(2)}) collective-permute-start(bf16[2,64,256]{2,1,0:T(8,128)(2,1)S(1)} %get-tuple-element.19), channel_id=1, source_target_pairs={{0,24},{1,25},{2,26},{3,27},{4,28},{5,29},{6,30},{7,31},{8,16},{9,... | collective-permute-start | bytes 196616 | tf_op jit(solution)/shard_map/ppermute | solution.py:373
  67.9 6.0 %collective-permute-start.20 = (bf16[2,64,256]{2,1,0:T(8,128)(2,1)S(1)}, bf16[2,64,256]{2,1,0:T(8,128)(2,1)S(1)}, u32[]{:S(2)}, u32[]{:S(2)}) collective-permute-start(bf16[2,64,256]{2,1,0:T(8,128)(2,1)S(1)} %get-tuple-element.19), channel_id=1, source_target_pairs={{0,16},{1,17},{2,18},{3,19},{4,20},{5,21},{6,22},{7,23},{8,24},{9,... | collective-permute-start | bytes 196616 | tf_op jit(solution)/shard_map/ppermute | solution.py:373
  68.2 5.8 %collective-permute-start.19 = (bf16[2,64,256]{2,1,0:T(8,128)(2,1)S(1)}, bf16[2,64,256]{2,1,0:T(8,128)(2,1)S(1)}, u32[]{:S(2)}, u32[]{:S(2)}) collective-permute-start(bf16[2,64,256]{2,1,0:T(8,128)(2,1)S(1)} %get-tuple-element.19), channel_id=1, source_target_pairs={{0,8},{1,9},{2,10},{3,11},{4,12},{5,13},{6,14},{7,15},{8,0},{9,1},... | collective-permute-start | bytes 196616 | tf_op jit(solution)/shard_map/ppermute | solution.py:373
  69.3 5.1 %collective-permute-start.15 = (bf16[64,128]{1,0:T(8,128)(2,1)S(1)}, bf16[64,128]{1,0:T(8,128)(2,1)S(1)}, u32[]{:S(2)}, u32[]{:S(2)}) collective-permute-start(bf16[64,128]{1,0:T(8,128)(2,1)S(1)} %multiply_convert_fusion.refs_0_), channel_id=1, source_target_pairs={{0,2},{1,3},{2,0},{3,1},{4,6},{5,7},{6,4},{7,5},{8,10},{9,11},{10,... | collective-permute-start | bytes 49160 | tf_op jit(solution)/shard_map/ppermute | solution.py:373
  74.0 8.0 %collective-permute-start.22 = (bf16[4,2,64,256]{3,2,1,0:T(8,128)(2,1)S(1)}, bf16[4,2,64,256]{3,2,1,0:T(8,128)(2,1)S(1)}, u32[]{:S(2)}, u32[]{:S(2)}) collective-permute-start(bf16[4,2,64,256]{3,2,1,0:T(8,128)(2,1)S(1)} %pad_maximum_fusion.1.near_ref), channel_id=1, source_target_pairs={{0,4},{1,5},{2,6},{3,7},{4,0},{5,1},{6,2},{7,3},{8,12},{9,13},{10,... | collective-permute-start | bytes 786440 | tf_op jit(solution)/shard_map/ppermute | solution.py:373
  76.4 3.6 %collective-permute-start.17 = (f32[2,256]{1,0:T(2,128)S(1)}, f32[2,256]{1,0:T(2,128)S(1)}, u32[]{:S(2)}, u32[]{:S(2)}) collective-permute-start(f32[2,256]{1,0:T(2,128)S(1)} %get-tuple-element.12), channel_id=1, source_target_pairs={{0,2},{1,3},{2,0},{3,1},{4,6},{5,7},{6,4},{7,5},{8,10},{9,11},{10,... | collective-permute-start | bytes 6152 | tf_op jit(solution)/shard_map/ppermute | solution.py:373
  76.9 5.0 %collective-permute-start.23 = (bf16[2,64,128]{2,1,0:T(8,128)(2,1)S(1)}, bf16[2,64,128]{2,1,0:T(8,128)(2,1)S(1)}, u32[]{:S(2)}, u32[]{:S(2)}) collective-permute-start(bf16[2,64,128]{2,1,0:T(8,128)(2,1)S(1)} %pad_maximum_fusion.3), channel_id=1, source_target_pairs={{0,1},{1,0},{2,3},{3,2},{4,5},{5,4},{6,7},{7,6},{8,9},{9,8},{10,11... | collective-permute-start | bytes 98312 | tf_op jit(solution)/shard_map/ppermute | solution.py:373
  (3 other events, 3.1 us)

commit v3 on v1

--- a/solution.py
+++ b/solution.py
@@ -3,14 +3,19 @@
 import jax
 import jax.numpy as jnp
 from jax import lax
+from jax.experimental import pallas as pl
+from jax.experimental.pallas import tpu as pltpu
 from jax.sharding import PartitionSpec as P
 
 AXES = ("tok", "store")
 BF16 = jnp.bfloat16
 F32 = jnp.float32
-
-
-def local(activations, out_grads, validity, proj_in, proj_out, precond, queries, store_rows, plan):
+LANES = 128
+VMEM_LIMIT = 16 * 1024 * 1024
+TOKEN = (8, 128)
+
+
+def plain(activations, out_grads, validity, proj_in, proj_out, precond, queries, store_rows, plan):
     nt = lax.axis_size("tok")
     ns = lax.axis_size("store")
     nx = ns // 2
@@ -125,6 +130,378 @@
     raw = jnp.take(raw.reshape(ns, -1, raw.shape[1]), order, axis=0)
     scores = raw * plan.astype(F32)[:, :, None]
     return scores.reshape(-1, raw.shape[2]), precond_docs, doc_scores
+
+
+def place():
+    t, s = lax.axis_index("tok"), lax.axis_index("store")
+    return t, s, s // 2, s % 2
+
+
+def dot_nt(a, b):
+    return lax.dot_general(a, b, (((1,), (1,)), ((), ())), preferred_element_type=F32)
+
+
+def call(name, body, out, *args, scratch=(), far=(), after=(), vmem=VMEM_LIMIT):
+    def run(*refs):
+        body(*refs[: len(args)], *refs[len(args) + len(after) :])
+
+    moved = sum(a.size * a.dtype.itemsize for a in args)
+    specs = [pl.BlockSpec(memory_space=pl.ANY if n in far else pltpu.VMEM) for n in range(len(args))]
+    return pl.pallas_call(
+        run,
+        name=name,
+        out_shape=out,
+        in_specs=specs + [pl.BlockSpec(memory_space=pltpu.VMEM)] * len(after),
+        scratch_shapes=scratch,
+        compiler_params=pltpu.CompilerParams(vmem_limit_bytes=vmem),
+        cost_estimate=pl.CostEstimate(flops=0, bytes_accessed=moved, transcendentals=0),
+    )(*args, *after)
+
+
+def shape(dims, dtype):
+    return jax.ShapeDtypeStruct(dims, dtype)
+
+
+def pack(nx, w_in, w_out):
+    feat = w_in.shape[0]
+    share = feat // nx
+    k_in, k_out = w_in.shape[1] // 2, w_out.shape[1] // 2
+
+    def body(in_ref, out_ref, piece_ref, wide, sems):
+        _, _, x, core = place()
+        rows = pl.ds(pl.multiple_of(x * share, share), share)
+        cols = pl.ds(pl.multiple_of(core * k_in, LANES), k_in)
+        copy_in = pltpu.make_async_copy(in_ref.at[rows, cols], piece_ref.at[:, :k_in], sems.at[0])
+        cols = pl.ds(pl.multiple_of(core * k_out, LANES), k_out)
+        copy_out = pltpu.make_async_copy(out_ref.at[:, cols], wide, sems.at[1])
+        copy_in.start()
+        copy_out.start()
+        row = lax.broadcasted_iota(jnp.int32, (share, feat), 0) + x * share
+        col = lax.broadcasted_iota(jnp.int32, (share, feat), 1)
+        pick = (col == (row % (feat // 2)) * 2 + row // (feat // 2)).astype(F32).astype(BF16)
+        copy_out.wait()
+        piece_ref[:, k_in:] = jnp.dot(pick, wide[...], preferred_element_type=F32).astype(BF16)
+        copy_in.wait()
+
+    return call(
+        "pack",
+        body,
+        shape((share, k_in + k_out), BF16),
+        w_in,
+        w_out,
+        far=(0, 1),
+        scratch=[pltpu.VMEM((feat, k_out), BF16), pltpu.SemaphoreType.DMA((2,))],
+    )
+
+
+def stack(blocks, after):
+    def body(*refs):
+        for n, ref in enumerate(refs[:-2]):
+            refs[-2][n] = ref[...]
+        refs[-1][...] = jnp.zeros_like(refs[-1])
+
+    out = (shape((len(blocks), *blocks[0].shape), BF16), shape(TOKEN, F32))
+    return call("stack", body, out, *blocks, after=after)
+
+
+def halves(by_x, by_y, n_half, after):
+    nx = len(by_x) + 1
+
+    def body(*refs):
+        ins, outs = refs[:nx], refs[nx:]
+        for n in range(nx - 1):
+            outs[n][...] = ins[n][:n_half]
+        outs[-1][...] = ins[-1][n_half:]
+
+    dims = by_y.shape[1:]
+    out = [shape((n_half, *dims), BF16)] * (nx - 1) + [shape((by_y.shape[0] - n_half, *dims), BF16)]
+    res = call("halves", body, tuple(out), *by_x, by_y, after=after)
+    return res[:-1], res[-1]
+
+
+def project_near(nt, nx, inputs, blocks, k_in, k_out):
+    n_tok = inputs[0].shape[0]
+    share = blocks[0].shape[1]
+    feat = share * nx
+    half = nt // 2
+
+    def body(*refs):
+        in_refs, block_refs = refs[:4], refs[4 : 4 + nx]
+        left_ref, right_ref, rest_ref, both, w_ref, sems = refs[4 + nx :]
+        t, _, x, core = place()
+        copies = []
+        for n, ref in enumerate(in_refs):
+            k, base = ((k_in, 0), (k_out, k_in))[n % 2]
+            row = n // 2 * n_tok
+            for dt in range(nt):
+                src = ref.at[:, pl.ds(pl.multiple_of((2 * (t ^ dt) + core) * k, LANES), k)]
+                dst = both.at[dt] if dt % 2 == 0 else rest_ref.at[dt // 2]
+                dst = dst.at[row : row + n_tok, base : base + k]
+                copies.append(pltpu.make_async_copy(src, dst, sems.at[len(copies)]))
+                copies[-1].start()
+        for n in range(half):
+            for dx in range(nx):
+                w_ref[n, pl.ds(pl.multiple_of((x ^ dx) * share, share), share), :] = block_refs[dx][n]
+        for copy in copies:
+            copy.wait()
+        left = jnp.zeros((2 * n_tok, feat), F32)
+        right = jnp.zeros((feat, 2 * n_tok), F32)
+        for n in range(half):
+            left += dot_nt(both[2 * n, :, :k_in], w_ref[n, :, :k_in])
+            right += dot_nt(w_ref[n, :, k_in:], both[2 * n, :, k_in:])
+        left_ref[...] = left
+        right_ref[...] = right
+
+    return call(
+        "project_near",
+        body,
+        (
+            shape((2 * n_tok, feat), F32),
+            shape((feat, 2 * n_tok), F32),
+            shape((half, 2 * n_tok, k_in + k_out), BF16),
+        ),
+        *inputs,
+        *blocks,
+        far=range(4),
+        scratch=[
+            pltpu.VMEM((nt, 2 * n_tok, k_in + k_out), BF16),
+            pltpu.VMEM((half, feat, k_in + k_out), BF16),
+            pltpu.SemaphoreType.DMA((4 * nt,)),
+        ],
+    )
+
+
+def project_rest(left, right, rest, by_y, firsts, lasts, k_in, after):
+    feat = left.shape[1]
+    n_tok = left.shape[0] // 2
+    n_half, share, k_both = firsts[0].shape
+    far = len(firsts)
+    half = 2 * n_half
+
+    def body(left_ref, right_ref, rest_ref, y_ref, *refs):
+        sides, (mine_ref, other_ref, w_ref) = (refs[:far], refs[far : 2 * far]), refs[2 * far :]
+        _, _, x, _ = place()
+        l, r = left_ref[...], right_ref[...]
+        for n in range(half):
+            w_ref[n, pl.ds(pl.multiple_of(x * share, share), share), :] = y_ref[n]
+            for dx in range(1, far + 1):
+                at = pl.ds(pl.multiple_of((x ^ dx) * share, share), share)
+                w_ref[n, at, :] = sides[n // n_half][dx - 1][n % n_half]
+        for n in range(half):
+            l += dot_nt(rest_ref[n, :, :k_in], w_ref[n, :, :k_in])
+            r += dot_nt(w_ref[n, :, k_in:], rest_ref[n, :, k_in:])
+        mine_ref[...] = jnp.concatenate([r[:, :n_tok], l[:n_tok]], axis=1)
+        other_ref[...] = jnp.concatenate([r[:, n_tok:], l[n_tok:]], axis=1)
+
+    out = shape((feat, n_tok + feat), F32)
+    return call(
+        "project_rest",
+        body,
+        (out, out),
+        left,
+        right,
+        rest,
+        by_y,
+        *firsts,
+        *lasts,
+        after=after,
+        scratch=[pltpu.VMEM((half, feat, k_both), BF16)],
+    )
+
+
+def outer(mine, got, validity):
+    docs, toks = validity.shape
+    feat = mine.shape[0]
+    half = feat // 2
+
+    def body(mine_ref, got_ref, valid_ref, out_ref, token_ref):
+        token_ref[...] = jnp.zeros_like(token_ref)
+        both = (mine_ref[...] + got_ref[...]).astype(BF16)
+        for d in range(docs):
+            mask = valid_ref[d : d + 1, :].astype(F32).astype(BF16)
+            right = both[:, d * toks : (d + 1) * toks] * mask
+            left = both[d * toks : (d + 1) * toks, docs * toks :]
+            parts = [
+                jnp.dot(right[n * half : (n + 1) * half], left, preferred_element_type=F32) for n in (0, 1)
+            ]
+            out_ref[d * half : (d + 1) * half, :] = jnp.concatenate(parts, axis=1)
+
+    return call("outer", body, (shape((docs * half, 2 * feat), F32), shape(TOKEN, F32)), mine, got, validity)
+
+
+def finish(nx, grads, p_own, p_got, queries, docs):
+    ns = len(grads)
+    high = grads[0].shape[0]
+    pairs = high // docs
+    cols = p_own.shape[0]
+    n_q = queries[0].shape[0]
+
+    def body(*refs):
+        g_refs, p_refs, q_refs, outs = refs[:ns], refs[ns : ns + 2], refs[ns + 2 : ns + 2 + nx], refs[ns + 2 + nx : -5]
+        token_ref, wide, pre, q_part, sems = refs[-5:]
+        token_ref[...] = jnp.zeros_like(token_ref)
+        t, s, x, core = place()
+        at = pl.multiple_of((t * nx + x) * 2 * cols, LANES)
+        copies = [
+            pltpu.make_async_copy(q_refs[n].at[:, pl.ds(at, 2 * cols)], q_part.at[n], sems.at[n]) for n in range(nx)
+        ]
+        for copy in copies:
+            copy.start()
+        for n in range(ns):
+            at = pl.multiple_of((s ^ n) * high, high)
+            wide[pl.ds(at, high), :] = g_refs[n][...].astype(F32)
+        rows = [wide[pl.ds(j, ns * docs, stride=pairs), :] for j in range(pairs)]
+        rows = jnp.concatenate(rows, axis=1).astype(BF16)
+        for ref, c in zip(p_refs, (core, 1 - core)):
+            pre[:, pl.ds(pl.multiple_of(c * cols, LANES), cols)] = dot_nt(rows, ref[...])
+        full = pre[...]
+        upper = full.astype(BF16)
+        lower = (full - upper.astype(F32)).astype(BF16)
+        for copy in copies:
+            copy.wait()
+        for n in range(nx):
+            mine = full[:docs]
+            for m in range(1, ns):
+                mine = jnp.where((s ^ (2 * n)) == m, full[m * docs : (m + 1) * docs], mine)
+            outs[n][:docs, :] = mine
+            outs[n][8:, :n_q] = dot_nt(upper, q_part[n]) + dot_nt(lower, q_part[n])
+
+    return call(
+        "finish",
+        body,
+        (*(shape((8 + ns * docs, 2 * cols), F32) for _ in range(nx)), shape(TOKEN, F32)),
+        *grads,
+        p_own,
+        p_got,
+        *queries,
+        far=range(ns + 2, ns + 2 + nx),
+        scratch=[
+            pltpu.VMEM((ns * high, LANES), F32),
+            pltpu.VMEM((ns * docs, 2 * cols), F32),
+            pltpu.VMEM((nx, n_q, 2 * cols), BF16),
+            pltpu.SemaphoreType.DMA((nx,)),
+        ],
+    )
+
+
+def assemble(near, far, docs, n_q, after):
+    nx = len(near)
+    height, cols = near[0].shape
+
+    def body(*refs):
+        near_refs, far_refs, (docs_ref, scores_ref) = refs[:nx], refs[nx : 2 * nx], refs[2 * nx :]
+        _, _, x, _ = place()
+        for n in range(nx):
+            docs_ref[:, pl.ds(pl.multiple_of((x ^ n) * cols, LANES), cols)] = near_refs[n][:docs, :]
+        sums = [sum(ref[8:, :n_q] for ref in side) for side in (near_refs, far_refs)]
+        scores_ref[...] = sums[0] + sums[1]
+
+    out = (shape((docs, nx * cols), F32), shape((height - 8, n_q), F32))
+    return call("assemble", body, out, *near, *far, after=after)
+
+
+def pair_sum(terms, after):
+    def body(*refs):
+        values = [ref[...] for ref in refs[:-1]]
+        while len(values) > 1:
+            values = [values[i] + values[i + 1] for i in range(0, len(values), 2)]
+        refs[-1][...] = values[0]
+
+    return call("pair_sum", body, shape(terms[0].shape, F32), *terms, after=after)
+
+
+def score_rows(queries, store_rows, plan, after):
+    ns = len(queries)
+    n_q, width = queries[0].shape
+    n_rows = store_rows.shape[0]
+    step = 4 * LANES
+
+    def body(*refs):
+        q_refs, (rows_ref, plan_ref, out_ref, q_all) = refs[:ns], refs[ns:]
+        _, s, _, _ = place()
+        for n in range(ns):
+            q_all[pl.ds(pl.multiple_of((s ^ n) * n_q, n_q), n_q), :] = q_refs[n][...]
+        total = jnp.zeros((ns * n_q, n_rows), F32)
+        for k in range(0, width, step):
+            rows = rows_ref[:, k : k + step]
+            high = rows.astype(BF16)
+            low = (rows - high.astype(F32)).astype(BF16)
+            q = q_all[:, k : k + step]
+            total += dot_nt(q, high) + dot_nt(q, low)
+        for n in range(ns):
+            weight = plan_ref[n : n + 1, :].astype(F32)
+            out_ref[n * n_q : (n + 1) * n_q, :] = total[n * n_q : (n + 1) * n_q] * weight
+
+    return call(
+        "score_rows",
+        body,
+        shape((ns * n_q, n_rows), F32),
+        *queries,
+        store_rows,
+        plan,
+        after=after,
+        scratch=[pltpu.VMEM((ns * n_q, width), BF16)],
+    )
+
+
+def tiled(activations, out_grads, validity, proj_in, proj_out, precond, queries, store_rows, plan):
+    nt = lax.axis_size("tok")
+    ns = lax.axis_size("store")
+    nx = ns // 2
+    docs, toks = activations.shape[:2]
+    z_offs = list(range(0, nt, 2))
+    x_offs = list(range(0, ns, 2))
+
+    def send(value, dt, ds):
+        perm = [(i * ns + j, (i ^ dt) * ns + (j ^ ds)) for i in range(nt) for j in range(ns)]
+        return lax.ppermute(value, AXES, perm)
+
+    k_in, k_out = proj_in.shape[0] // 2, proj_out.shape[0] // 2
+    acts = activations.reshape(docs * toks, -1)
+    grads = out_grads.reshape(docs * toks, -1)
+
+    inputs = [acts, grads, send(acts, 0, 1), send(grads, 0, 1)]
+    mine = pack(nx, proj_in.T, proj_out.T)
+    near, token = stack([mine] + [send(mine, o, 0) for o in z_offs[1:]], inputs[2:])
+    token, p_late, q_late = lax.optimization_barrier((token, precond, queries))
+    tokens = [token]
+    p_got = send(p_late, 0, 1)
+    q_near = send(q_late, 0, 1)
+    by_x = [send(near, 0, o) for o in x_offs[1:]]
+    by_y = send(near, 1, 0)
+    firsts, lasts = halves(by_x, by_y, len(z_offs) // 2, [p_got, q_near])
+    firsts = [send(b, 1, 0) for b in firsts]
+    lasts = [send(lasts, 0, o) for o in x_offs[1:]]
+    left, right, rest = project_near(nt, nx, inputs, [near] + by_x, k_in, k_out)
+    own, other = project_rest(left, right, rest, by_y, firsts, lasts, k_in, [])
+    part, token = outer(own, send(other, 0, 1), validity)
+
+    token, q_late = lax.optimization_barrier((token, queries))
+    tokens.append(token)
+    q_x = [queries] + [send(q_late, 0, o) for o in x_offs[1:]]
+
+    total = pair_sum([part] + [send(part, o, 0) for o in z_offs[1:]], [])
+    total = total + send(total, 1, 0)
+    g_own = (total * (1.0 / math.sqrt(toks * nt))).astype(BF16)
+    g_all = [g_own] + [send(g_own, 0, o) for o in range(1, ns)]
+
+    *res, token = finish(nx, g_all, precond, p_got, q_x, docs)
+    token, *q_far = lax.optimization_barrier((token, *q_x[1:]))
+    tokens.append(token)
+    q_core = [q_near] + [send(q, 0, 1) for q in q_far]
+    near = [send(r, 0, o) if o else r for r, o in zip(res, x_offs)]
+    far = [send(r, 1, o) for r, o in zip(res, x_offs)]
+    scores = score_rows([q for pair in zip(q_x, q_core) for q in pair], store_rows, plan, tokens)
+    precond_docs, partial = assemble(near, far, docs, queries.shape[0], [scores])
+    doc_scores = pair_sum([partial] + [send(partial, o, 0) for o in z_offs[1:]], [])
+    return scores, precond_docs, doc_scores.T
+
+
+def local(*args):
+    rows_in, rows_out = args[3].shape[0], args[4].shape[0]
+    whole_tiles = all(n % (2 * LANES) == 0 for n in (rows_in, rows_out)) and args[5].shape[0] % LANES == 0
+    whole_tiles = whole_tiles and lax.axis_size("tok") >= 4 and lax.axis_size("store") >= 4
+    return (tiled if whole_tiles else plain)(*args)
 
 
 def solution(mesh):

time: 147 us -> 67.7 us (0.46)
  local copies, waits for them, and re-layouts: 49.4 us -> 3.86 us
  other arithmetic: 31.5 us -> 0.01 us
  matrix products: 10.5 us -> 0 us
  Pallas kernels: 0 us -> 7.56 us
  starting transfers between devices: 25.8 us -> 29.5 us
  waiting for transfers between devices: 27.7 us -> 25.7 us
    gather x15 -> x0, local copies, waits for them, and re-layouts: 20.6 us -> none  [the longest x8 16.4 us: local(): w = jnp.take(w, x ^ jnp.arange(nx), axis=0).reshape(feat, k_in + k_out)]
    concatenate x7 -> x0, other arithmetic: 17.7 us -> none  [the longest x4 15.4 us: halves(): return jnp.concatenate([own, send(other, 0, 1)], axis=0)]
    dot_general x22 -> x0, matrix products: 10.5 us -> none  [the longest x8 4.85 us: local(): lax.dot_general(grad, w[:, k_in:], nt_dims, preferred_element_type=F32)]
    another operation x11 -> x0, other arithmetic: 8.52 us -> none  [the longest x4 5.88 us: local(): w = jnp.stack([blocks[dt, dx] for dx in x_offs])]
    pallas_call x0 -> x11, Pallas kernels: none -> 7.56 us  [call(): pl.pallas_call(run, name=name, out_shape=out, in_specs=specs + [pl.BlockS...]
    dynamic_slice x2 -> x0, local copies, waits for them, and re-layouts: 7.46 us -> none  [halves(): lax.dynamic_slice(view, (0, 0, 1 - core, 0), (n_tok, nt, 1, k))[:, :, 0]]
    reshape x8 -> x0, local copies, waits for them, and re-layouts: 6.94 us -> none  [the longest x2 6.01 us: halves(): view = a.reshape(n_tok, nt, 2, k)]
    ppermute x24 -> x27, starting transfers between devices: 25.8 us -> 29.5 us  [send(): return lax.ppermute(value, AXES, perm)]
  transfers between devices with their start and end apart: 24 -> 27, of which waited for: 9 -> 14; matrix products, arithmetic and copies ran while one was open for 57% -> 0% of each run, Pallas kernels for 0% -> 7%
where the time goes in v3:
time: 67.7 us; the launch traced here: 67.5 us
  starting transfers between devices  29.5 us (44%)
  waiting for transfers between devices  25.7 us (38%)
  Pallas kernels  7.56 us (11%)
  local copies, waits for them, and re-layouts  3.86 us (6%)
  between operations  0.85 us (1%)
    ppermute x27, starting transfers between devices, send(): return lax.ppermute(value, AXES, perm)  29.5 us
    ppermute x27, waiting for transfers between devices, send(): return lax.ppermute(value, AXES, perm)  25.7 us
    pallas_call x11, Pallas kernels, call(): pl.pallas_call(run, name=name, out_shape=out, in_specs=specs + [pl.BlockS...  7.56 us
    unnamed x25, local copies, waits for them, and re-layouts  3.86 us
  transfers between devices with their start and end apart: 27, of which 14 were waited for; matrix products, arithmetic and copies ran while one was open for 0% of the time, Pallas kernels for 7%

profile of v3, /device:TPU:0, one launch (start us, length us, event | category | flops | bytes accessed | tf_op | source)
XLA Modules:
  0.0 67.5 jit_solution(8804384036644694018)
XLA Ops:
  1.3 0.9 %copy-done.8 = bf16[1792,64]{0,1:T(8,128)(2,1)S(1)} copy-done((bf16[1792,64]{0,1:T(8,128)(2,1)S(1)}, bf16[1792,64]{0,1:T(8,128)(2,1)}, u32[]{:S(2)}) %copy-start.8) | copy-done | bytes 229400
  2.2 0.8 %copy-done.9 = bf16[512,64]{0,1:T(8,128)(2,1)S(1)} copy-done((bf16[512,64]{0,1:T(8,128)(2,1)S(1)}, bf16[512,64]{0,1:T(8,128)(2,1)}, u32[]{:S(2)}) %copy-start.9) | copy-done | bytes 65560
  3.2 5.1 %collective-permute-start.2 = (bf16[32,1152]{1,0:T(8,128)(2,1)S(1)}, bf16[32,1152]{1,0:T(8,128)(2,1)S(1)}, u32[]{:S(2)}, u32[]{:S(2)}) collective-permute-start(bf16[32,1152]{1,0:T(8,128)(2,1)S(1)} %pack.1.refs_0_), channel_id=1, source_target_pairs={{0,24},{1,25},{2,26},{3,27},{4,28},{5,29},{6,30},{7,31},{8,16},{9,... | collective-permute-start | bytes 221192 | tf_op jit(solution)/shard_map/ppermute | solution.py:457
  9.0 2.2 %collective-permute-done.2.refs_3_ = bf16[32,1152]{1,0:T(8,128)(2,1)S(1)} collective-permute-done((bf16[32,1152]{1,0:T(8,128)(2,1)S(1)}, bf16[32,1152]{1,0:T(8,128)(2,1)S(1)}, u32[]{:S(2)}, u32[]{:S(2)}) %collective-permute-start.2) | collective-permute-done | bytes 73760 | tf_op jit(solution)/shard_map/ppermute | solution.py:457
  11.2 3.6 %collective-permute-done.1.refs_2_ = bf16[32,1152]{1,0:T(8,128)(2,1)S(1)} collective-permute-done((bf16[32,1152]{1,0:T(8,128)(2,1)S(1)}, bf16[32,1152]{1,0:T(8,128)(2,1)S(1)}, u32[]{:S(2)}, u32[]{:S(2)}) %collective-permute-start.1) | collective-permute-done | bytes 73760 | tf_op jit(solution)/shard_map/ppermute | solution.py:457
  15.4 1.5 %collective-permute-start.7 = (bf16[4,32,1152]{2,1,0:T(8,128)(2,1)S(1)}, bf16[4,32,1152]{2,1,0:T(8,128)(2,1)S(1)}, u32[]{:S(2)}, u32[]{:S(2)}) collective-permute-start(bf16[4,32,1152]{2,1,0:T(8,128)(2,1)S(1)} %get-tuple-element.28.refs_4_), channel_id=1, source_target_pairs={{0,4},{1,5},{2,6},{3,7},{4,0},{5,1},{6,2},{7,3},{8,12},{9,13},{10,... | collective-permute-start | bytes 884744 | tf_op jit(solution)/shard_map/ppermute | solution.py:457
  16.9 1.5 %collective-permute-start.6 = (bf16[4,32,1152]{2,1,0:T(8,128)(2,1)S(1)}, bf16[4,32,1152]{2,1,0:T(8,128)(2,1)S(1)}, u32[]{:S(2)}, u32[]{:S(2)}) collective-permute-start(bf16[4,32,1152]{2,1,0:T(8,128)(2,1)S(1)} %get-tuple-element.28.refs_4_), channel_id=1, source_target_pairs={{0,2},{1,3},{2,0},{3,1},{4,6},{5,7},{6,4},{7,5},{8,10},{9,11},{10,... | collective-permute-start | bytes 884744 | tf_op jit(solution)/shard_map/ppermute | solution.py:457
  18.4 6.0 %collective-permute-done.7.refs_1_.refs_3_ = bf16[4,32,1152]{2,1,0:T(8,128)(2,1)S(1)} collective-permute-done((bf16[4,32,1152]{2,1,0:T(8,128)(2,1)S(1)}, bf16[4,32,1152]{2,1,0:T(8,128)(2,1)S(1)}, u32[]{:S(2)}, u32[]{:S(2)}) %collective-permute-start.7) | collective-permute-done | bytes 294944 | tf_op jit(solution)/shard_map/ppermute | solution.py:457
  24.4 1.2 %collective-permute-done.6.refs_5_.refs_0_ = bf16[4,32,1152]{2,1,0:T(8,128)(2,1)S(1)} collective-permute-done((bf16[4,32,1152]{2,1,0:T(8,128)(2,1)S(1)}, bf16[4,32,1152]{2,1,0:T(8,128)(2,1)S(1)}, u32[]{:S(2)}, u32[]{:S(2)}) %collective-permute-start.6) | collective-permute-done | bytes 294944 | tf_op jit(solution)/shard_map/ppermute | solution.py:457
  26.3 1.5 %collective-permute-start.10 = (bf16[2,32,1152]{2,1,0:T(8,128)(2,1)S(1)}, bf16[2,32,1152]{2,1,0:T(8,128)(2,1)S(1)}, u32[]{:S(2)}, u32[]{:S(2)}) collective-permute-start(bf16[2,32,1152]{2,1,0:T(8,128)(2,1)S(1)} %get-tuple-element.34), channel_id=1, source_target_pairs={{0,2},{1,3},{2,0},{3,1},{4,6},{5,7},{6,4},{7,5},{8,10},{9,11},{10,... | collective-permute-start | bytes 442376 | tf_op jit(solution)/shard_map/ppermute | solution.py:457
  27.8 1.3 %project_near.1 = (f32[128,64]{1,0:T(8,128)S(1)}, f32[64,128]{1,0:T(8,128)S(1)}, bf16[4,128,1152]{2,1,0:T(8,128)(2,1)S(1)}) custom-call(bf16[64,14336]{1,0:T(8,128)(2,1)S(1)} %bitcast.6, bf16[64,4096]{1,0:T(8,128)(2,1)S(1)} %bitcast.8, bf16[64,14336]{1,0:T(8,128)(2,1)S(1)} %collective-permute-done.3.refs_4_.refs_2_, ...), custom_call_target="tpu_custom_call" | custom-call | bytes 5308416 | tf_op jit(solution)/shard_map/project_near/pallas_call | solution.py:150
  29.1 1.8 %collective-permute-done.9.refs_4_ = bf16[2,32,1152]{2,1,0:T(8,128)(2,1)S(1)} collective-permute-done((bf16[2,32,1152]{2,1,0:T(8,128)(2,1)S(1)}, bf16[2,32,1152]{2,1,0:T(8,128)(2,1)S(1)}, u32[]{:S(2)}, u32[]{:S(2)}) %collective-permute-start.9) | collective-permute-done | bytes 147488 | tf_op jit(solution)/shard_map/ppermute | solution.py:457
  32.1 1.2 %collective-permute-done.11.refs_1_ = f32[64,128]{1,0:T(8,128)S(1)} collective-permute-done((f32[64,128]{1,0:T(8,128)S(1)}, f32[64,128]{1,0:T(8,128)S(1)}, u32[]{:S(2)}, u32[]{:S(2)}) %collective-permute-start.11) | collective-permute-done | bytes 32800 | tf_op jit(solution)/shard_map/ppermute | solution.py:457
  33.6 1.5 %collective-permute-start.12 = (bf16[64,4096]{1,0:T(8,128)(2,1)S(1)}, bf16[64,4096]{1,0:T(8,128)(2,1)S(1)}, u32[]{:S(2)}, u32[]{:S(2)}) collective-permute-start(bf16[64,4096]{1,0:T(8,128)(2,1)S(1)} %copy-done), channel_id=1, source_target_pairs={{0,2},{1,3},{2,0},{3,1},{4,6},{5,7},{6,4},{7,5},{8,10},{9,11},{10,... | collective-permute-start | bytes 1572872 | tf_op jit(solution)/shard_map/ppermute | solution.py:457
  35.1 2.5 %collective-permute-start.15 = (f32[64,128]{1,0:T(8,128)S(1)}, f32[64,128]{1,0:T(8,128)S(1)}, u32[]{:S(2)}, u32[]{:S(2)}) collective-permute-start(f32[64,128]{1,0:T(8,128)S(1)} %get-tuple-element.39.refs_0_), channel_id=1, source_target_pairs={{0,24},{1,25},{2,26},{3,27},{4,28},{5,29},{6,30},{7,31},{8,16},{9,... | collective-permute-start | bytes 98312 | tf_op jit(solution)/shard_map/ppermute | solution.py:457
  37.7 1.9 %collective-permute-start.13 = (f32[64,128]{1,0:T(8,128)S(1)}, f32[64,128]{1,0:T(8,128)S(1)}, u32[]{:S(2)}, u32[]{:S(2)}) collective-permute-start(f32[64,128]{1,0:T(8,128)S(1)} %get-tuple-element.39.refs_0_), channel_id=1, source_target_pairs={{0,8},{1,9},{2,10},{3,11},{4,12},{5,13},{6,14},{7,15},{8,0},{9,1},... | collective-permute-start | bytes 98312 | tf_op jit(solution)/shard_map/ppermute | solution.py:457
  39.5 1.3 %collective-permute-done.15.refs_3_ = f32[64,128]{1,0:T(8,128)S(1)} collective-permute-done((f32[64,128]{1,0:T(8,128)S(1)}, f32[64,128]{1,0:T(8,128)S(1)}, u32[]{:S(2)}, u32[]{:S(2)}) %collective-permute-start.15) | collective-permute-done | bytes 32800 | tf_op jit(solution)/shard_map/ppermute | solution.py:457
  40.9 1.6 %collective-permute-done.14.refs_2_ = f32[64,128]{1,0:T(8,128)S(1)} collective-permute-done((f32[64,128]{1,0:T(8,128)S(1)}, f32[64,128]{1,0:T(8,128)S(1)}, u32[]{:S(2)}, u32[]{:S(2)}) %collective-permute-start.14) | collective-permute-done | bytes 32800 | tf_op jit(solution)/shard_map/ppermute | solution.py:457
  42.5 1.6 %collective-permute-start.16 = (f32[64,128]{1,0:T(8,128)S(1)}, f32[64,128]{1,0:T(8,128)S(1)}, u32[]{:S(2)}, u32[]{:S(2)}) collective-permute-start(f32[64,128]{1,0:T(8,128)S(1)} %pair_sum.2), channel_id=1, source_target_pairs={{0,4},{1,5},{2,6},{3,7},{4,0},{5,1},{6,2},{7,3},{8,12},{9,13},{10,... | collective-permute-start | bytes 98312 | tf_op jit(solution)/shard_map/ppermute | solution.py:457
  44.1 2.4 %collective-permute-done.16 = f32[64,128]{1,0:T(8,128)S(1)} collective-permute-done((f32[64,128]{1,0:T(8,128)S(1)}, f32[64,128]{1,0:T(8,128)S(1)}, u32[]{:S(2)}, u32[]{:S(2)}) %collective-permute-start.16) | collective-permute-done | bytes 32800 | tf_op jit(solution)/shard_map/ppermute | solution.py:457
  47.2 1.2 %collective-permute-start.17 = (bf16[64,128]{1,0:T(8,128)(2,1)S(1)}, bf16[64,128]{1,0:T(8,128)(2,1)S(1)}, u32[]{:S(2)}, u32[]{:S(2)}) collective-permute-start(bf16[64,128]{1,0:T(8,128)(2,1)S(1)} %multiply_convert_fusion.refs_0_), channel_id=1, source_target_pairs={{0,1},{1,0},{2,3},{3,2},{4,5},{5,4},{6,7},{7,6},{8,9},{9,8},{10,11... | collective-permute-start | bytes 49160 | tf_op jit(solution)/shard_map/ppermute | solution.py:457
  48.4 1.3 %collective-permute-done.19.refs_3_ = bf16[64,128]{1,0:T(8,128)(2,1)S(1)} collective-permute-done((bf16[64,128]{1,0:T(8,128)(2,1)S(1)}, bf16[64,128]{1,0:T(8,128)(2,1)S(1)}, u32[]{:S(2)}, u32[]{:S(2)}) %collective-permute-start.19) | collective-permute-done | bytes 16416 | tf_op jit(solution)/shard_map/ppermute | solution.py:457
  50.4 0.9 %finish.1 = (f32[16,256]{1,0:T(8,128)S(1)}, f32[16,256]{1,0:T(8,128)S(1)}, f32[8,128]{1,0:T(8,128)S(1)}) custom-call(bf16[64,128]{1,0:T(8,128)(2,1)S(1)} %multiply_convert_fusion.refs_0_, bf16[64,128]{1,0:T(8,128)(2,1)S(1)} %collective-permute-done.17.refs_1_, bf16[64,128]{1,0:T(8,128)(2,1)S(1)} %collective-permute-done.18.refs_2_, ...), custom_call_target="tpu_custom_call" | custom-call | bytes 3211264 | tf_op jit(solution)/shard_map/finish/pallas_call | solution.py:150
  51.3 1.6 %collective-permute-start.22 = (f32[16,256]{1,0:T(8,128)S(1)}, f32[16,256]{1,0:T(8,128)S(1)}, u32[]{:S(2)}, u32[]{:S(2)}) collective-permute-start(f32[16,256]{1,0:T(8,128)S(1)} %get-tuple-element.45.refs_0_), channel_id=1, source_target_pairs={{0,4},{1,5},{2,6},{3,7},{4,0},{5,1},{6,2},{7,3},{8,12},{9,13},{10,... | collective-permute-start | bytes 49160 | tf_op jit(solution)/shard_map/ppermute | solution.py:457
  53.7 1.2 %collective-permute-start.21 = (f32[16,256]{1,0:T(8,128)S(1)}, f32[16,256]{1,0:T(8,128)S(1)}, u32[]{:S(2)}, u32[]{:S(2)}) collective-permute-start(f32[16,256]{1,0:T(8,128)S(1)} %get-tuple-element.46), channel_id=1, source_target_pairs={{0,2},{1,3},{2,0},{3,1},{4,6},{5,7},{6,4},{7,5},{8,10},{9,11},{10,... | collective-permute-start | bytes 49160 | tf_op jit(solution)/shard_map/ppermute | solution.py:457
  55.0 1.0 %copy-done.3 = bf16[64,4096]{1,0:T(8,128)(2,1)S(1)} copy-done((bf16[64,4096]{1,0:T(8,128)(2,1)S(1)}, bf16[64,4096]{1,0:T(8,128)(2,1)}, u32[]{:S(2)}) %copy-start.3) | copy-done | bytes 524312
  56.0 3.1 %score_rows.1.refs_4_ = f32[256,128]{1,0:T(8,128)} custom-call(bf16[64,4096]{1,0:T(8,128)(2,1)S(1)} %copy-done, bf16[64,4096]{1,0:T(8,128)(2,1)S(1)} %copy-done.3, bf16[64,4096]{1,0:T(8,128)(2,1)S(1)} %collective-permute-done.12.refs_7_.refs_2_, bf16[64,4096]{1,0:T(8,128)(2,1)} %collective-permute-done.20.refs_3_, f32[128,4096]{1,0:T(8,128)S(1)} %copy-done.1, ...), custom_call_target="tpu_custom_call" | custom-call | bytes 4194320 | tf_op jit(solution)/shard_map/score_rows/pallas_call | solution.py:150
  59.1 0.9 %copy-done.6 = f32[256,128]{1,0:T(8,128)S(1)} copy-done((f32[256,128]{1,0:T(8,128)S(1)}, f32[256,128]{1,0:T(8,128)}, u32[]{:S(2)}) %copy-start.6) | copy-done | bytes 131096
  60.6 1.7 %collective-permute-start.26 = (f32[8,64]{1,0:T(8,128)S(1)}, f32[8,64]{1,0:T(8,128)S(1)}, u32[]{:S(2)}, u32[]{:S(2)}) collective-permute-start(f32[8,64]{1,0:T(8,128)S(1)} %get-tuple-element.48.refs_0_), channel_id=1, source_target_pairs={{0,24},{1,25},{2,26},{3,27},{4,28},{5,29},{6,30},{7,31},{8,16},{9,... | collective-permute-start | bytes 6152 | tf_op jit(solution)/shard_map/ppermute | solution.py:457
  63.1 1.9 %collective-permute-start.24 = (f32[8,64]{1,0:T(8,128)S(1)}, f32[8,64]{1,0:T(8,128)S(1)}, u32[]{:S(2)}, u32[]{:S(2)}) collective-permute-start(f32[8,64]{1,0:T(8,128)S(1)} %get-tuple-element.48.refs_0_), channel_id=1, source_target_pairs={{0,8},{1,9},{2,10},{3,11},{4,12},{5,13},{6,14},{7,15},{8,0},{9,1},... | collective-permute-start | bytes 6152 | tf_op jit(solution)/shard_map/ppermute | solution.py:457
  65.0 1.0 %collective-permute-done.26.refs_3_ = f32[8,64]{1,0:T(8,128)S(1)} collective-permute-done((f32[8,64]{1,0:T(8,128)S(1)}, f32[8,64]{1,0:T(8,128)S(1)}, u32[]{:S(2)}, u32[]{:S(2)}) %collective-permute-start.26) | collective-permute-done | bytes 2080 | tf_op jit(solution)/shard_map/ppermute | solution.py:457
  66.0 0.8 %collective-permute-done.25.refs_2_ = f32[8,64]{1,0:T(8,128)S(1)} collective-permute-done((f32[8,64]{1,0:T(8,128)S(1)}, f32[8,64]{1,0:T(8,128)S(1)}, u32[]{:S(2)}, u32[]{:S(2)}) %collective-permute-start.25) | collective-permute-done | bytes 2080 | tf_op jit(solution)/shard_map/ppermute | solution.py:457
  (59 shorter events, 8.3 us)
Async XLA Ops:
  0.6 14.3 %copy-start = (bf16[64,4096]{1,0:T(8,128)(2,1)S(1)}, bf16[64,4096]{1,0:T(8,128)(2,1)}, u32[]{:S(2)}) copy-start(bf16[64,4096]{1,0:T(8,128)(2,1)} %refs_0_.1) | copy-start | bytes 1572868
  0.7 14.1 %collective-permute-start.3 = (bf16[64,14336]{1,0:T(8,128)(2,1)}, bf16[64,14336]{1,0:T(8,128)(2,1)S(1)}, u32[]{:S(2)}, u32[]{:S(2)}) collective-permute-start(bf16[64,14336]{1,0:T(8,128)(2,1)} %bitcast.5), channel_id=1, source_target_pairs={{0,1},{1,0},{2,3},{3,2},{4,5},{5,4},{6,7},{7,6},{8,9},{9,8},{10,11... | collective-permute-start | bytes 5505032 | tf_op jit(solution)/shard_map/ppermute | solution.py:457
  1.2 13.6 %collective-permute-start.4 = (bf16[64,4096]{1,0:T(8,128)(2,1)}, bf16[64,4096]{1,0:T(8,128)(2,1)S(1)}, u32[]{:S(2)}, u32[]{:S(2)}) collective-permute-start(bf16[64,4096]{1,0:T(8,128)(2,1)} %bitcast.7), channel_id=1, source_target_pairs={{0,1},{1,0},{2,3},{3,2},{4,5},{5,4},{6,7},{7,6},{8,9},{9,8},{10,11... | collective-permute-start | bytes 1572872 | tf_op jit(solution)/shard_map/ppermute | solution.py:457
  3.2 24.6 %copy-start.4 = (bf16[2,32,14336]{2,1,0:T(8,128)(2,1)S(1)}, bf16[2,32,14336]{2,1,0:T(8,128)(2,1)}, u32[]{:S(2)}) copy-start(bf16[2,32,14336]{2,1,0:T(8,128)(2,1)} %param.9) | copy-start | bytes 5505028
  3.2 24.6 %copy-start.7 = (bf16[2,32,4096]{2,1,0:T(8,128)(2,1)S(1)}, bf16[2,32,4096]{2,1,0:T(8,128)(2,1)}, u32[]{:S(2)}) copy-start(bf16[2,32,4096]{2,1,0:T(8,128)(2,1)} %param.10) | copy-start | bytes 1572868
  3.2 8.0 %collective-permute-start.2 = (bf16[32,1152]{1,0:T(8,128)(2,1)S(1)}, bf16[32,1152]{1,0:T(8,128)(2,1)S(1)}, u32[]{:S(2)}, u32[]{:S(2)}) collective-permute-start(bf16[32,1152]{1,0:T(8,128)(2,1)S(1)} %pack.1.refs_0_), channel_id=1, source_target_pairs={{0,24},{1,25},{2,26},{3,27},{4,28},{5,29},{6,30},{7,31},{8,16},{9,... | collective-permute-start | bytes 221192 | tf_op jit(solution)/shard_map/ppermute | solution.py:457
  8.3 6.5 %collective-permute-start.1 = (bf16[32,1152]{1,0:T(8,128)(2,1)S(1)}, bf16[32,1152]{1,0:T(8,128)(2,1)S(1)}, u32[]{:S(2)}, u32[]{:S(2)}) collective-permute-start(bf16[32,1152]{1,0:T(8,128)(2,1)S(1)} %pack.1.refs_0_), channel_id=1, source_target_pairs={{0,16},{1,17},{2,18},{3,19},{4,20},{5,21},{6,22},{7,23},{8,24},{9,... | collective-permute-start | bytes 221192 | tf_op jit(solution)/shard_map/ppermute | solution.py:457
  8.3 6.5 %collective-permute-start = (bf16[32,1152]{1,0:T(8,128)(2,1)S(1)}, bf16[32,1152]{1,0:T(8,128)(2,1)S(1)}, u32[]{:S(2)}, u32[]{:S(2)}) collective-permute-start(bf16[32,1152]{1,0:T(8,128)(2,1)S(1)} %pack.1.refs_0_), channel_id=1, source_target_pairs={{0,8},{1,9},{2,10},{3,11},{4,12},{5,13},{6,14},{7,15},{8,0},{9,1},... | collective-permute-start | bytes 221192 | tf_op jit(solution)/shard_map/ppermute | solution.py:457
  14.8 10.8 %collective-permute-start.8 = (bf16[128,4096]{1,0:T(8,128)(2,1)S(1)}, bf16[128,4096]{1,0:T(8,128)(2,1)S(1)}, u32[]{:S(2)}, u32[]{:S(2)}) collective-permute-start(bf16[128,4096]{1,0:T(8,128)(2,1)S(1)} %copy-done.5), channel_id=1, source_target_pairs={{0,1},{1,0},{2,3},{3,2},{4,5},{5,4},{6,7},{7,6},{8,9},{9,8},{10,11... | collective-permute-start | bytes 3145736 | tf_op jit(solution)/shard_map/ppermute | solution.py:457
  14.9 10.7 %collective-permute-start.5 = (bf16[64,4096]{1,0:T(8,128)(2,1)S(1)}, bf16[64,4096]{1,0:T(8,128)(2,1)S(1)}, u32[]{:S(2)}, u32[]{:S(2)}) collective-permute-start(bf16[64,4096]{1,0:T(8,128)(2,1)S(1)} %copy-done), channel_id=1, source_target_pairs={{0,1},{1,0},{2,3},{3,2},{4,5},{5,4},{6,7},{7,6},{8,9},{9,8},{10,11... | collective-permute-start | bytes 1572872 | tf_op jit(solution)/shard_map/ppermute | solution.py:457
  15.4 9.0 %collective-permute-start.7 = (bf16[4,32,1152]{2,1,0:T(8,128)(2,1)S(1)}, bf16[4,32,1152]{2,1,0:T(8,128)(2,1)S(1)}, u32[]{:S(2)}, u32[]{:S(2)}) collective-permute-start(bf16[4,32,1152]{2,1,0:T(8,128)(2,1)S(1)} %get-tuple-element.28.refs_4_), channel_id=1, source_target_pairs={{0,4},{1,5},{2,6},{3,7},{4,0},{5,1},{6,2},{7,3},{8,12},{9,13},{10,... | collective-permute-start | bytes 884744 | tf_op jit(solution)/shard_map/ppermute | solution.py:457
  16.9 8.7 %collective-permute-start.6 = (bf16[4,32,1152]{2,1,0:T(8,128)(2,1)S(1)}, bf16[4,32,1152]{2,1,0:T(8,128)(2,1)S(1)}, u32[]{:S(2)}, u32[]{:S(2)}) collective-permute-start(bf16[4,32,1152]{2,1,0:T(8,128)(2,1)S(1)} %get-tuple-element.28.refs_4_), channel_id=1, source_target_pairs={{0,2},{1,3},{2,0},{3,1},{4,6},{5,7},{6,4},{7,5},{8,10},{9,11},{10,... | collective-permute-start | bytes 884744 | tf_op jit(solution)/shard_map/ppermute | solution.py:457
  25.7 5.2 %collective-permute-start.9 = (bf16[2,32,1152]{2,1,0:T(8,128)(2,1)S(1)}, bf16[2,32,1152]{2,1,0:T(8,128)(2,1)S(1)}, u32[]{:S(2)}, u32[]{:S(2)}) collective-permute-start(bf16[2,32,1152]{2,1,0:T(8,128)(2,1)S(1)} %get-tuple-element.33), channel_id=1, source_target_pairs={{0,4},{1,5},{2,6},{3,7},{4,0},{5,1},{6,2},{7,3},{8,12},{9,13},{10,... | collective-permute-start | bytes 442376 | tf_op jit(solution)/shard_map/ppermute | solution.py:457
  26.3 5.1 %collective-permute-start.10 = (bf16[2,32,1152]{2,1,0:T(8,128)(2,1)S(1)}, bf16[2,32,1152]{2,1,0:T(8,128)(2,1)S(1)}, u32[]{:S(2)}, u32[]{:S(2)}) collective-permute-start(bf16[2,32,1152]{2,1,0:T(8,128)(2,1)S(1)} %get-tuple-element.34), channel_id=1, source_target_pairs={{0,2},{1,3},{2,0},{3,1},{4,6},{5,7},{6,4},{7,5},{8,10},{9,11},{10,... | collective-permute-start | bytes 442376 | tf_op jit(solution)/shard_map/ppermute | solution.py:457
  32.0 22.9 %copy-start.11 = (s32[4,1]{0,1:T(1,128)S(1)}, s32[4,1]{0,1:T(1,128)}, u32[]{:S(2)}) copy-start(s32[4,1]{0,1:T(1,128)} %param.17) | copy-start | bytes 52
  32.0 22.9 %copy-start.1 = (f32[128,4096]{1,0:T(8,128)S(1)}, f32[128,4096]{1,0:T(8,128)}, u32[]{:S(2)}) copy-start(f32[128,4096]{1,0:T(8,128)} %refs_4_.3) | copy-start | bytes 6291460
  32.0 1.3 %collective-permute-start.11 = (f32[64,128]{1,0:T(8,128)S(1)}, f32[64,128]{1,0:T(8,128)S(1)}, u32[]{:S(2)}, u32[]{:S(2)}) collective-permute-start(f32[64,128]{1,0:T(8,128)S(1)} %get-tuple-element.36), channel_id=1, source_target_pairs={{0,1},{1,0},{2,3},{3,2},{4,5},{5,4},{6,7},{7,6},{8,9},{9,8},{10,11... | collective-permute-start | bytes 98312 | tf_op jit(solution)/shard_map/ppermute | solution.py:457
  33.6 16.7 %collective-permute-start.12 = (bf16[64,4096]{1,0:T(8,128)(2,1)S(1)}, bf16[64,4096]{1,0:T(8,128)(2,1)S(1)}, u32[]{:S(2)}, u32[]{:S(2)}) collective-permute-start(bf16[64,4096]{1,0:T(8,128)(2,1)S(1)} %copy-done), channel_id=1, source_target_pairs={{0,2},{1,3},{2,0},{3,1},{4,6},{5,7},{6,4},{7,5},{8,10},{9,11},{10,... | collective-permute-start | bytes 1572872 | tf_op jit(solution)/shard_map/ppermute | solution.py:457
  35.1 5.7 %collective-permute-start.15 = (f32[64,128]{1,0:T(8,128)S(1)}, f32[64,128]{1,0:T(8,128)S(1)}, u32[]{:S(2)}, u32[]{:S(2)}) collective-permute-start(f32[64,128]{1,0:T(8,128)S(1)} %get-tuple-element.39.refs_0_), channel_id=1, source_target_pairs={{0,24},{1,25},{2,26},{3,27},{4,28},{5,29},{6,30},{7,31},{8,16},{9,... | collective-permute-start | bytes 98312 | tf_op jit(solution)/shard_map/ppermute | solution.py:457
  37.7 4.8 %collective-permute-start.14 = (f32[64,128]{1,0:T(8,128)S(1)}, f32[64,128]{1,0:T(8,128)S(1)}, u32[]{:S(2)}, u32[]{:S(2)}) collective-permute-start(f32[64,128]{1,0:T(8,128)S(1)} %get-tuple-element.39.refs_0_), channel_id=1, source_target_pairs={{0,16},{1,17},{2,18},{3,19},{4,20},{5,21},{6,22},{7,23},{8,24},{9,... | collective-permute-start | bytes 98312 | tf_op jit(solution)/shard_map/ppermute | solution.py:457
  37.7 4.8 %collective-permute-start.13 = (f32[64,128]{1,0:T(8,128)S(1)}, f32[64,128]{1,0:T(8,128)S(1)}, u32[]{:S(2)}, u32[]{:S(2)}) collective-permute-start(f32[64,128]{1,0:T(8,128)S(1)} %get-tuple-element.39.refs_0_), channel_id=1, source_target_pairs={{0,8},{1,9},{2,10},{3,11},{4,12},{5,13},{6,14},{7,15},{8,0},{9,1},... | collective-permute-start | bytes 98312 | tf_op jit(solution)/shard_map/ppermute | solution.py:457
  42.5 4.0 %collective-permute-start.16 = (f32[64,128]{1,0:T(8,128)S(1)}, f32[64,128]{1,0:T(8,128)S(1)}, u32[]{:S(2)}, u32[]{:S(2)}) collective-permute-start(f32[64,128]{1,0:T(8,128)S(1)} %pair_sum.2), channel_id=1, source_target_pairs={{0,4},{1,5},{2,6},{3,7},{4,0},{5,1},{6,2},{7,3},{8,12},{9,13},{10,... | collective-permute-start | bytes 98312 | tf_op jit(solution)/shard_map/ppermute | solution.py:457
  46.5 3.2 %collective-permute-start.19 = (bf16[64,128]{1,0:T(8,128)(2,1)S(1)}, bf16[64,128]{1,0:T(8,128)(2,1)S(1)}, u32[]{:S(2)}, u32[]{:S(2)}) collective-permute-start(bf16[64,128]{1,0:T(8,128)(2,1)S(1)} %multiply_convert_fusion.refs_0_), channel_id=1, source_target_pairs={{0,3},{1,2},{2,1},{3,0},{4,7},{5,6},{6,5},{7,4},{8,11},{9,10},{10,... | collective-permute-start | bytes 49160 | tf_op jit(solution)/shard_map/ppermute | solution.py:457
  46.6 3.8 %collective-permute-start.18 = (bf16[64,128]{1,0:T(8,128)(2,1)S(1)}, bf16[64,128]{1,0:T(8,128)(2,1)S(1)}, u32[]{:S(2)}, u32[]{:S(2)}) collective-permute-start(bf16[64,128]{1,0:T(8,128)(2,1)S(1)} %multiply_convert_fusion.refs_0_), channel_id=1, source_target_pairs={{0,2},{1,3},{2,0},{3,1},{4,6},{5,7},{6,4},{7,5},{8,10},{9,11},{10,... | collective-permute-start | bytes 49160 | tf_op jit(solution)/shard_map/ppermute | solution.py:457
  47.2 3.2 %collective-permute-start.17 = (bf16[64,128]{1,0:T(8,128)(2,1)S(1)}, bf16[64,128]{1,0:T(8,128)(2,1)S(1)}, u32[]{:S(2)}, u32[]{:S(2)}) collective-permute-start(bf16[64,128]{1,0:T(8,128)(2,1)S(1)} %multiply_convert_fusion.refs_0_), channel_id=1, source_target_pairs={{0,1},{1,0},{2,3},{3,2},{4,5},{5,4},{6,7},{7,6},{8,9},{9,8},{10,11... | collective-permute-start | bytes 49160 | tf_op jit(solution)/shard_map/ppermute | solution.py:457
  51.2 3.7 %collective-permute-start.20 = (bf16[64,4096]{1,0:T(8,128)(2,1)S(1)}, bf16[64,4096]{1,0:T(8,128)(2,1)}, u32[]{:S(2)}, u32[]{:S(2)}) collective-permute-start(bf16[64,4096]{1,0:T(8,128)(2,1)S(1)} %collective-permute-done.12.refs_7_.refs_2_), channel_id=1, source_target_pairs={{0,1},{1,0},{2,3},{3,2},{4,5},{5,4},{6,7},{7,6},{8,9},{9,8},{10,11... | collective-permute-start | bytes 1572872 | tf_op jit(solution)/shard_map/ppermute | solution.py:457
  51.3 7.8 %collective-permute-start.22 = (f32[16,256]{1,0:T(8,128)S(1)}, f32[16,256]{1,0:T(8,128)S(1)}, u32[]{:S(2)}, u32[]{:S(2)}) collective-permute-start(f32[16,256]{1,0:T(8,128)S(1)} %get-tuple-element.45.refs_0_), channel_id=1, source_target_pairs={{0,4},{1,5},{2,6},{3,7},{4,0},{5,1},{6,2},{7,3},{8,12},{9,13},{10,... | collective-permute-start | bytes 49160 | tf_op jit(solution)/shard_map/ppermute | solution.py:457
  52.9 6.2 %collective-permute-start.23 = (f32[16,256]{1,0:T(8,128)S(1)}, f32[16,256]{1,0:T(8,128)S(1)}, u32[]{:S(2)}, u32[]{:S(2)}) collective-permute-start(f32[16,256]{1,0:T(8,128)S(1)} %get-tuple-element.46), channel_id=1, source_target_pairs={{0,6},{1,7},{2,4},{3,5},{4,2},{5,3},{6,0},{7,1},{8,14},{9,15},{10,... | collective-permute-start | bytes 49160 | tf_op jit(solution)/shard_map/ppermute | solution.py:457
  53.7 5.4 %collective-permute-start.21 = (f32[16,256]{1,0:T(8,128)S(1)}, f32[16,256]{1,0:T(8,128)S(1)}, u32[]{:S(2)}, u32[]{:S(2)}) collective-permute-start(f32[16,256]{1,0:T(8,128)S(1)} %get-tuple-element.46), channel_id=1, source_target_pairs={{0,2},{1,3},{2,0},{3,1},{4,6},{5,7},{6,4},{7,5},{8,10},{9,11},{10,... | collective-permute-start | bytes 49160 | tf_op jit(solution)/shard_map/ppermute | solution.py:457
  60.6 5.4 %collective-permute-start.26 = (f32[8,64]{1,0:T(8,128)S(1)}, f32[8,64]{1,0:T(8,128)S(1)}, u32[]{:S(2)}, u32[]{:S(2)}) collective-permute-start(f32[8,64]{1,0:T(8,128)S(1)} %get-tuple-element.48.refs_0_), channel_id=1, source_target_pairs={{0,24},{1,25},{2,26},{3,27},{4,28},{5,29},{6,30},{7,31},{8,16},{9,... | collective-permute-start | bytes 6152 | tf_op jit(solution)/shard_map/ppermute | solution.py:457
  62.3 4.5 %collective-permute-start.25 = (f32[8,64]{1,0:T(8,128)S(1)}, f32[8,64]{1,0:T(8,128)S(1)}, u32[]{:S(2)}, u32[]{:S(2)}) collective-permute-start(f32[8,64]{1,0:T(8,128)S(1)} %get-tuple-element.48.refs_0_), channel_id=1, source_target_pairs={{0,16},{1,17},{2,18},{3,19},{4,20},{5,21},{6,22},{7,23},{8,24},{9,... | collective-permute-start | bytes 6152 | tf_op jit(solution)/shard_map/ppermute | solution.py:457
  63.1 3.8 %collective-permute-start.24 = (f32[8,64]{1,0:T(8,128)S(1)}, f32[8,64]{1,0:T(8,128)S(1)}, u32[]{:S(2)}, u32[]{:S(2)}) collective-permute-start(f32[8,64]{1,0:T(8,128)S(1)} %get-tuple-element.48.refs_0_), channel_id=1, source_target_pairs={{0,8},{1,9},{2,10},{3,11},{4,12},{5,13},{6,14},{7,15},{8,0},{9,1},... | collective-permute-start | bytes 6152 | tf_op jit(solution)/shard_map/ppermute | solution.py:457
  (7 other events, 25.6 us)

commit v4 on v3

--- a/solution.py
+++ b/solution.py
@@ -163,45 +163,21 @@
 
 
 def pack(nx, w_in, w_out):
-    feat = w_in.shape[0]
-    share = feat // nx
-    k_in, k_out = w_in.shape[1] // 2, w_out.shape[1] // 2
-
-    def body(in_ref, out_ref, piece_ref, wide, sems):
-        _, _, x, core = place()
-        rows = pl.ds(pl.multiple_of(x * share, share), share)
-        cols = pl.ds(pl.multiple_of(core * k_in, LANES), k_in)
-        copy_in = pltpu.make_async_copy(in_ref.at[rows, cols], piece_ref.at[:, :k_in], sems.at[0])
-        cols = pl.ds(pl.multiple_of(core * k_out, LANES), k_out)
-        copy_out = pltpu.make_async_copy(out_ref.at[:, cols], wide, sems.at[1])
-        copy_in.start()
-        copy_out.start()
-        row = lax.broadcasted_iota(jnp.int32, (share, feat), 0) + x * share
-        col = lax.broadcasted_iota(jnp.int32, (share, feat), 1)
-        pick = (col == (row % (feat // 2)) * 2 + row // (feat // 2)).astype(F32).astype(BF16)
-        copy_out.wait()
-        piece_ref[:, k_in:] = jnp.dot(pick, wide[...], preferred_element_type=F32).astype(BF16)
-        copy_in.wait()
-
-    return call(
-        "pack",
-        body,
-        shape((share, k_in + k_out), BF16),
-        w_in,
-        w_out,
-        far=(0, 1),
-        scratch=[pltpu.VMEM((feat, k_out), BF16), pltpu.SemaphoreType.DMA((2,))],
-    )
+    _, _, x, core = place()
+    share = w_in.shape[0] // nx
+    parts = []
+    for w in (w_in, w_out):
+        k = w.shape[1] // 2
+        parts.append(lax.dynamic_slice(w, (x * share, core * k), (share, k)))
+    return jnp.concatenate(parts, axis=1)
 
 
 def stack(blocks, after):
     def body(*refs):
-        for n, ref in enumerate(refs[:-2]):
-            refs[-2][n] = ref[...]
-        refs[-1][...] = jnp.zeros_like(refs[-1])
-
-    out = (shape((len(blocks), *blocks[0].shape), BF16), shape(TOKEN, F32))
-    return call("stack", body, out, *blocks, after=after)
+        for n, ref in enumerate(refs[:-1]):
+            refs[-1][n] = ref[...]
+
+    return call("stack", body, shape((len(blocks), *blocks[0].shape), BF16), *blocks, after=after)
 
 
 def halves(by_x, by_y, n_half, after):
@@ -219,7 +195,7 @@
     return res[:-1], res[-1]
 
 
-def project_near(nt, nx, inputs, blocks, k_in, k_out):
+def project_near(nt, nx, inputs, blocks, k_in, k_out, after):
     n_tok = inputs[0].shape[0]
     share = blocks[0].shape[1]
     feat = share * nx
@@ -263,6 +239,7 @@
         *inputs,
         *blocks,
         far=range(4),
+        after=after,
         scratch=[
             pltpu.VMEM((nt, 2 * n_tok, k_in + k_out), BF16),
             pltpu.VMEM((half, feat, k_in + k_out), BF16),
@@ -279,7 +256,8 @@
     half = 2 * n_half
 
     def body(left_ref, right_ref, rest_ref, y_ref, *refs):
-        sides, (mine_ref, other_ref, w_ref) = (refs[:far], refs[far : 2 * far]), refs[2 * far :]
+        sides, (mine_ref, other_ref, token_ref, w_ref) = (refs[:far], refs[far : 2 * far]), refs[2 * far :]
+        token_ref[...] = jnp.zeros_like(token_ref)
         _, _, x, _ = place()
         l, r = left_ref[...], right_ref[...]
         for n in range(half):
@@ -297,7 +275,7 @@
     return call(
         "project_rest",
         body,
-        (out, out),
+        (out, out, shape(TOKEN, F32)),
         left,
         right,
         rest,
@@ -314,19 +292,18 @@
     feat = mine.shape[0]
     half = feat // 2
 
-    def body(mine_ref, got_ref, valid_ref, out_ref, token_ref):
-        token_ref[...] = jnp.zeros_like(token_ref)
-        both = (mine_ref[...] + got_ref[...]).astype(BF16)
+    def body(mine_ref, got_ref, valid_ref, out_ref, both):
+        both[...] = mine_ref[...] + got_ref[...]
+        rights = [both[pl.ds(n, half, stride=2), : docs * toks].astype(BF16) for n in (0, 1)]
+        lefts = both[:, docs * toks :].astype(BF16)
         for d in range(docs):
+            at = slice(d * toks, (d + 1) * toks)
             mask = valid_ref[d : d + 1, :].astype(F32).astype(BF16)
-            right = both[:, d * toks : (d + 1) * toks] * mask
-            left = both[d * toks : (d + 1) * toks, docs * toks :]
-            parts = [
-                jnp.dot(right[n * half : (n + 1) * half], left, preferred_element_type=F32) for n in (0, 1)
-            ]
+            parts = [jnp.dot(r[:, at] * mask, lefts[at], preferred_element_type=F32) for r in rights]
             out_ref[d * half : (d + 1) * half, :] = jnp.concatenate(parts, axis=1)
 
-    return call("outer", body, (shape((docs * half, 2 * feat), F32), shape(TOKEN, F32)), mine, got, validity)
+    out = shape((docs * half, 2 * feat), F32)
+    return call("outer", body, out, mine, got, validity, scratch=[pltpu.VMEM(mine.shape, F32)])
 
 
 def finish(nx, grads, p_own, p_got, queries, docs):
@@ -410,37 +387,47 @@
     return call("pair_sum", body, shape(terms[0].shape, F32), *terms, after=after)
 
 
-def score_rows(queries, store_rows, plan, after):
-    ns = len(queries)
+def score_rows(queries, order, store_rows, plan, scores, after):
+    ns = plan.shape[0]
     n_q, width = queries[0].shape
     n_rows = store_rows.shape[0]
+    count = len(queries)
     step = 4 * LANES
-
-    def body(*refs):
-        q_refs, (rows_ref, plan_ref, out_ref, q_all) = refs[:ns], refs[ns:]
+    have = [] if scores is None else [scores]
+
+    def body(*refs):
+        q_refs, (rows_ref, plan_ref), rest = refs[:count], refs[count : count + 2], refs[count + 2 :]
+        out_ref, token_ref, plan_smem, sem = rest[-4:]
+        token_ref[...] = jnp.zeros_like(token_ref)
         _, s, _, _ = place()
-        for n in range(ns):
-            q_all[pl.ds(pl.multiple_of((s ^ n) * n_q, n_q), n_q), :] = q_refs[n][...]
-        total = jnp.zeros((ns * n_q, n_rows), F32)
+        copy = pltpu.make_async_copy(plan_ref, plan_smem, sem)
+        copy.start()
+        if have:
+            out_ref[...] = rest[0][...]
+        totals = [jnp.zeros((n_q, n_rows), F32) for _ in range(count)]
         for k in range(0, width, step):
             rows = rows_ref[:, k : k + step]
             high = rows.astype(BF16)
             low = (rows - high.astype(F32)).astype(BF16)
-            q = q_all[:, k : k + step]
-            total += dot_nt(q, high) + dot_nt(q, low)
-        for n in range(ns):
-            weight = plan_ref[n : n + 1, :].astype(F32)
-            out_ref[n * n_q : (n + 1) * n_q, :] = total[n * n_q : (n + 1) * n_q] * weight
+            q = jnp.concatenate([ref[:, k : k + step] for ref in q_refs], axis=0)
+            res = dot_nt(q, high) + dot_nt(q, low)
+            totals = [total + res[n * n_q : (n + 1) * n_q] for n, total in enumerate(totals)]
+        copy.wait()
+        for n, total in enumerate(totals):
+            at = s ^ order[n]
+            weight = plan_smem[0, at].astype(F32)
+            out_ref[pl.ds(pl.multiple_of(at * n_q, n_q), n_q), :] = total * weight
 
     return call(
         "score_rows",
         body,
-        shape((ns * n_q, n_rows), F32),
+        (shape((ns * n_q, n_rows), F32), shape(TOKEN, F32)),
         *queries,
         store_rows,
-        plan,
+        plan.T,
+        *have,
         after=after,
-        scratch=[pltpu.VMEM((ns * n_q, width), BF16)],
+        scratch=[pltpu.SMEM((1, ns), jnp.int32), pltpu.SemaphoreType.DMA],
     )
 
 
@@ -462,23 +449,19 @@
 
     inputs = [acts, grads, send(acts, 0, 1), send(grads, 0, 1)]
     mine = pack(nx, proj_in.T, proj_out.T)
-    near, token = stack([mine] + [send(mine, o, 0) for o in z_offs[1:]], inputs[2:])
+    near = stack([mine] + [send(mine, o, 0) for o in z_offs[1:]], inputs[2:])
+    by_x = [send(near, 0, o) for o in x_offs[1:]]
+    by_y = send(near, 1, 0)
+    firsts, lasts = halves(by_x, by_y, len(z_offs) // 2, [])
+    left, right, rest = project_near(nt, nx, inputs, [near] + by_x, k_in, k_out, [lasts])
+    firsts = [send(b, 1, 0) for b in firsts]
+    lasts = [send(lasts, 0, o) for o in x_offs[1:]]
+    own, other, token = project_rest(left, right, rest, by_y, firsts, lasts, k_in, [])
     token, p_late, q_late = lax.optimization_barrier((token, precond, queries))
     tokens = [token]
     p_got = send(p_late, 0, 1)
-    q_near = send(q_late, 0, 1)
-    by_x = [send(near, 0, o) for o in x_offs[1:]]
-    by_y = send(near, 1, 0)
-    firsts, lasts = halves(by_x, by_y, len(z_offs) // 2, [p_got, q_near])
-    firsts = [send(b, 1, 0) for b in firsts]
-    lasts = [send(lasts, 0, o) for o in x_offs[1:]]
-    left, right, rest = project_near(nt, nx, inputs, [near] + by_x, k_in, k_out)
-    own, other = project_rest(left, right, rest, by_y, firsts, lasts, k_in, [])
-    part, token = outer(own, send(other, 0, 1), validity)
-
-    token, q_late = lax.optimization_barrier((token, queries))
-    tokens.append(token)
     q_x = [queries] + [send(q_late, 0, o) for o in x_offs[1:]]
+    part = outer(own, send(other, 0, 1), validity)
 
     total = pair_sum([part] + [send(part, o, 0) for o in z_offs[1:]], [])
     total = total + send(total, 1, 0)
@@ -486,14 +469,16 @@
     g_all = [g_own] + [send(g_own, 0, o) for o in range(1, ns)]
 
     *res, token = finish(nx, g_all, precond, p_got, q_x, docs)
-    token, *q_far = lax.optimization_barrier((token, *q_x[1:]))
+    token, *q_late = lax.optimization_barrier((token, *q_x))
     tokens.append(token)
-    q_core = [q_near] + [send(q, 0, 1) for q in q_far]
+    q_near, *q_far = [send(q, 0, 1) for q in q_late]
     near = [send(r, 0, o) if o else r for r, o in zip(res, x_offs)]
     far = [send(r, 1, o) for r, o in zip(res, x_offs)]
-    scores = score_rows([q for pair in zip(q_x, q_core) for q in pair], store_rows, plan, tokens)
-    precond_docs, partial = assemble(near, far, docs, queries.shape[0], [scores])
-    doc_scores = pair_sum([partial] + [send(partial, o, 0) for o in z_offs[1:]], [])
+    scores, token = score_rows([queries, q_near], [0, 1], store_rows, plan, None, tokens)
+    precond_docs, partial = assemble(near, far, docs, queries.shape[0], [token])
+    order = [o + c for c in (0, 1) for o in x_offs[1:]]
+    scores, token = score_rows(q_x[1:] + q_far, order, store_rows, plan, scores, [])
+    doc_scores = pair_sum([partial] + [send(partial, o, 0) for o in z_offs[1:]], [token])
     return scores, precond_docs, doc_scores.T
 
 

time: 67.7 us -> 64 us (0.945)
  local copies, waits for them, and re-layouts: 3.86 us -> 0.78 us
  Pallas kernels: 7.56 us -> 6.77 us
    unnamed x25 -> x16, local copies, waits for them, and re-layouts: 3.86 us -> 0.05 us
    pallas_call x11, Pallas kernels: 7.56 us -> 6.77 us  [call(): pl.pallas_call(run, name=name, out_shape=out, in_specs=specs + [pl.BlockS...]
    dynamic_slice x0 -> x2, local copies, waits for them, and re-layouts: none -> 0.72 us  [pack(): parts.append(lax.dynamic_slice(w, (x * share, core * k), (share, k)))]
  transfers between devices with their start and end apart: 27 -> 27, of which waited for: 14 -> 15; matrix products, arithmetic and copies ran while one was open for 0% -> 1% of each run, Pallas kernels for 7% -> 7%
where the time goes in v4:
time: 64 us; the launch traced here: 63.8 us
  starting transfers between devices  29.6 us (46%)
  waiting for transfers between devices  25.8 us (40%)
  Pallas kernels  6.77 us (11%)
  between operations  0.85 us (1%)
  local copies, waits for them, and re-layouts  0.78 us (1%)
    ppermute x27, starting transfers between devices, send(): return lax.ppermute(value, AXES, perm)  29.6 us
    ppermute x27, waiting for transfers between devices, send(): return lax.ppermute(value, AXES, perm)  25.8 us
    pallas_call x11, Pallas kernels, call(): pl.pallas_call(run, name=name, out_shape=out, in_specs=specs + [pl.BlockS...  6.77 us
  transfers between devices with their start and end apart: 27, of which 15 were waited for; matrix products, arithmetic and copies ran while one was open for 1% of the time, Pallas kernels for 7%

profile of v4, /device:TPU:0, one launch (start us, length us, event | category | flops | bytes accessed | tf_op | source)
XLA Modules:
  0.0 63.8 jit_solution(1465022646991548009)
XLA Ops:
  1.2 0.7 %dynamic-slice_bitcast_fusion.1 = bf16[32,256]{1,0:T(8,128)(2,1)S(1)} fusion(bf16[512,64]{0,1:T(8,128)(2,1)} %param.13, s32[]{:T(128)S(6)} %select_n.25, s32[]{:T(128)S(6)} %select_n.24), kind=kLoop, calls=%fused_computation.3 | loop fusion | bytes 32776 | tf_op jit(solution)/shard_map/dynamic_slice | solution.py:171
  2.0 5.1 %collective-permute-start.4 = (bf16[32,1152]{1,0:T(8,128)(2,1)S(1)}, bf16[32,1152]{1,0:T(8,128)(2,1)S(1)}, u32[]{:S(2)}, u32[]{:S(2)}) collective-permute-start(bf16[32,1152]{1,0:T(8,128)(2,1)S(1)} %pad_maximum_fusion.refs_0_), channel_id=1, source_target_pairs={{0,24},{1,25},{2,26},{3,27},{4,28},{5,29},{6,30},{7,31},{8,16},{9,... | collective-permute-start | bytes 221192 | tf_op jit(solution)/shard_map/ppermute | solution.py:444
  7.1 0.6 %collective-permute-start.2 = (bf16[32,1152]{1,0:T(8,128)(2,1)S(1)}, bf16[32,1152]{1,0:T(8,128)(2,1)S(1)}, u32[]{:S(2)}, u32[]{:S(2)}) collective-permute-start(bf16[32,1152]{1,0:T(8,128)(2,1)S(1)} %pad_maximum_fusion.refs_0_), channel_id=1, source_target_pairs={{0,8},{1,9},{2,10},{3,11},{4,12},{5,13},{6,14},{7,15},{8,0},{9,1},... | collective-permute-start | bytes 221192 | tf_op jit(solution)/shard_map/ppermute | solution.py:444
  7.8 2.2 %collective-permute-done.4.refs_3_ = bf16[32,1152]{1,0:T(8,128)(2,1)S(1)} collective-permute-done((bf16[32,1152]{1,0:T(8,128)(2,1)S(1)}, bf16[32,1152]{1,0:T(8,128)(2,1)S(1)}, u32[]{:S(2)}, u32[]{:S(2)}) %collective-permute-start.4) | collective-permute-done | bytes 73760 | tf_op jit(solution)/shard_map/ppermute | solution.py:444
  10.0 3.6 %collective-permute-done.3.refs_2_ = bf16[32,1152]{1,0:T(8,128)(2,1)S(1)} collective-permute-done((bf16[32,1152]{1,0:T(8,128)(2,1)S(1)}, bf16[32,1152]{1,0:T(8,128)(2,1)S(1)}, u32[]{:S(2)}, u32[]{:S(2)}) %collective-permute-start.3) | collective-permute-done | bytes 73760 | tf_op jit(solution)/shard_map/ppermute | solution.py:444
  13.6 1.6 %collective-permute-start.6 = (bf16[4,32,1152]{2,1,0:T(8,128)(2,1)S(1)}, bf16[4,32,1152]{2,1,0:T(8,128)(2,1)S(1)}, u32[]{:S(2)}, u32[]{:S(2)}) collective-permute-start(bf16[4,32,1152]{2,1,0:T(8,128)(2,1)S(1)} %stack.1.refs_4_), channel_id=1, source_target_pairs={{0,4},{1,5},{2,6},{3,7},{4,0},{5,1},{6,2},{7,3},{8,12},{9,13},{10,... | collective-permute-start | bytes 884744 | tf_op jit(solution)/shard_map/ppermute | solution.py:444
  15.2 1.5 %collective-permute-start.5 = (bf16[4,32,1152]{2,1,0:T(8,128)(2,1)S(1)}, bf16[4,32,1152]{2,1,0:T(8,128)(2,1)S(1)}, u32[]{:S(2)}, u32[]{:S(2)}) collective-permute-start(bf16[4,32,1152]{2,1,0:T(8,128)(2,1)S(1)} %stack.1.refs_4_), channel_id=1, source_target_pairs={{0,2},{1,3},{2,0},{3,1},{4,6},{5,7},{6,4},{7,5},{8,10},{9,11},{10,... | collective-permute-start | bytes 884744 | tf_op jit(solution)/shard_map/ppermute | solution.py:444
  16.7 5.3 %collective-permute-done.6.refs_1_.refs_3_ = bf16[4,32,1152]{2,1,0:T(8,128)(2,1)S(1)} collective-permute-done((bf16[4,32,1152]{2,1,0:T(8,128)(2,1)S(1)}, bf16[4,32,1152]{2,1,0:T(8,128)(2,1)S(1)}, u32[]{:S(2)}, u32[]{:S(2)}) %collective-permute-start.6) | collective-permute-done | bytes 294944 | tf_op jit(solution)/shard_map/ppermute | solution.py:444
  22.0 1.2 %collective-permute-done.5.refs_0_.refs_5_ = bf16[4,32,1152]{2,1,0:T(8,128)(2,1)S(1)} collective-permute-done((bf16[4,32,1152]{2,1,0:T(8,128)(2,1)S(1)}, bf16[4,32,1152]{2,1,0:T(8,128)(2,1)S(1)}, u32[]{:S(2)}, u32[]{:S(2)}) %collective-permute-start.5) | collective-permute-done | bytes 294944 | tf_op jit(solution)/shard_map/ppermute | solution.py:444
  23.9 1.5 %collective-permute-start.8 = (bf16[2,32,1152]{2,1,0:T(8,128)(2,1)S(1)}, bf16[2,32,1152]{2,1,0:T(8,128)(2,1)S(1)}, u32[]{:S(2)}, u32[]{:S(2)}) collective-permute-start(bf16[2,32,1152]{2,1,0:T(8,128)(2,1)S(1)} %get-tuple-element.26.refs_6_), channel_id=1, source_target_pairs={{0,2},{1,3},{2,0},{3,1},{4,6},{5,7},{6,4},{7,5},{8,10},{9,11},{10,... | collective-permute-start | bytes 442376 | tf_op jit(solution)/shard_map/ppermute | solution.py:444
  25.3 1.3 %project_near.1 = (f32[128,64]{1,0:T(8,128)S(1)}, f32[64,128]{1,0:T(8,128)S(1)}, bf16[4,128,1152]{2,1,0:T(8,128)(2,1)S(1)}) custom-call(bf16[64,14336]{1,0:T(8,128)(2,1)S(1)} %bitcast.9, bf16[64,4096]{1,0:T(8,128)(2,1)S(1)} %bitcast.11, bf16[64,14336]{1,0:T(8,128)(2,1)S(1)} %collective-permute-done.refs_4_.refs_2_, ...), custom_call_target="tpu_custom_call" | custom-call | bytes 5308416 | tf_op jit(solution)/shard_map/project_near/pallas_call | solution.py:150
  26.7 1.8 %collective-permute-done.7.refs_4_ = bf16[2,32,1152]{2,1,0:T(8,128)(2,1)S(1)} collective-permute-done((bf16[2,32,1152]{2,1,0:T(8,128)(2,1)S(1)}, bf16[2,32,1152]{2,1,0:T(8,128)(2,1)S(1)}, u32[]{:S(2)}, u32[]{:S(2)}) %collective-permute-start.7) | collective-permute-done | bytes 147488 | tf_op jit(solution)/shard_map/ppermute | solution.py:444
  29.7 1.6 %collective-permute-start.9 = (bf16[64,4096]{1,0:T(8,128)(2,1)S(1)}, bf16[64,4096]{1,0:T(8,128)(2,1)S(1)}, u32[]{:S(2)}, u32[]{:S(2)}) collective-permute-start(bf16[64,4096]{1,0:T(8,128)(2,1)S(1)} %copy-done.2), channel_id=1, source_target_pairs={{0,2},{1,3},{2,0},{3,1},{4,6},{5,7},{6,4},{7,5},{8,10},{9,11},{10,... | collective-permute-start | bytes 1572872 | tf_op jit(solution)/shard_map/ppermute | solution.py:444
  31.4 1.0 %collective-permute-done.10.refs_1_ = f32[64,128]{1,0:T(8,128)S(1)} collective-permute-done((f32[64,128]{1,0:T(8,128)S(1)}, f32[64,128]{1,0:T(8,128)S(1)}, u32[]{:S(2)}, u32[]{:S(2)}) %collective-permute-start.10) | collective-permute-done | bytes 32800 | tf_op jit(solution)/shard_map/ppermute | solution.py:444
  32.8 2.5 %collective-permute-start.13 = (f32[64,128]{1,0:T(8,128)S(1)}, f32[64,128]{1,0:T(8,128)S(1)}, u32[]{:S(2)}, u32[]{:S(2)}) collective-permute-start(f32[64,128]{1,0:T(8,128)S(1)} %outer.1.refs_0_), channel_id=1, source_target_pairs={{0,24},{1,25},{2,26},{3,27},{4,28},{5,29},{6,30},{7,31},{8,16},{9,... | collective-permute-start | bytes 98312 | tf_op jit(solution)/shard_map/ppermute | solution.py:444
  35.3 1.9 %collective-permute-start.11 = (f32[64,128]{1,0:T(8,128)S(1)}, f32[64,128]{1,0:T(8,128)S(1)}, u32[]{:S(2)}, u32[]{:S(2)}) collective-permute-start(f32[64,128]{1,0:T(8,128)S(1)} %outer.1.refs_0_), channel_id=1, source_target_pairs={{0,8},{1,9},{2,10},{3,11},{4,12},{5,13},{6,14},{7,15},{8,0},{9,1},... | collective-permute-start | bytes 98312 | tf_op jit(solution)/shard_map/ppermute | solution.py:444
  37.2 1.3 %collective-permute-done.13.refs_3_ = f32[64,128]{1,0:T(8,128)S(1)} collective-permute-done((f32[64,128]{1,0:T(8,128)S(1)}, f32[64,128]{1,0:T(8,128)S(1)}, u32[]{:S(2)}, u32[]{:S(2)}) %collective-permute-start.13) | collective-permute-done | bytes 32800 | tf_op jit(solution)/shard_map/ppermute | solution.py:444
  38.5 1.5 %collective-permute-done.12.refs_2_ = f32[64,128]{1,0:T(8,128)S(1)} collective-permute-done((f32[64,128]{1,0:T(8,128)S(1)}, f32[64,128]{1,0:T(8,128)S(1)}, u32[]{:S(2)}, u32[]{:S(2)}) %collective-permute-start.12) | collective-permute-done | bytes 32800 | tf_op jit(solution)/shard_map/ppermute | solution.py:444
  40.1 1.6 %collective-permute-start.14 = (f32[64,128]{1,0:T(8,128)S(1)}, f32[64,128]{1,0:T(8,128)S(1)}, u32[]{:S(2)}, u32[]{:S(2)}) collective-permute-start(f32[64,128]{1,0:T(8,128)S(1)} %pair_sum.2), channel_id=1, source_target_pairs={{0,4},{1,5},{2,6},{3,7},{4,0},{5,1},{6,2},{7,3},{8,12},{9,13},{10,... | collective-permute-start | bytes 98312 | tf_op jit(solution)/shard_map/ppermute | solution.py:444
  41.7 2.4 %collective-permute-done.14 = f32[64,128]{1,0:T(8,128)S(1)} collective-permute-done((f32[64,128]{1,0:T(8,128)S(1)}, f32[64,128]{1,0:T(8,128)S(1)}, u32[]{:S(2)}, u32[]{:S(2)}) %collective-permute-start.14) | collective-permute-done | bytes 32800 | tf_op jit(solution)/shard_map/ppermute | solution.py:444
  44.2 1.5 %collective-permute-start.16 = (bf16[64,128]{1,0:T(8,128)(2,1)S(1)}, bf16[64,128]{1,0:T(8,128)(2,1)S(1)}, u32[]{:S(2)}, u32[]{:S(2)}) collective-permute-start(bf16[64,128]{1,0:T(8,128)(2,1)S(1)} %multiply_convert_fusion.refs_0_), channel_id=1, source_target_pairs={{0,2},{1,3},{2,0},{3,1},{4,6},{5,7},{6,4},{7,5},{8,10},{9,11},{10,... | collective-permute-start | bytes 49160 | tf_op jit(solution)/shard_map/ppermute | solution.py:444
  46.0 1.4 %collective-permute-done.17.refs_3_ = bf16[64,128]{1,0:T(8,128)(2,1)S(1)} collective-permute-done((bf16[64,128]{1,0:T(8,128)(2,1)S(1)}, bf16[64,128]{1,0:T(8,128)(2,1)S(1)}, u32[]{:S(2)}, u32[]{:S(2)}) %collective-permute-start.17) | collective-permute-done | bytes 16416 | tf_op jit(solution)/shard_map/ppermute | solution.py:444
  48.0 0.9 %finish.1 = (f32[16,256]{1,0:T(8,128)S(1)}, f32[16,256]{1,0:T(8,128)S(1)}, f32[8,128]{1,0:T(8,128)S(1)}) custom-call(bf16[64,128]{1,0:T(8,128)(2,1)S(1)} %multiply_convert_fusion.refs_0_, bf16[64,128]{1,0:T(8,128)(2,1)S(1)} %collective-permute-done.15.refs_1_, bf16[64,128]{1,0:T(8,128)(2,1)S(1)} %collective-permute-done.16.refs_2_, ...), custom_call_target="tpu_custom_call" | custom-call | bytes 3211264 | tf_op jit(solution)/shard_map/finish/pallas_call | solution.py:150
  49.4 1.5 %collective-permute-start.22 = (f32[16,256]{1,0:T(8,128)S(1)}, f32[16,256]{1,0:T(8,128)S(1)}, u32[]{:S(2)}, u32[]{:S(2)}) collective-permute-start(f32[16,256]{1,0:T(8,128)S(1)} %get-tuple-element.43.refs_0_), channel_id=1, source_target_pairs={{0,4},{1,5},{2,6},{3,7},{4,0},{5,1},{6,2},{7,3},{8,12},{9,13},{10,... | collective-permute-start | bytes 49160 | tf_op jit(solution)/shard_map/ppermute | solution.py:444
  51.0 1.3 %collective-permute-start.23 = (f32[16,256]{1,0:T(8,128)S(1)}, f32[16,256]{1,0:T(8,128)S(1)}, u32[]{:S(2)}, u32[]{:S(2)}) collective-permute-start(f32[16,256]{1,0:T(8,128)S(1)} %get-tuple-element.44), channel_id=1, source_target_pairs={{0,6},{1,7},{2,4},{3,5},{4,2},{5,3},{6,0},{7,1},{8,14},{9,15},{10,... | collective-permute-start | bytes 49160 | tf_op jit(solution)/shard_map/ppermute | solution.py:444
  52.3 0.6 collective-permute-start.21
  52.9 0.7 %score_rows.2 = (f32[256,128]{1,0:T(8,128)S(1)}, f32[8,128]{1,0:T(8,128)S(1)}) custom-call(bf16[64,4096]{1,0:T(8,128)(2,1)S(1)} %copy-done.2, bf16[64,4096]{1,0:T(8,128)(2,1)S(1)} %collective-permute-done.20.refs_1_, f32[128,4096]{1,0:T(8,128)S(1)} %copy-done.1, s32[1,4]{1,0:T(1,128)S(1)} %bitcast.12, f32[8,128]{1,0:T(8,128)S(1)} %get-tuple-element.39.refs_4_, ...), custom_call_target="tpu_custom_call" | custom-call | bytes 3145744 | tf_op jit(solution)/shard_map/score_rows/pallas_call | solution.py:150
  53.7 2.0 %collective-permute-done.23.refs_3_ = f32[16,256]{1,0:T(8,128)S(1)} collective-permute-done((f32[16,256]{1,0:T(8,128)S(1)}, f32[16,256]{1,0:T(8,128)S(1)}, u32[]{:S(2)}, u32[]{:S(2)}) %collective-permute-start.23) | collective-permute-done | bytes 16416 | tf_op jit(solution)/shard_map/ppermute | solution.py:444
  56.0 0.6 assemble.1
  56.6 2.0 %collective-permute-start.26 = (f32[8,64]{1,0:T(8,128)S(1)}, f32[8,64]{1,0:T(8,128)S(1)}, u32[]{:S(2)}, u32[]{:S(2)}) collective-permute-start(f32[8,64]{1,0:T(8,128)S(1)} %get-tuple-element.47.refs_0_), channel_id=1, source_target_pairs={{0,24},{1,25},{2,26},{3,27},{4,28},{5,29},{6,30},{7,31},{8,16},{9,... | collective-permute-start | bytes 6152 | tf_op jit(solution)/shard_map/ppermute | solution.py:444
  59.2 1.9 %collective-permute-start.24 = (f32[8,64]{1,0:T(8,128)S(1)}, f32[8,64]{1,0:T(8,128)S(1)}, u32[]{:S(2)}, u32[]{:S(2)}) collective-permute-start(f32[8,64]{1,0:T(8,128)S(1)} %get-tuple-element.47.refs_0_), channel_id=1, source_target_pairs={{0,8},{1,9},{2,10},{3,11},{4,12},{5,13},{6,14},{7,15},{8,0},{9,1},... | collective-permute-start | bytes 6152 | tf_op jit(solution)/shard_map/ppermute | solution.py:444
  61.0 1.7 %score_rows.3 = (f32[256,128]{1,0:T(8,128)}, f32[8,128]{1,0:T(8,128)S(1)}) custom-call(bf16[64,4096]{1,0:T(8,128)(2,1)S(1)} %collective-permute-done.9.refs_7_.refs_0_, bf16[64,4096]{1,0:T(8,128)(2,1)S(1)} %collective-permute-done.19.refs_1_, f32[128,4096]{1,0:T(8,128)S(1)} %copy-done.1, s32[1,4]{1,0:T(1,128)S(1)} %bitcast.13, ...), custom_call_target="tpu_custom_call" | custom-call | bytes 3276816 | tf_op jit(solution)/shard_map/score_rows/pallas_call | solution.py:150
  (53 shorter events, 6.3 us)
Async XLA Ops:
  0.6 12.9 %collective-permute-start = (bf16[64,14336]{1,0:T(8,128)(2,1)}, bf16[64,14336]{1,0:T(8,128)(2,1)S(1)}, u32[]{:S(2)}, u32[]{:S(2)}) collective-permute-start(bf16[64,14336]{1,0:T(8,128)(2,1)} %bitcast.8), channel_id=1, source_target_pairs={{0,1},{1,0},{2,3},{3,2},{4,5},{5,4},{6,7},{7,6},{8,9},{9,8},{10,11... | collective-permute-start | bytes 5505032 | tf_op jit(solution)/shard_map/ppermute | solution.py:444
  1.2 12.4 %collective-permute-start.1 = (bf16[64,4096]{1,0:T(8,128)(2,1)}, bf16[64,4096]{1,0:T(8,128)(2,1)S(1)}, u32[]{:S(2)}, u32[]{:S(2)}) collective-permute-start(bf16[64,4096]{1,0:T(8,128)(2,1)} %bitcast.10), channel_id=1, source_target_pairs={{0,1},{1,0},{2,3},{3,2},{4,5},{5,4},{6,7},{7,6},{8,9},{9,8},{10,11... | collective-permute-start | bytes 1572872 | tf_op jit(solution)/shard_map/ppermute | solution.py:444
  2.0 23.4 %copy-start.3 = (bf16[2,32,14336]{2,1,0:T(8,128)(2,1)S(1)}, bf16[2,32,14336]{2,1,0:T(8,128)(2,1)}, u32[]{:S(2)}) copy-start(bf16[2,32,14336]{2,1,0:T(8,128)(2,1)} %param.9) | copy-start | bytes 5505028
  2.0 23.4 %copy-start.5 = (bf16[2,32,4096]{2,1,0:T(8,128)(2,1)S(1)}, bf16[2,32,4096]{2,1,0:T(8,128)(2,1)}, u32[]{:S(2)}) copy-start(bf16[2,32,4096]{2,1,0:T(8,128)(2,1)} %param.10) | copy-start | bytes 1572868
  2.0 8.0 %collective-permute-start.4 = (bf16[32,1152]{1,0:T(8,128)(2,1)S(1)}, bf16[32,1152]{1,0:T(8,128)(2,1)S(1)}, u32[]{:S(2)}, u32[]{:S(2)}) collective-permute-start(bf16[32,1152]{1,0:T(8,128)(2,1)S(1)} %pad_maximum_fusion.refs_0_), channel_id=1, source_target_pairs={{0,24},{1,25},{2,26},{3,27},{4,28},{5,29},{6,30},{7,31},{8,16},{9,... | collective-permute-start | bytes 221192 | tf_op jit(solution)/shard_map/ppermute | solution.py:444
  7.1 6.5 %collective-permute-start.3 = (bf16[32,1152]{1,0:T(8,128)(2,1)S(1)}, bf16[32,1152]{1,0:T(8,128)(2,1)S(1)}, u32[]{:S(2)}, u32[]{:S(2)}) collective-permute-start(bf16[32,1152]{1,0:T(8,128)(2,1)S(1)} %pad_maximum_fusion.refs_0_), channel_id=1, source_target_pairs={{0,16},{1,17},{2,18},{3,19},{4,20},{5,21},{6,22},{7,23},{8,24},{9,... | collective-permute-start | bytes 221192 | tf_op jit(solution)/shard_map/ppermute | solution.py:444
  7.1 6.5 %collective-permute-start.2 = (bf16[32,1152]{1,0:T(8,128)(2,1)S(1)}, bf16[32,1152]{1,0:T(8,128)(2,1)S(1)}, u32[]{:S(2)}, u32[]{:S(2)}) collective-permute-start(bf16[32,1152]{1,0:T(8,128)(2,1)S(1)} %pad_maximum_fusion.refs_0_), channel_id=1, source_target_pairs={{0,8},{1,9},{2,10},{3,11},{4,12},{5,13},{6,14},{7,15},{8,0},{9,1},... | collective-permute-start | bytes 221192 | tf_op jit(solution)/shard_map/ppermute | solution.py:444
  13.6 8.4 %collective-permute-start.6 = (bf16[4,32,1152]{2,1,0:T(8,128)(2,1)S(1)}, bf16[4,32,1152]{2,1,0:T(8,128)(2,1)S(1)}, u32[]{:S(2)}, u32[]{:S(2)}) collective-permute-start(bf16[4,32,1152]{2,1,0:T(8,128)(2,1)S(1)} %stack.1.refs_4_), channel_id=1, source_target_pairs={{0,4},{1,5},{2,6},{3,7},{4,0},{5,1},{6,2},{7,3},{8,12},{9,13},{10,... | collective-permute-start | bytes 884744 | tf_op jit(solution)/shard_map/ppermute | solution.py:444
  15.2 8.1 %collective-permute-start.5 = (bf16[4,32,1152]{2,1,0:T(8,128)(2,1)S(1)}, bf16[4,32,1152]{2,1,0:T(8,128)(2,1)S(1)}, u32[]{:S(2)}, u32[]{:S(2)}) collective-permute-start(bf16[4,32,1152]{2,1,0:T(8,128)(2,1)S(1)} %stack.1.refs_4_), channel_id=1, source_target_pairs={{0,2},{1,3},{2,0},{3,1},{4,6},{5,7},{6,4},{7,5},{8,10},{9,11},{10,... | collective-permute-start | bytes 884744 | tf_op jit(solution)/shard_map/ppermute | solution.py:444
  23.3 5.2 %collective-permute-start.7 = (bf16[2,32,1152]{2,1,0:T(8,128)(2,1)S(1)}, bf16[2,32,1152]{2,1,0:T(8,128)(2,1)S(1)}, u32[]{:S(2)}, u32[]{:S(2)}) collective-permute-start(bf16[2,32,1152]{2,1,0:T(8,128)(2,1)S(1)} %get-tuple-element.30), channel_id=1, source_target_pairs={{0,4},{1,5},{2,6},{3,7},{4,0},{5,1},{6,2},{7,3},{8,12},{9,13},{10,... | collective-permute-start | bytes 442376 | tf_op jit(solution)/shard_map/ppermute | solution.py:444
  23.9 5.1 %collective-permute-start.8 = (bf16[2,32,1152]{2,1,0:T(8,128)(2,1)S(1)}, bf16[2,32,1152]{2,1,0:T(8,128)(2,1)S(1)}, u32[]{:S(2)}, u32[]{:S(2)}) collective-permute-start(bf16[2,32,1152]{2,1,0:T(8,128)(2,1)S(1)} %get-tuple-element.26.refs_6_), channel_id=1, source_target_pairs={{0,2},{1,3},{2,0},{3,1},{4,6},{5,7},{6,4},{7,5},{8,10},{9,11},{10,... | collective-permute-start | bytes 442376 | tf_op jit(solution)/shard_map/ppermute | solution.py:444
  26.7 5.8 %copy-start.7 = (s32[2,32]{1,0:T(2,128)S(1)}, s32[2,32]{1,0:T(2,128)}, u32[]{:S(2)}) copy-start(s32[2,32]{1,0:T(2,128)} %refs_2_.3) | copy-start | bytes 772
  29.6 23.4 %copy-start.1 = (f32[128,4096]{1,0:T(8,128)S(1)}, f32[128,4096]{1,0:T(8,128)}, u32[]{:S(2)}) copy-start(f32[128,4096]{1,0:T(8,128)} %refs_2_.5) | copy-start | bytes 6291460
  29.6 23.3 %copy-start.6 = (s32[4,1]{0,1:T(1,128)S(1)}, s32[4,1]{0,1:T(1,128)}, u32[]{:S(2)}) copy-start(s32[4,1]{0,1:T(1,128)} %param.17) | copy-start | bytes 52
  29.6 18.4 %collective-permute-start.18 = (bf16[128,4096]{1,0:T(8,128)(2,1)S(1)}, bf16[128,4096]{1,0:T(8,128)(2,1)S(1)}, u32[]{:S(2)}, u32[]{:S(2)}) collective-permute-start(bf16[128,4096]{1,0:T(8,128)(2,1)S(1)} %copy-done.4), channel_id=1, source_target_pairs={{0,1},{1,0},{2,3},{3,2},{4,5},{5,4},{6,7},{7,6},{8,9},{9,8},{10,11... | collective-permute-start | bytes 3145736 | tf_op jit(solution)/shard_map/ppermute | solution.py:444
  29.7 18.3 %collective-permute-start.9 = (bf16[64,4096]{1,0:T(8,128)(2,1)S(1)}, bf16[64,4096]{1,0:T(8,128)(2,1)S(1)}, u32[]{:S(2)}, u32[]{:S(2)}) collective-permute-start(bf16[64,4096]{1,0:T(8,128)(2,1)S(1)} %copy-done.2), channel_id=1, source_target_pairs={{0,2},{1,3},{2,0},{3,1},{4,6},{5,7},{6,4},{7,5},{8,10},{9,11},{10,... | collective-permute-start | bytes 1572872 | tf_op jit(solution)/shard_map/ppermute | solution.py:444
  31.3 1.2 %collective-permute-start.10 = (f32[64,128]{1,0:T(8,128)S(1)}, f32[64,128]{1,0:T(8,128)S(1)}, u32[]{:S(2)}, u32[]{:S(2)}) collective-permute-start(f32[64,128]{1,0:T(8,128)S(1)} %get-tuple-element.34), channel_id=1, source_target_pairs={{0,1},{1,0},{2,3},{3,2},{4,5},{5,4},{6,7},{7,6},{8,9},{9,8},{10,11... | collective-permute-start | bytes 98312 | tf_op jit(solution)/shard_map/ppermute | solution.py:444
  32.8 5.7 %collective-permute-start.13 = (f32[64,128]{1,0:T(8,128)S(1)}, f32[64,128]{1,0:T(8,128)S(1)}, u32[]{:S(2)}, u32[]{:S(2)}) collective-permute-start(f32[64,128]{1,0:T(8,128)S(1)} %outer.1.refs_0_), channel_id=1, source_target_pairs={{0,24},{1,25},{2,26},{3,27},{4,28},{5,29},{6,30},{7,31},{8,16},{9,... | collective-permute-start | bytes 98312 | tf_op jit(solution)/shard_map/ppermute | solution.py:444
  35.3 4.8 %collective-permute-start.12 = (f32[64,128]{1,0:T(8,128)S(1)}, f32[64,128]{1,0:T(8,128)S(1)}, u32[]{:S(2)}, u32[]{:S(2)}) collective-permute-start(f32[64,128]{1,0:T(8,128)S(1)} %outer.1.refs_0_), channel_id=1, source_target_pairs={{0,16},{1,17},{2,18},{3,19},{4,20},{5,21},{6,22},{7,23},{8,24},{9,... | collective-permute-start | bytes 98312 | tf_op jit(solution)/shard_map/ppermute | solution.py:444
  35.3 4.8 %collective-permute-start.11 = (f32[64,128]{1,0:T(8,128)S(1)}, f32[64,128]{1,0:T(8,128)S(1)}, u32[]{:S(2)}, u32[]{:S(2)}) collective-permute-start(f32[64,128]{1,0:T(8,128)S(1)} %outer.1.refs_0_), channel_id=1, source_target_pairs={{0,8},{1,9},{2,10},{3,11},{4,12},{5,13},{6,14},{7,15},{8,0},{9,1},... | collective-permute-start | bytes 98312 | tf_op jit(solution)/shard_map/ppermute | solution.py:444
  40.1 4.0 %collective-permute-start.14 = (f32[64,128]{1,0:T(8,128)S(1)}, f32[64,128]{1,0:T(8,128)S(1)}, u32[]{:S(2)}, u32[]{:S(2)}) collective-permute-start(f32[64,128]{1,0:T(8,128)S(1)} %pair_sum.2), channel_id=1, source_target_pairs={{0,4},{1,5},{2,6},{3,7},{4,0},{5,1},{6,2},{7,3},{8,12},{9,13},{10,... | collective-permute-start | bytes 98312 | tf_op jit(solution)/shard_map/ppermute | solution.py:444
  44.1 3.4 %collective-permute-start.17 = (bf16[64,128]{1,0:T(8,128)(2,1)S(1)}, bf16[64,128]{1,0:T(8,128)(2,1)S(1)}, u32[]{:S(2)}, u32[]{:S(2)}) collective-permute-start(bf16[64,128]{1,0:T(8,128)(2,1)S(1)} %multiply_convert_fusion.refs_0_), channel_id=1, source_target_pairs={{0,3},{1,2},{2,1},{3,0},{4,7},{5,6},{6,5},{7,4},{8,11},{9,10},{10,... | collective-permute-start | bytes 49160 | tf_op jit(solution)/shard_map/ppermute | solution.py:444
  44.2 3.8 %collective-permute-start.16 = (bf16[64,128]{1,0:T(8,128)(2,1)S(1)}, bf16[64,128]{1,0:T(8,128)(2,1)S(1)}, u32[]{:S(2)}, u32[]{:S(2)}) collective-permute-start(bf16[64,128]{1,0:T(8,128)(2,1)S(1)} %multiply_convert_fusion.refs_0_), channel_id=1, source_target_pairs={{0,2},{1,3},{2,0},{3,1},{4,6},{5,7},{6,4},{7,5},{8,10},{9,11},{10,... | collective-permute-start | bytes 49160 | tf_op jit(solution)/shard_map/ppermute | solution.py:444
  45.6 2.3 %collective-permute-start.15 = (bf16[64,128]{1,0:T(8,128)(2,1)S(1)}, bf16[64,128]{1,0:T(8,128)(2,1)S(1)}, u32[]{:S(2)}, u32[]{:S(2)}) collective-permute-start(bf16[64,128]{1,0:T(8,128)(2,1)S(1)} %multiply_convert_fusion.refs_0_), channel_id=1, source_target_pairs={{0,1},{1,0},{2,3},{3,2},{4,5},{5,4},{6,7},{7,6},{8,9},{9,8},{10,11... | collective-permute-start | bytes 49160 | tf_op jit(solution)/shard_map/ppermute | solution.py:444
  48.9 4.1 %collective-permute-start.20 = (bf16[64,4096]{1,0:T(8,128)(2,1)S(1)}, bf16[64,4096]{1,0:T(8,128)(2,1)S(1)}, u32[]{:S(2)}, u32[]{:S(2)}) collective-permute-start(bf16[64,4096]{1,0:T(8,128)(2,1)S(1)} %copy-done.2), channel_id=1, source_target_pairs={{0,1},{1,0},{2,3},{3,2},{4,5},{5,4},{6,7},{7,6},{8,9},{9,8},{10,11... | collective-permute-start | bytes 1572872 | tf_op jit(solution)/shard_map/ppermute | solution.py:444
  49.2 11.8 %collective-permute-start.19 = (bf16[64,4096]{1,0:T(8,128)(2,1)S(1)}, bf16[64,4096]{1,0:T(8,128)(2,1)S(1)}, u32[]{:S(2)}, u32[]{:S(2)}) collective-permute-start(bf16[64,4096]{1,0:T(8,128)(2,1)S(1)} %collective-permute-done.9.refs_7_.refs_0_), channel_id=1, source_target_pairs={{0,1},{1,0},{2,3},{3,2},{4,5},{5,4},{6,7},{7,6},{8,9},{9,8},{10,11... | collective-permute-start | bytes 1572872 | tf_op jit(solution)/shard_map/ppermute | solution.py:444
  49.4 4.3 %collective-permute-start.22 = (f32[16,256]{1,0:T(8,128)S(1)}, f32[16,256]{1,0:T(8,128)S(1)}, u32[]{:S(2)}, u32[]{:S(2)}) collective-permute-start(f32[16,256]{1,0:T(8,128)S(1)} %get-tuple-element.43.refs_0_), channel_id=1, source_target_pairs={{0,4},{1,5},{2,6},{3,7},{4,0},{5,1},{6,2},{7,3},{8,12},{9,13},{10,... | collective-permute-start | bytes 49160 | tf_op jit(solution)/shard_map/ppermute | solution.py:444
  51.0 4.8 %collective-permute-start.23 = (f32[16,256]{1,0:T(8,128)S(1)}, f32[16,256]{1,0:T(8,128)S(1)}, u32[]{:S(2)}, u32[]{:S(2)}) collective-permute-start(f32[16,256]{1,0:T(8,128)S(1)} %get-tuple-element.44), channel_id=1, source_target_pairs={{0,6},{1,7},{2,4},{3,5},{4,2},{5,3},{6,0},{7,1},{8,14},{9,15},{10,... | collective-permute-start | bytes 49160 | tf_op jit(solution)/shard_map/ppermute | solution.py:444
  52.3 3.7 %collective-permute-start.21 = (f32[16,256]{1,0:T(8,128)S(1)}, f32[16,256]{1,0:T(8,128)S(1)}, u32[]{:S(2)}, u32[]{:S(2)}) collective-permute-start(f32[16,256]{1,0:T(8,128)S(1)} %get-tuple-element.44), channel_id=1, source_target_pairs={{0,2},{1,3},{2,0},{3,1},{4,6},{5,7},{6,4},{7,5},{8,10},{9,11},{10,... | collective-permute-start | bytes 49160 | tf_op jit(solution)/shard_map/ppermute | solution.py:444
  56.6 6.1 %collective-permute-start.26 = (f32[8,64]{1,0:T(8,128)S(1)}, f32[8,64]{1,0:T(8,128)S(1)}, u32[]{:S(2)}, u32[]{:S(2)}) collective-permute-start(f32[8,64]{1,0:T(8,128)S(1)} %get-tuple-element.47.refs_0_), channel_id=1, source_target_pairs={{0,24},{1,25},{2,26},{3,27},{4,28},{5,29},{6,30},{7,31},{8,16},{9,... | collective-permute-start | bytes 6152 | tf_op jit(solution)/shard_map/ppermute | solution.py:444
  58.7 4.5 %collective-permute-start.25 = (f32[8,64]{1,0:T(8,128)S(1)}, f32[8,64]{1,0:T(8,128)S(1)}, u32[]{:S(2)}, u32[]{:S(2)}) collective-permute-start(f32[8,64]{1,0:T(8,128)S(1)} %get-tuple-element.47.refs_0_), channel_id=1, source_target_pairs={{0,16},{1,17},{2,18},{3,19},{4,20},{5,21},{6,22},{7,23},{8,24},{9,... | collective-permute-start | bytes 6152 | tf_op jit(solution)/shard_map/ppermute | solution.py:444
  59.2 4.1 %collective-permute-start.24 = (f32[8,64]{1,0:T(8,128)S(1)}, f32[8,64]{1,0:T(8,128)S(1)}, u32[]{:S(2)}, u32[]{:S(2)}) collective-permute-start(f32[8,64]{1,0:T(8,128)S(1)} %get-tuple-element.47.refs_0_), channel_id=1, source_target_pairs={{0,8},{1,9},{2,10},{3,11},{4,12},{5,13},{6,14},{7,15},{8,0},{9,1},... | collective-permute-start | bytes 6152 | tf_op jit(solution)/shard_map/ppermute | solution.py:444
  (3 other events, 7.3 us)

commit v5 on v4

--- a/solution.py
+++ b/solution.py
@@ -178,21 +178,6 @@
             refs[-1][n] = ref[...]
 
     return call("stack", body, shape((len(blocks), *blocks[0].shape), BF16), *blocks, after=after)
-
-
-def halves(by_x, by_y, n_half, after):
-    nx = len(by_x) + 1
-
-    def body(*refs):
-        ins, outs = refs[:nx], refs[nx:]
-        for n in range(nx - 1):
-            outs[n][...] = ins[n][:n_half]
-        outs[-1][...] = ins[-1][n_half:]
-
-    dims = by_y.shape[1:]
-    out = [shape((n_half, *dims), BF16)] * (nx - 1) + [shape((by_y.shape[0] - n_half, *dims), BF16)]
-    res = call("halves", body, tuple(out), *by_x, by_y, after=after)
-    return res[:-1], res[-1]
 
 
 def project_near(nt, nx, inputs, blocks, k_in, k_out, after):
@@ -248,23 +233,22 @@
     )
 
 
-def project_rest(left, right, rest, by_y, firsts, lasts, k_in, after):
+def project_rest(left, right, rest, by_y, far, k_in):
     feat = left.shape[1]
     n_tok = left.shape[0] // 2
-    n_half, share, k_both = firsts[0].shape
-    far = len(firsts)
-    half = 2 * n_half
+    half, share, k_both = by_y.shape
+    flat = [b for blocks in far for b in blocks]
 
     def body(left_ref, right_ref, rest_ref, y_ref, *refs):
-        sides, (mine_ref, other_ref, token_ref, w_ref) = (refs[:far], refs[far : 2 * far]), refs[2 * far :]
+        far_refs, (mine_ref, other_ref, token_ref, w_ref) = refs[: len(flat)], refs[len(flat) :]
         token_ref[...] = jnp.zeros_like(token_ref)
         _, _, x, _ = place()
         l, r = left_ref[...], right_ref[...]
         for n in range(half):
             w_ref[n, pl.ds(pl.multiple_of(x * share, share), share), :] = y_ref[n]
-            for dx in range(1, far + 1):
+            for dx in range(1, len(far) + 1):
                 at = pl.ds(pl.multiple_of((x ^ dx) * share, share), share)
-                w_ref[n, at, :] = sides[n // n_half][dx - 1][n % n_half]
+                w_ref[n, at, :] = far_refs[(dx - 1) * half + n][...]
         for n in range(half):
             l += dot_nt(rest_ref[n, :, :k_in], w_ref[n, :, :k_in])
             r += dot_nt(w_ref[n, :, k_in:], rest_ref[n, :, k_in:])
@@ -280,9 +264,7 @@
         right,
         rest,
         by_y,
-        *firsts,
-        *lasts,
-        after=after,
+        *flat,
         scratch=[pltpu.VMEM((half, feat, k_both), BF16)],
     )
 
@@ -306,17 +288,19 @@
     return call("outer", body, out, mine, got, validity, scratch=[pltpu.VMEM(mine.shape, F32)])
 
 
-def finish(nx, grads, p_own, p_got, queries, docs):
+def finish(nt, nx, grads, p_own, p_got, queries, docs, after):
     ns = len(grads)
     high = grads[0].shape[0]
     pairs = high // docs
     cols = p_own.shape[0]
     n_q = queries[0].shape[0]
+    n_rows = ns * docs
+    folds = n_rows // docs
+    k_fold = 2 * cols // folds
 
     def body(*refs):
-        g_refs, p_refs, q_refs, outs = refs[:ns], refs[ns : ns + 2], refs[ns + 2 : ns + 2 + nx], refs[ns + 2 + nx : -5]
-        token_ref, wide, pre, q_part, sems = refs[-5:]
-        token_ref[...] = jnp.zeros_like(token_ref)
+        g_refs, p_refs, q_refs = refs[:ns], refs[ns : ns + 2], refs[ns + 2 : ns + 2 + nx]
+        out_ref, wide, pre, q_part, sems = refs[-5:]
         t, s, x, core = place()
         at = pl.multiple_of((t * nx + x) * 2 * cols, LANES)
         copies = [
@@ -327,7 +311,7 @@
         for n in range(ns):
             at = pl.multiple_of((s ^ n) * high, high)
             wide[pl.ds(at, high), :] = g_refs[n][...].astype(F32)
-        rows = [wide[pl.ds(j, ns * docs, stride=pairs), :] for j in range(pairs)]
+        rows = [wide[pl.ds(j, n_rows, stride=pairs), :] for j in range(pairs)]
         rows = jnp.concatenate(rows, axis=1).astype(BF16)
         for ref, c in zip(p_refs, (core, 1 - core)):
             pre[:, pl.ds(pl.multiple_of(c * cols, LANES), cols)] = dot_nt(rows, ref[...])
@@ -340,51 +324,63 @@
             mine = full[:docs]
             for m in range(1, ns):
                 mine = jnp.where((s ^ (2 * n)) == m, full[m * docs : (m + 1) * docs], mine)
-            outs[n][:docs, :] = mine
-            outs[n][8:, :n_q] = dot_nt(upper, q_part[n]) + dot_nt(lower, q_part[n])
+            folded = [mine[d : d + 1, i * k_fold : (i + 1) * k_fold] for d in range(docs) for i in range(folds)]
+            share = dot_nt(upper, q_part[n]) + dot_nt(lower, q_part[n])
+            piece = jnp.concatenate([share, jnp.concatenate(folded, axis=0)], axis=1)
+            for i in range(nt):
+                out_ref[i * ns + (s ^ (2 * n))] = piece
+                out_ref[i * ns + (s ^ (2 * n + 1))] = piece
 
     return call(
         "finish",
         body,
-        (*(shape((8 + ns * docs, 2 * cols), F32) for _ in range(nx)), shape(TOKEN, F32)),
+        shape((nt * ns, n_rows, n_q + k_fold), F32),
         *grads,
         p_own,
         p_got,
         *queries,
         far=range(ns + 2, ns + 2 + nx),
+        after=after,
         scratch=[
             pltpu.VMEM((ns * high, LANES), F32),
-            pltpu.VMEM((ns * docs, 2 * cols), F32),
+            pltpu.VMEM((n_rows, 2 * cols), F32),
             pltpu.VMEM((nx, n_q, 2 * cols), BF16),
             pltpu.SemaphoreType.DMA((nx,)),
         ],
     )
 
 
-def assemble(near, far, docs, n_q, after):
-    nx = len(near)
-    height, cols = near[0].shape
-
+def assemble(pieces, nt, docs, n_q, cols):
+    ns = pieces.shape[0] // nt
+    nx = ns // 2
+    folds, k_fold = pieces.shape[1] // docs, pieces.shape[2] - n_q
+
+    def body(in_ref, docs_ref, scores_ref):
+        t, _, _, core = place()
+        shares = [in_ref[i * ns + 2 * n + core][:, :n_q] for i in range(nt) for n in range(nx)]
+        while len(shares) > 1:
+            shares = [shares[i] + shares[i + 1] for i in range(0, len(shares), 2)]
+        scores_ref[...] = shares[0]
+        for n in range(nx):
+            folded = in_ref[t * ns + 2 * n + core][:, n_q:]
+            for d in range(docs):
+                parts = [folded[d * folds + i : d * folds + i + 1] for i in range(folds)]
+                docs_ref[d : d + 1, n * cols : (n + 1) * cols] = jnp.concatenate(parts, axis=1)
+
+    out = (shape((docs, nx * cols), F32), shape((pieces.shape[1], n_q), F32))
+    return call("assemble", body, out, pieces)
+
+
+def pair_sum(terms):
     def body(*refs):
-        near_refs, far_refs, (docs_ref, scores_ref) = refs[:nx], refs[nx : 2 * nx], refs[2 * nx :]
-        _, _, x, _ = place()
-        for n in range(nx):
-            docs_ref[:, pl.ds(pl.multiple_of((x ^ n) * cols, LANES), cols)] = near_refs[n][:docs, :]
-        sums = [sum(ref[8:, :n_q] for ref in side) for side in (near_refs, far_refs)]
-        scores_ref[...] = sums[0] + sums[1]
-
-    out = (shape((docs, nx * cols), F32), shape((height - 8, n_q), F32))
-    return call("assemble", body, out, *near, *far, after=after)
-
-
-def pair_sum(terms, after):
-    def body(*refs):
-        values = [ref[...] for ref in refs[:-1]]
+        refs, (out_ref, token_ref) = refs[:-2], refs[-2:]
+        values = [ref[...] for ref in refs]
         while len(values) > 1:
             values = [values[i] + values[i + 1] for i in range(0, len(values), 2)]
-        refs[-1][...] = values[0]
-
-    return call("pair_sum", body, shape(terms[0].shape, F32), *terms, after=after)
+        out_ref[...] = values[0]
+        token_ref[...] = jnp.zeros_like(token_ref)
+
+    return call("pair_sum", body, (shape(terms[0].shape, F32), shape(TOKEN, F32)), *terms)
 
 
 def score_rows(queries, order, store_rows, plan, scores, after):
@@ -449,36 +445,32 @@
 
     inputs = [acts, grads, send(acts, 0, 1), send(grads, 0, 1)]
     mine = pack(nx, proj_in.T, proj_out.T)
-    near = stack([mine] + [send(mine, o, 0) for o in z_offs[1:]], inputs[2:])
+    z_blocks = [mine] + [send(mine, o, 0) for o in z_offs[1:]]
+    across = [send(mine, 1, o) for o in x_offs[1:]]
+    near = stack(z_blocks, inputs[2:] + across)
     by_x = [send(near, 0, o) for o in x_offs[1:]]
     by_y = send(near, 1, 0)
-    firsts, lasts = halves(by_x, by_y, len(z_offs) // 2, [])
-    left, right, rest = project_near(nt, nx, inputs, [near] + by_x, k_in, k_out, [lasts])
-    firsts = [send(b, 1, 0) for b in firsts]
-    lasts = [send(lasts, 0, o) for o in x_offs[1:]]
-    own, other, token = project_rest(left, right, rest, by_y, firsts, lasts, k_in, [])
+    far = [[b] + [send(b, o, 0) for o in z_offs[1:]] for b in across]
+    left, right, rest = project_near(nt, nx, inputs, [near] + by_x, k_in, k_out, [])
+    own, other, token = project_rest(left, right, rest, by_y, far, k_in)
     token, p_late, q_late = lax.optimization_barrier((token, precond, queries))
     tokens = [token]
     p_got = send(p_late, 0, 1)
     q_x = [queries] + [send(q_late, 0, o) for o in x_offs[1:]]
     part = outer(own, send(other, 0, 1), validity)
 
-    total = pair_sum([part] + [send(part, o, 0) for o in z_offs[1:]], [])
+    total, token = pair_sum([part] + [send(part, o, 0) for o in z_offs[1:]])
+    token, *q_late = lax.optimization_barrier((token, *q_x))
+    tokens.append(token)
+    q_near, *q_far = [send(q, 0, 1) for q in q_late]
     total = total + send(total, 1, 0)
     g_own = (total * (1.0 / math.sqrt(toks * nt))).astype(BF16)
     g_all = [g_own] + [send(g_own, 0, o) for o in range(1, ns)]
 
-    *res, token = finish(nx, g_all, precond, p_got, q_x, docs)
-    token, *q_late = lax.optimization_barrier((token, *q_x))
-    tokens.append(token)
-    q_near, *q_far = [send(q, 0, 1) for q in q_late]
-    near = [send(r, 0, o) if o else r for r, o in zip(res, x_offs)]
-    far = [send(r, 1, o) for r, o in zip(res, x_offs)]
-    scores, token = score_rows([queries, q_near], [0, 1], store_rows, plan, None, tokens)
-    precond_docs, partial = assemble(near, far, docs, queries.shape[0], [token])
-    order = [o + c for c in (0, 1) for o in x_offs[1:]]
-    scores, token = score_rows(q_x[1:] + q_far, order, store_rows, plan, scores, [])
-    doc_scores = pair_sum([partial] + [send(partial, o, 0) for o in z_offs[1:]], [token])
+    scores, token = score_rows([q for pair in zip(q_x, [q_near, *q_far]) for q in pair], range(ns), store_rows, plan, None, tokens)
+    pieces = finish(nt, nx, g_all, precond, p_got, q_x, docs, [token])
+    pieces = lax.all_to_all(pieces, AXES, split_axis=0, concat_axis=0, tiled=True)
+    precond_docs, doc_scores = assemble(pieces, nt, docs, queries.shape[0], 2 * precond.shape[0])
     return scores, precond_docs, doc_scores.T
 
 

time: 64 us -> 60 us (0.938)
  blocking collectives: 0 us -> 10.9 us
  waiting for transfers between devices: 25.8 us -> 16.2 us
  starting transfers between devices: 29.6 us -> 25.2 us
  Pallas kernels: 6.77 us -> 5.95 us
    all_to_all x0 -> x1, blocking collectives: none -> 10.9 us  [tiled(): lax.all_to_all(pieces, AXES, split_axis=0, concat_axis=0, tiled=True)]
    ppermute x27 -> x23, waiting for transfers between devices: 25.8 us -> 16.2 us  [send(): return lax.ppermute(value, AXES, perm)]
    ppermute x27 -> x23, starting transfers between devices: 29.6 us -> 25.2 us  [send(): return lax.ppermute(value, AXES, perm)]
    pallas_call x11 -> x8, Pallas kernels: 6.77 us -> 5.95 us  [call(): pl.pallas_call(run, name=name, out_shape=out, in_specs=specs + [pl.BlockS...]
  transfers between devices with their start and end apart: 27 -> 23, of which waited for: 15 -> 11; matrix products, arithmetic and copies ran while one was open for 1% -> 1% of each run, Pallas kernels for 7% -> 6%
where the time goes in v5:
time: 60 us; the launch traced here: 59.9 us
  starting transfers between devices  25.2 us (42%)
  waiting for transfers between devices  16.2 us (27%)
  blocking collectives  10.9 us (18%)
  Pallas kernels  5.95 us (10%)
  between operations  0.81 us (1%)
  local copies, waits for them, and re-layouts  0.77 us (1%)
    ppermute x23, starting transfers between devices, send(): return lax.ppermute(value, AXES, perm)  25.2 us
    ppermute x23, waiting for transfers between devices, send(): return lax.ppermute(value, AXES, perm)  16.2 us
    all_to_all x1, blocking collectives, tiled(): lax.all_to_all(pieces, AXES, split_axis=0, concat_axis=0, tiled=True)  10.9 us
    pallas_call x8, Pallas kernels, call(): pl.pallas_call(run, name=name, out_shape=out, in_specs=specs + [pl.BlockS...  5.95 us
  transfers between devices with their start and end apart: 23, of which 11 were waited for; matrix products, arithmetic and copies ran while one was open for 1% of the time, Pallas kernels for 6%

profile of v5, /device:TPU:0, one launch (start us, length us, event | category | flops | bytes accessed | tf_op | source)
XLA Modules:
  0.0 59.9 jit_solution(1283028644526702088)
XLA Ops:
  0.7 0.5 collective-permute-start
  1.3 0.7 %dynamic-slice_bitcast_fusion.1 = bf16[32,256]{1,0:T(8,128)(2,1)S(1)} fusion(bf16[512,64]{0,1:T(8,128)(2,1)} %param.13, s32[]{:T(128)S(6)} %select_n.25, s32[]{:T(128)S(6)} %select_n.24), kind=kLoop, calls=%fused_computation.3 | loop fusion | bytes 32776 | tf_op jit(solution)/shard_map/dynamic_slice | solution.py:171
  2.0 3.1 %collective-permute-start.2 = (bf16[32,1152]{1,0:T(8,128)(2,1)S(1)}, bf16[32,1152]{1,0:T(8,128)(2,1)S(1)}, u32[]{:S(2)}, u32[]{:S(2)}) collective-permute-start(bf16[32,1152]{1,0:T(8,128)(2,1)S(1)} %pad_maximum_fusion.refs_0_), channel_id=1, source_target_pairs={{0,8},{1,9},{2,10},{3,11},{4,12},{5,13},{6,14},{7,15},{8,0},{9,1},... | collective-permute-start | bytes 221192 | tf_op jit(solution)/shard_map/ppermute | solution.py:440
  5.1 2.6 %collective-permute-start.3 = (bf16[32,1152]{1,0:T(8,128)(2,1)S(1)}, bf16[32,1152]{1,0:T(8,128)(2,1)S(1)}, u32[]{:S(2)}, u32[]{:S(2)}) collective-permute-start(bf16[32,1152]{1,0:T(8,128)(2,1)S(1)} %pad_maximum_fusion.refs_0_), channel_id=1, source_target_pairs={{0,16},{1,17},{2,18},{3,19},{4,20},{5,21},{6,22},{7,23},{8,24},{9,... | collective-permute-start | bytes 221192 | tf_op jit(solution)/shard_map/ppermute | solution.py:440
  7.7 2.7 %collective-permute-start.5 = (bf16[32,1152]{1,0:T(8,128)(2,1)S(1)}, bf16[32,1152]{1,0:T(8,128)(2,1)S(1)}, u32[]{:S(2)}, u32[]{:S(2)}) collective-permute-start(bf16[32,1152]{1,0:T(8,128)(2,1)S(1)} %pad_maximum_fusion.refs_0_), channel_id=1, source_target_pairs={{0,6},{1,7},{2,4},{3,5},{4,2},{5,3},{6,0},{7,1},{8,14},{9,15},{10,... | collective-permute-start | bytes 221192 | tf_op jit(solution)/shard_map/ppermute | solution.py:440
  10.3 2.8 %collective-permute-done.3.refs_2_ = bf16[32,1152]{1,0:T(8,128)(2,1)S(1)} collective-permute-done((bf16[32,1152]{1,0:T(8,128)(2,1)S(1)}, bf16[32,1152]{1,0:T(8,128)(2,1)S(1)}, u32[]{:S(2)}, u32[]{:S(2)}) %collective-permute-start.3) | collective-permute-done | bytes 73760 | tf_op jit(solution)/shard_map/ppermute | solution.py:440
  13.1 0.8 %collective-permute-done.4.refs_3_ = bf16[32,1152]{1,0:T(8,128)(2,1)S(1)} collective-permute-done((bf16[32,1152]{1,0:T(8,128)(2,1)S(1)}, bf16[32,1152]{1,0:T(8,128)(2,1)S(1)}, u32[]{:S(2)}, u32[]{:S(2)}) %collective-permute-start.4) | collective-permute-done | bytes 73760 | tf_op jit(solution)/shard_map/ppermute | solution.py:440
  14.0 1.6 %collective-permute-start.6 = (bf16[4,32,1152]{2,1,0:T(8,128)(2,1)S(1)}, bf16[4,32,1152]{2,1,0:T(8,128)(2,1)S(1)}, u32[]{:S(2)}, u32[]{:S(2)}) collective-permute-start(bf16[4,32,1152]{2,1,0:T(8,128)(2,1)S(1)} %stack.1.refs_4_), channel_id=1, source_target_pairs={{0,2},{1,3},{2,0},{3,1},{4,6},{5,7},{6,4},{7,5},{8,10},{9,11},{10,... | collective-permute-start | bytes 884744 | tf_op jit(solution)/shard_map/ppermute | solution.py:440
  15.5 1.5 %collective-permute-start.7 = (bf16[4,32,1152]{2,1,0:T(8,128)(2,1)S(1)}, bf16[4,32,1152]{2,1,0:T(8,128)(2,1)S(1)}, u32[]{:S(2)}, u32[]{:S(2)}) collective-permute-start(bf16[4,32,1152]{2,1,0:T(8,128)(2,1)S(1)} %stack.1.refs_4_), channel_id=1, source_target_pairs={{0,4},{1,5},{2,6},{3,7},{4,0},{5,1},{6,2},{7,3},{8,12},{9,13},{10,... | collective-permute-start | bytes 884744 | tf_op jit(solution)/shard_map/ppermute | solution.py:440
  17.0 3.6 %collective-permute-start.10 = (bf16[32,1152]{1,0:T(8,128)(2,1)S(1)}, bf16[32,1152]{1,0:T(8,128)(2,1)S(1)}, u32[]{:S(2)}, u32[]{:S(2)}) collective-permute-start(bf16[32,1152]{1,0:T(8,128)(2,1)S(1)} %collective-permute-done.5.refs_6_.refs_4_), channel_id=1, source_target_pairs={{0,24},{1,25},{2,26},{3,27},{4,28},{5,29},{6,30},{7,31},{8,16},{9,... | collective-permute-start | bytes 221192 | tf_op jit(solution)/shard_map/ppermute | solution.py:440
  20.6 0.8 %collective-permute-start.9 = (bf16[32,1152]{1,0:T(8,128)(2,1)S(1)}, bf16[32,1152]{1,0:T(8,128)(2,1)S(1)}, u32[]{:S(2)}, u32[]{:S(2)}) collective-permute-start(bf16[32,1152]{1,0:T(8,128)(2,1)S(1)} %collective-permute-done.5.refs_6_.refs_4_), channel_id=1, source_target_pairs={{0,16},{1,17},{2,18},{3,19},{4,20},{5,21},{6,22},{7,23},{8,24},{9,... | collective-permute-start | bytes 221192 | tf_op jit(solution)/shard_map/ppermute | solution.py:440
  21.5 1.3 %project_near.1 = (f32[128,64]{1,0:T(8,128)S(1)}, f32[64,128]{1,0:T(8,128)S(1)}, bf16[4,128,1152]{2,1,0:T(8,128)(2,1)S(1)}) custom-call(bf16[64,14336]{1,0:T(8,128)(2,1)S(1)} %bitcast.9, bf16[64,4096]{1,0:T(8,128)(2,1)S(1)} %bitcast.11, bf16[64,14336]{1,0:T(8,128)(2,1)S(1)} %collective-permute-done.refs_4_.refs_2_, ...), custom_call_target="tpu_custom_call" | custom-call | bytes 5308416 | tf_op jit(solution)/shard_map/project_near/pallas_call | solution.py:150
  22.8 0.9 %collective-permute-done.10.refs_7_ = bf16[32,1152]{1,0:T(8,128)(2,1)S(1)} collective-permute-done((bf16[32,1152]{1,0:T(8,128)(2,1)S(1)}, bf16[32,1152]{1,0:T(8,128)(2,1)S(1)}, u32[]{:S(2)}, u32[]{:S(2)}) %collective-permute-start.10) | collective-permute-done | bytes 73760 | tf_op jit(solution)/shard_map/ppermute | solution.py:440
  23.8 1.2 %collective-permute-done.8.refs_5_ = bf16[32,1152]{1,0:T(8,128)(2,1)S(1)} collective-permute-done((bf16[32,1152]{1,0:T(8,128)(2,1)S(1)}, bf16[32,1152]{1,0:T(8,128)(2,1)S(1)}, u32[]{:S(2)}, u32[]{:S(2)}) %collective-permute-start.8) | collective-permute-done | bytes 73760 | tf_op jit(solution)/shard_map/ppermute | solution.py:440
  25.0 0.9 %collective-permute-done.9.refs_6_ = bf16[32,1152]{1,0:T(8,128)(2,1)S(1)} collective-permute-done((bf16[32,1152]{1,0:T(8,128)(2,1)S(1)}, bf16[32,1152]{1,0:T(8,128)(2,1)S(1)}, u32[]{:S(2)}, u32[]{:S(2)}) %collective-permute-start.9) | collective-permute-done | bytes 73760 | tf_op jit(solution)/shard_map/ppermute | solution.py:440
  25.9 0.6 project_rest.1
  26.5 0.6 %collective-permute-start.15 = (bf16[64,4096]{1,0:T(8,128)(2,1)S(1)}, bf16[64,4096]{1,0:T(8,128)(2,1)S(1)}, u32[]{:S(2)}, u32[]{:S(2)}) collective-permute-start(bf16[64,4096]{1,0:T(8,128)(2,1)S(1)} %copy-done.1), channel_id=1, source_target_pairs={{0,2},{1,3},{2,0},{3,1},{4,6},{5,7},{6,4},{7,5},{8,10},{9,11},{10,... | collective-permute-start | bytes 1572872 | tf_op jit(solution)/shard_map/ppermute | solution.py:440
  27.1 0.5 collective-permute-start.11
  27.6 2.2 %collective-permute-done.11.refs_1_ = f32[64,128]{1,0:T(8,128)S(1)} collective-permute-done((f32[64,128]{1,0:T(8,128)S(1)}, f32[64,128]{1,0:T(8,128)S(1)}, u32[]{:S(2)}, u32[]{:S(2)}) %collective-permute-start.11) | collective-permute-done | bytes 32800 | tf_op jit(solution)/shard_map/ppermute | solution.py:440
  30.1 2.1 %collective-permute-start.12 = (f32[64,128]{1,0:T(8,128)S(1)}, f32[64,128]{1,0:T(8,128)S(1)}, u32[]{:S(2)}, u32[]{:S(2)}) collective-permute-start(f32[64,128]{1,0:T(8,128)S(1)} %outer.1.refs_0_), channel_id=1, source_target_pairs={{0,8},{1,9},{2,10},{3,11},{4,12},{5,13},{6,14},{7,15},{8,0},{9,1},... | collective-permute-start | bytes 98312 | tf_op jit(solution)/shard_map/ppermute | solution.py:440
  32.4 2.2 %collective-permute-start.14 = (f32[64,128]{1,0:T(8,128)S(1)}, f32[64,128]{1,0:T(8,128)S(1)}, u32[]{:S(2)}, u32[]{:S(2)}) collective-permute-start(f32[64,128]{1,0:T(8,128)S(1)} %outer.1.refs_0_), channel_id=1, source_target_pairs={{0,24},{1,25},{2,26},{3,27},{4,28},{5,29},{6,30},{7,31},{8,16},{9,... | collective-permute-start | bytes 98312 | tf_op jit(solution)/shard_map/ppermute | solution.py:440
  34.6 2.8 %collective-permute-done.13.refs_2_ = f32[64,128]{1,0:T(8,128)S(1)} collective-permute-done((f32[64,128]{1,0:T(8,128)S(1)}, f32[64,128]{1,0:T(8,128)S(1)}, u32[]{:S(2)}, u32[]{:S(2)}) %collective-permute-start.13) | collective-permute-done | bytes 32800 | tf_op jit(solution)/shard_map/ppermute | solution.py:440
  37.4 0.7 %collective-permute-done.14.refs_3_ = f32[64,128]{1,0:T(8,128)S(1)} collective-permute-done((f32[64,128]{1,0:T(8,128)S(1)}, f32[64,128]{1,0:T(8,128)S(1)}, u32[]{:S(2)}, u32[]{:S(2)}) %collective-permute-start.14) | collective-permute-done | bytes 32800 | tf_op jit(solution)/shard_map/ppermute | solution.py:440
  38.3 0.5 collective-permute-start.17
  38.8 0.8 %collective-permute-start.18 = (f32[64,128]{1,0:T(8,128)S(1)}, f32[64,128]{1,0:T(8,128)S(1)}, u32[]{:S(2)}, u32[]{:S(2)}) collective-permute-start(f32[64,128]{1,0:T(8,128)S(1)} %get-tuple-element.34), channel_id=1, source_target_pairs={{0,4},{1,5},{2,6},{3,7},{4,0},{5,1},{6,2},{7,3},{8,12},{9,13},{10,... | collective-permute-start | bytes 98312 | tf_op jit(solution)/shard_map/ppermute | solution.py:440
  39.6 3.1 %collective-permute-done.18 = f32[64,128]{1,0:T(8,128)S(1)} collective-permute-done((f32[64,128]{1,0:T(8,128)S(1)}, f32[64,128]{1,0:T(8,128)S(1)}, u32[]{:S(2)}, u32[]{:S(2)}) %collective-permute-start.18) | collective-permute-done | bytes 32800 | tf_op jit(solution)/shard_map/ppermute | solution.py:440
  42.8 1.4 %collective-permute-start.20 = (bf16[64,128]{1,0:T(8,128)(2,1)S(1)}, bf16[64,128]{1,0:T(8,128)(2,1)S(1)}, u32[]{:S(2)}, u32[]{:S(2)}) collective-permute-start(bf16[64,128]{1,0:T(8,128)(2,1)S(1)} %multiply_convert_fusion.refs_0_), channel_id=1, source_target_pairs={{0,2},{1,3},{2,0},{3,1},{4,6},{5,7},{6,4},{7,5},{8,10},{9,11},{10,... | collective-permute-start | bytes 49160 | tf_op jit(solution)/shard_map/ppermute | solution.py:440
  44.7 2.2 %score_rows.1 = (f32[256,128]{1,0:T(8,128)}, f32[8,128]{1,0:T(8,128)S(1)}) custom-call(bf16[64,4096]{1,0:T(8,128)(2,1)S(1)} %copy-done.1, bf16[64,4096]{1,0:T(8,128)(2,1)S(1)} %collective-permute-done.16.refs_1_, bf16[64,4096]{1,0:T(8,128)(2,1)S(1)} %collective-permute-done.15.refs_2_.refs_7_, bf16[64,4096]{1,0:T(8,128)(2,1)S(1)} %collective-permute-done.17.refs_3_, ...), custom_call_target="tpu_custom_call" | custom-call | bytes 4194320 | tf_op jit(solution)/shard_map/score_rows/pallas_call | solution.py:150
  46.9 0.5 collective-permute-done.21.refs_3_
  47.4 0.9 %finish.1 = f32[32,8,128]{2,1,0:T(8,128)S(1)} custom-call(bf16[64,128]{1,0:T(8,128)(2,1)S(1)} %multiply_convert_fusion.refs_0_, bf16[64,128]{1,0:T(8,128)(2,1)S(1)} %collective-permute-done.19.refs_1_, bf16[64,128]{1,0:T(8,128)(2,1)S(1)} %collective-permute-done.20.refs_2_, bf16[64,128]{1,0:T(8,128)(2,1)S(1)} %collective-permute-done.21.refs_3_, ...), custom_call_target="tpu_custom_call" | custom-call | bytes 3211264 | tf_op jit(solution)/shard_map/finish/pallas_call | solution.py:150
  48.3 10.9 %all_to_all.5.refs_0_ = f32[32,8,128]{2,1,0:T(8,128)S(1)} all-to-all(f32[32,8,128]{2,1,0:T(8,128)S(1)} %finish.1), channel_id=1, replica_groups=mesh['tok'=8,'store'=4] {'tok','store'}, dimensions={0} | all-to-all | bytes 262144 | tf_op jit(solution)/shard_map/all_to_all | solution.py:472
  59.2 0.7 %assemble.1 = (f32[2,512]{1,0:T(2,128)}, f32[8,64]{1,0:T(8,128)}) custom-call(f32[32,8,128]{2,1,0:T(8,128)S(1)} %all_to_all.5.refs_0_), custom_call_target="tpu_custom_call" | custom-call | bytes 131072 | tf_op jit(solution)/shard_map/assemble/pallas_call | solution.py:150
  (43 shorter events, 1.5 us)
Async XLA Ops:
  0.6 1.3 %copy-start = (bf16[1792,64]{0,1:T(8,128)(2,1)S(1)}, bf16[1792,64]{0,1:T(8,128)(2,1)}, u32[]{:S(2)}) copy-start(bf16[1792,64]{0,1:T(8,128)(2,1)} %param.12) | copy-start | bytes 688132
  0.6 20.8 %copy-start.5 = (bf16[2,32,4096]{2,1,0:T(8,128)(2,1)S(1)}, bf16[2,32,4096]{2,1,0:T(8,128)(2,1)}, u32[]{:S(2)}) copy-start(bf16[2,32,4096]{2,1,0:T(8,128)(2,1)} %param.10) | copy-start | bytes 1572868
  0.7 13.3 %collective-permute-start = (bf16[64,14336]{1,0:T(8,128)(2,1)}, bf16[64,14336]{1,0:T(8,128)(2,1)S(1)}, u32[]{:S(2)}, u32[]{:S(2)}) collective-permute-start(bf16[64,14336]{1,0:T(8,128)(2,1)} %bitcast.8), channel_id=1, source_target_pairs={{0,1},{1,0},{2,3},{3,2},{4,5},{5,4},{6,7},{7,6},{8,9},{9,8},{10,11... | collective-permute-start | bytes 5505032 | tf_op jit(solution)/shard_map/ppermute | solution.py:440
  1.2 12.7 %collective-permute-start.1 = (bf16[64,4096]{1,0:T(8,128)(2,1)}, bf16[64,4096]{1,0:T(8,128)(2,1)S(1)}, u32[]{:S(2)}, u32[]{:S(2)}) collective-permute-start(bf16[64,4096]{1,0:T(8,128)(2,1)} %bitcast.10), channel_id=1, source_target_pairs={{0,1},{1,0},{2,3},{3,2},{4,5},{5,4},{6,7},{7,6},{8,9},{9,8},{10,11... | collective-permute-start | bytes 1572872 | tf_op jit(solution)/shard_map/ppermute | solution.py:440
  2.0 19.5 %copy-start.3 = (bf16[2,32,14336]{2,1,0:T(8,128)(2,1)S(1)}, bf16[2,32,14336]{2,1,0:T(8,128)(2,1)}, u32[]{:S(2)}) copy-start(bf16[2,32,14336]{2,1,0:T(8,128)(2,1)} %param.9) | copy-start | bytes 5505028
  2.0 5.7 %collective-permute-start.2 = (bf16[32,1152]{1,0:T(8,128)(2,1)S(1)}, bf16[32,1152]{1,0:T(8,128)(2,1)S(1)}, u32[]{:S(2)}, u32[]{:S(2)}) collective-permute-start(bf16[32,1152]{1,0:T(8,128)(2,1)S(1)} %pad_maximum_fusion.refs_0_), channel_id=1, source_target_pairs={{0,8},{1,9},{2,10},{3,11},{4,12},{5,13},{6,14},{7,15},{8,0},{9,1},... | collective-permute-start | bytes 221192 | tf_op jit(solution)/shard_map/ppermute | solution.py:440
  5.1 8.0 %collective-permute-start.3 = (bf16[32,1152]{1,0:T(8,128)(2,1)S(1)}, bf16[32,1152]{1,0:T(8,128)(2,1)S(1)}, u32[]{:S(2)}, u32[]{:S(2)}) collective-permute-start(bf16[32,1152]{1,0:T(8,128)(2,1)S(1)} %pad_maximum_fusion.refs_0_), channel_id=1, source_target_pairs={{0,16},{1,17},{2,18},{3,19},{4,20},{5,21},{6,22},{7,23},{8,24},{9,... | collective-permute-start | bytes 221192 | tf_op jit(solution)/shard_map/ppermute | solution.py:440
  7.7 6.3 %collective-permute-start.4 = (bf16[32,1152]{1,0:T(8,128)(2,1)S(1)}, bf16[32,1152]{1,0:T(8,128)(2,1)S(1)}, u32[]{:S(2)}, u32[]{:S(2)}) collective-permute-start(bf16[32,1152]{1,0:T(8,128)(2,1)S(1)} %pad_maximum_fusion.refs_0_), channel_id=1, source_target_pairs={{0,24},{1,25},{2,26},{3,27},{4,28},{5,29},{6,30},{7,31},{8,16},{9,... | collective-permute-start | bytes 221192 | tf_op jit(solution)/shard_map/ppermute | solution.py:440
  7.7 6.3 %collective-permute-start.5 = (bf16[32,1152]{1,0:T(8,128)(2,1)S(1)}, bf16[32,1152]{1,0:T(8,128)(2,1)S(1)}, u32[]{:S(2)}, u32[]{:S(2)}) collective-permute-start(bf16[32,1152]{1,0:T(8,128)(2,1)S(1)} %pad_maximum_fusion.refs_0_), channel_id=1, source_target_pairs={{0,6},{1,7},{2,4},{3,5},{4,2},{5,3},{6,0},{7,1},{8,14},{9,15},{10,... | collective-permute-start | bytes 221192 | tf_op jit(solution)/shard_map/ppermute | solution.py:440
  14.0 7.5 %collective-permute-start.6 = (bf16[4,32,1152]{2,1,0:T(8,128)(2,1)S(1)}, bf16[4,32,1152]{2,1,0:T(8,128)(2,1)S(1)}, u32[]{:S(2)}, u32[]{:S(2)}) collective-permute-start(bf16[4,32,1152]{2,1,0:T(8,128)(2,1)S(1)} %stack.1.refs_4_), channel_id=1, source_target_pairs={{0,2},{1,3},{2,0},{3,1},{4,6},{5,7},{6,4},{7,5},{8,10},{9,11},{10,... | collective-permute-start | bytes 884744 | tf_op jit(solution)/shard_map/ppermute | solution.py:440
  15.5 10.3 %collective-permute-start.7 = (bf16[4,32,1152]{2,1,0:T(8,128)(2,1)S(1)}, bf16[4,32,1152]{2,1,0:T(8,128)(2,1)S(1)}, u32[]{:S(2)}, u32[]{:S(2)}) collective-permute-start(bf16[4,32,1152]{2,1,0:T(8,128)(2,1)S(1)} %stack.1.refs_4_), channel_id=1, source_target_pairs={{0,4},{1,5},{2,6},{3,7},{4,0},{5,1},{6,2},{7,3},{8,12},{9,13},{10,... | collective-permute-start | bytes 884744 | tf_op jit(solution)/shard_map/ppermute | solution.py:440
  17.0 6.7 %collective-permute-start.10 = (bf16[32,1152]{1,0:T(8,128)(2,1)S(1)}, bf16[32,1152]{1,0:T(8,128)(2,1)S(1)}, u32[]{:S(2)}, u32[]{:S(2)}) collective-permute-start(bf16[32,1152]{1,0:T(8,128)(2,1)S(1)} %collective-permute-done.5.refs_6_.refs_4_), channel_id=1, source_target_pairs={{0,24},{1,25},{2,26},{3,27},{4,28},{5,29},{6,30},{7,31},{8,16},{9,... | collective-permute-start | bytes 221192 | tf_op jit(solution)/shard_map/ppermute | solution.py:440
  20.6 4.4 %collective-permute-start.8 = (bf16[32,1152]{1,0:T(8,128)(2,1)S(1)}, bf16[32,1152]{1,0:T(8,128)(2,1)S(1)}, u32[]{:S(2)}, u32[]{:S(2)}) collective-permute-start(bf16[32,1152]{1,0:T(8,128)(2,1)S(1)} %collective-permute-done.5.refs_6_.refs_4_), channel_id=1, source_target_pairs={{0,8},{1,9},{2,10},{3,11},{4,12},{5,13},{6,14},{7,15},{8,0},{9,1},... | collective-permute-start | bytes 221192 | tf_op jit(solution)/shard_map/ppermute | solution.py:440
  20.6 5.3 %collective-permute-start.9 = (bf16[32,1152]{1,0:T(8,128)(2,1)S(1)}, bf16[32,1152]{1,0:T(8,128)(2,1)S(1)}, u32[]{:S(2)}, u32[]{:S(2)}) collective-permute-start(bf16[32,1152]{1,0:T(8,128)(2,1)S(1)} %collective-permute-done.5.refs_6_.refs_4_), channel_id=1, source_target_pairs={{0,16},{1,17},{2,18},{3,19},{4,20},{5,21},{6,22},{7,23},{8,24},{9,... | collective-permute-start | bytes 221192 | tf_op jit(solution)/shard_map/ppermute | solution.py:440
  21.4 23.3 %copy-start.2 = (f32[128,4096]{1,0:T(8,128)S(1)}, f32[128,4096]{1,0:T(8,128)}, u32[]{:S(2)}) copy-start(f32[128,4096]{1,0:T(8,128)} %refs_4_.2) | copy-start | bytes 6291460
  22.8 3.7 %copy-start.1 = (bf16[64,4096]{1,0:T(8,128)(2,1)S(1)}, bf16[64,4096]{1,0:T(8,128)(2,1)}, u32[]{:S(2)}) copy-start(bf16[64,4096]{1,0:T(8,128)(2,1)} %refs_6_.1) | copy-start | bytes 1572868
  22.8 4.3 %copy-start.4 = (bf16[128,4096]{1,0:T(8,128)(2,1)S(1)}, bf16[128,4096]{1,0:T(8,128)(2,1)}, u32[]{:S(2)}) copy-start(bf16[128,4096]{1,0:T(8,128)(2,1)} %refs_4_.3) | copy-start | bytes 3145732
  22.8 7.0 %copy-start.6 = (s32[2,32]{1,0:T(2,128)S(1)}, s32[2,32]{1,0:T(2,128)}, u32[]{:S(2)}) copy-start(s32[2,32]{1,0:T(2,128)} %refs_2_.1) | copy-start | bytes 772
  22.8 21.9 %copy-start.7 = (s32[4,1]{0,1:T(1,128)S(1)}, s32[4,1]{0,1:T(1,128)}, u32[]{:S(2)}) copy-start(s32[4,1]{0,1:T(1,128)} %param.17) | copy-start | bytes 52
  26.5 11.9 %collective-permute-start.15 = (bf16[64,4096]{1,0:T(8,128)(2,1)S(1)}, bf16[64,4096]{1,0:T(8,128)(2,1)S(1)}, u32[]{:S(2)}, u32[]{:S(2)}) collective-permute-start(bf16[64,4096]{1,0:T(8,128)(2,1)S(1)} %copy-done.1), channel_id=1, source_target_pairs={{0,2},{1,3},{2,0},{3,1},{4,6},{5,7},{6,4},{7,5},{8,10},{9,11},{10,... | collective-permute-start | bytes 1572872 | tf_op jit(solution)/shard_map/ppermute | solution.py:440
  27.1 20.4 %collective-permute-start.22 = (bf16[128,4096]{1,0:T(8,128)(2,1)S(1)}, bf16[128,4096]{1,0:T(8,128)(2,1)S(1)}, u32[]{:S(2)}, u32[]{:S(2)}) collective-permute-start(bf16[128,4096]{1,0:T(8,128)(2,1)S(1)} %copy-done.4), channel_id=1, source_target_pairs={{0,1},{1,0},{2,3},{3,2},{4,5},{5,4},{6,7},{7,6},{8,9},{9,8},{10,11... | collective-permute-start | bytes 3145736 | tf_op jit(solution)/shard_map/ppermute | solution.py:440
  27.1 2.7 %collective-permute-start.11 = (f32[64,128]{1,0:T(8,128)S(1)}, f32[64,128]{1,0:T(8,128)S(1)}, u32[]{:S(2)}, u32[]{:S(2)}) collective-permute-start(f32[64,128]{1,0:T(8,128)S(1)} %get-tuple-element.25), channel_id=1, source_target_pairs={{0,1},{1,0},{2,3},{3,2},{4,5},{5,4},{6,7},{7,6},{8,9},{9,8},{10,11... | collective-permute-start | bytes 98312 | tf_op jit(solution)/shard_map/ppermute | solution.py:440
  30.1 4.5 %collective-permute-start.12 = (f32[64,128]{1,0:T(8,128)S(1)}, f32[64,128]{1,0:T(8,128)S(1)}, u32[]{:S(2)}, u32[]{:S(2)}) collective-permute-start(f32[64,128]{1,0:T(8,128)S(1)} %outer.1.refs_0_), channel_id=1, source_target_pairs={{0,8},{1,9},{2,10},{3,11},{4,12},{5,13},{6,14},{7,15},{8,0},{9,1},... | collective-permute-start | bytes 98312 | tf_op jit(solution)/shard_map/ppermute | solution.py:440
  32.1 5.2 %collective-permute-start.13 = (f32[64,128]{1,0:T(8,128)S(1)}, f32[64,128]{1,0:T(8,128)S(1)}, u32[]{:S(2)}, u32[]{:S(2)}) collective-permute-start(f32[64,128]{1,0:T(8,128)S(1)} %outer.1.refs_0_), channel_id=1, source_target_pairs={{0,16},{1,17},{2,18},{3,19},{4,20},{5,21},{6,22},{7,23},{8,24},{9,... | collective-permute-start | bytes 98312 | tf_op jit(solution)/shard_map/ppermute | solution.py:440
  32.4 5.7 %collective-permute-start.14 = (f32[64,128]{1,0:T(8,128)S(1)}, f32[64,128]{1,0:T(8,128)S(1)}, u32[]{:S(2)}, u32[]{:S(2)}) collective-permute-start(f32[64,128]{1,0:T(8,128)S(1)} %outer.1.refs_0_), channel_id=1, source_target_pairs={{0,24},{1,25},{2,26},{3,27},{4,28},{5,29},{6,30},{7,31},{8,16},{9,... | collective-permute-start | bytes 98312 | tf_op jit(solution)/shard_map/ppermute | solution.py:440
  38.3 5.9 %collective-permute-start.16 = (bf16[64,4096]{1,0:T(8,128)(2,1)S(1)}, bf16[64,4096]{1,0:T(8,128)(2,1)S(1)}, u32[]{:S(2)}, u32[]{:S(2)}) collective-permute-start(bf16[64,4096]{1,0:T(8,128)(2,1)S(1)} %copy-done.1), channel_id=1, source_target_pairs={{0,1},{1,0},{2,3},{3,2},{4,5},{5,4},{6,7},{7,6},{8,9},{9,8},{10,11... | collective-permute-start | bytes 1572872 | tf_op jit(solution)/shard_map/ppermute | solution.py:440
  38.3 6.4 %collective-permute-start.17 = (bf16[64,4096]{1,0:T(8,128)(2,1)S(1)}, bf16[64,4096]{1,0:T(8,128)(2,1)S(1)}, u32[]{:S(2)}, u32[]{:S(2)}) collective-permute-start(bf16[64,4096]{1,0:T(8,128)(2,1)S(1)} %collective-permute-done.15.refs_2_.refs_7_), channel_id=1, source_target_pairs={{0,1},{1,0},{2,3},{3,2},{4,5},{5,4},{6,7},{7,6},{8,9},{9,8},{10,11... | collective-permute-start | bytes 1572872 | tf_op jit(solution)/shard_map/ppermute | solution.py:440
  38.8 3.9 %collective-permute-start.18 = (f32[64,128]{1,0:T(8,128)S(1)}, f32[64,128]{1,0:T(8,128)S(1)}, u32[]{:S(2)}, u32[]{:S(2)}) collective-permute-start(f32[64,128]{1,0:T(8,128)S(1)} %get-tuple-element.34), channel_id=1, source_target_pairs={{0,4},{1,5},{2,6},{3,7},{4,0},{5,1},{6,2},{7,3},{8,12},{9,13},{10,... | collective-permute-start | bytes 98312 | tf_op jit(solution)/shard_map/ppermute | solution.py:440
  42.8 4.1 %collective-permute-start.19 = (bf16[64,128]{1,0:T(8,128)(2,1)S(1)}, bf16[64,128]{1,0:T(8,128)(2,1)S(1)}, u32[]{:S(2)}, u32[]{:S(2)}) collective-permute-start(bf16[64,128]{1,0:T(8,128)(2,1)S(1)} %multiply_convert_fusion.refs_0_), channel_id=1, source_target_pairs={{0,1},{1,0},{2,3},{3,2},{4,5},{5,4},{6,7},{7,6},{8,9},{9,8},{10,11... | collective-permute-start | bytes 49160 | tf_op jit(solution)/shard_map/ppermute | solution.py:440
  42.8 4.1 %collective-permute-start.20 = (bf16[64,128]{1,0:T(8,128)(2,1)S(1)}, bf16[64,128]{1,0:T(8,128)(2,1)S(1)}, u32[]{:S(2)}, u32[]{:S(2)}) collective-permute-start(bf16[64,128]{1,0:T(8,128)(2,1)S(1)} %multiply_convert_fusion.refs_0_), channel_id=1, source_target_pairs={{0,2},{1,3},{2,0},{3,1},{4,6},{5,7},{6,4},{7,5},{8,10},{9,11},{10,... | collective-permute-start | bytes 49160 | tf_op jit(solution)/shard_map/ppermute | solution.py:440
  44.3 3.2 %collective-permute-start.21 = (bf16[64,128]{1,0:T(8,128)(2,1)S(1)}, bf16[64,128]{1,0:T(8,128)(2,1)S(1)}, u32[]{:S(2)}, u32[]{:S(2)}) collective-permute-start(bf16[64,128]{1,0:T(8,128)(2,1)S(1)} %multiply_convert_fusion.refs_0_), channel_id=1, source_target_pairs={{0,3},{1,2},{2,1},{3,0},{4,7},{5,6},{6,5},{7,4},{8,11},{9,10},{10,... | collective-permute-start | bytes 49160 | tf_op jit(solution)/shard_map/ppermute | solution.py:440

commit v6 on v5

--- a/solution.py
+++ b/solution.py
@@ -274,7 +274,8 @@
     feat = mine.shape[0]
     half = feat // 2
 
-    def body(mine_ref, got_ref, valid_ref, out_ref, both):
+    def body(mine_ref, got_ref, valid_ref, out_ref, token_ref, both):
+        token_ref[...] = jnp.zeros_like(token_ref)
         both[...] = mine_ref[...] + got_ref[...]
         rights = [both[pl.ds(n, half, stride=2), : docs * toks].astype(BF16) for n in (0, 1)]
         lefts = both[:, docs * toks :].astype(BF16)
@@ -284,11 +285,11 @@
             parts = [jnp.dot(r[:, at] * mask, lefts[at], preferred_element_type=F32) for r in rights]
             out_ref[d * half : (d + 1) * half, :] = jnp.concatenate(parts, axis=1)
 
-    out = shape((docs * half, 2 * feat), F32)
+    out = (shape((docs * half, 2 * feat), F32), shape(TOKEN, F32))
     return call("outer", body, out, mine, got, validity, scratch=[pltpu.VMEM(mine.shape, F32)])
 
 
-def finish(nt, nx, grads, p_own, p_got, queries, docs, after):
+def finish(nt, nx, grads, p_own, p_got, queries, docs):
     ns = len(grads)
     high = grads[0].shape[0]
     pairs = high // docs
@@ -300,7 +301,8 @@
 
     def body(*refs):
         g_refs, p_refs, q_refs = refs[:ns], refs[ns : ns + 2], refs[ns + 2 : ns + 2 + nx]
-        out_ref, wide, pre, q_part, sems = refs[-5:]
+        out_ref, token_ref, wide, pre, q_part, sems = refs[-6:]
+        token_ref[...] = jnp.zeros_like(token_ref)
         t, s, x, core = place()
         at = pl.multiple_of((t * nx + x) * 2 * cols, LANES)
         copies = [
@@ -328,19 +330,17 @@
             share = dot_nt(upper, q_part[n]) + dot_nt(lower, q_part[n])
             piece = jnp.concatenate([share, jnp.concatenate(folded, axis=0)], axis=1)
             for i in range(nt):
-                out_ref[i * ns + (s ^ (2 * n))] = piece
-                out_ref[i * ns + (s ^ (2 * n + 1))] = piece
+                out_ref[i * nx + (x ^ n)] = piece
 
     return call(
         "finish",
         body,
-        shape((nt * ns, n_rows, n_q + k_fold), F32),
+        (shape((nt * nx, n_rows, n_q + k_fold), F32), shape(TOKEN, F32)),
         *grads,
         p_own,
         p_got,
         *queries,
         far=range(ns + 2, ns + 2 + nx),
-        after=after,
         scratch=[
             pltpu.VMEM((ns * high, LANES), F32),
             pltpu.VMEM((n_rows, 2 * cols), F32),
@@ -350,25 +350,24 @@
     )
 
 
-def assemble(pieces, nt, docs, n_q, cols):
-    ns = pieces.shape[0] // nt
-    nx = ns // 2
+def assemble(pieces, nt, docs, n_q, cols, after):
+    nx = pieces.shape[0] // nt
     folds, k_fold = pieces.shape[1] // docs, pieces.shape[2] - n_q
 
     def body(in_ref, docs_ref, scores_ref):
-        t, _, _, core = place()
-        shares = [in_ref[i * ns + 2 * n + core][:, :n_q] for i in range(nt) for n in range(nx)]
+        t, _, _, _ = place()
+        shares = [in_ref[i][:, :n_q] for i in range(nt * nx)]
         while len(shares) > 1:
             shares = [shares[i] + shares[i + 1] for i in range(0, len(shares), 2)]
         scores_ref[...] = shares[0]
         for n in range(nx):
-            folded = in_ref[t * ns + 2 * n + core][:, n_q:]
+            folded = in_ref[t * nx + n][:, n_q:]
             for d in range(docs):
                 parts = [folded[d * folds + i : d * folds + i + 1] for i in range(folds)]
                 docs_ref[d : d + 1, n * cols : (n + 1) * cols] = jnp.concatenate(parts, axis=1)
 
     out = (shape((docs, nx * cols), F32), shape((pieces.shape[1], n_q), F32))
-    return call("assemble", body, out, pieces)
+    return call("assemble", body, out, pieces, after=after)
 
 
 def pair_sum(terms):
@@ -453,24 +452,31 @@
     far = [[b] + [send(b, o, 0) for o in z_offs[1:]] for b in across]
     left, right, rest = project_near(nt, nx, inputs, [near] + by_x, k_in, k_out, [])
     own, other, token = project_rest(left, right, rest, by_y, far, k_in)
-    token, p_late, q_late = lax.optimization_barrier((token, precond, queries))
+    token, q_late = lax.optimization_barrier((token, queries))
     tokens = [token]
+    q_x = [queries] + [send(q_late, 0, o) for o in x_offs[1:]]
+    part, token = outer(own, send(other, 0, 1), validity)
+    token, p_late = lax.optimization_barrier((token, precond))
+    tokens.append(token)
     p_got = send(p_late, 0, 1)
-    q_x = [queries] + [send(q_late, 0, o) for o in x_offs[1:]]
-    part = outer(own, send(other, 0, 1), validity)
 
     total, token = pair_sum([part] + [send(part, o, 0) for o in z_offs[1:]])
-    token, *q_late = lax.optimization_barrier((token, *q_x))
+    token, q_late = lax.optimization_barrier((token, queries))
     tokens.append(token)
-    q_near, *q_far = [send(q, 0, 1) for q in q_late]
+    q_near = send(q_late, 0, 1)
     total = total + send(total, 1, 0)
     g_own = (total * (1.0 / math.sqrt(toks * nt))).astype(BF16)
     g_all = [g_own] + [send(g_own, 0, o) for o in range(1, ns)]
 
-    scores, token = score_rows([q for pair in zip(q_x, [q_near, *q_far]) for q in pair], range(ns), store_rows, plan, None, tokens)
-    pieces = finish(nt, nx, g_all, precond, p_got, q_x, docs, [token])
-    pieces = lax.all_to_all(pieces, AXES, split_axis=0, concat_axis=0, tiled=True)
-    precond_docs, doc_scores = assemble(pieces, nt, docs, queries.shape[0], 2 * precond.shape[0])
+    pieces, token = finish(nt, nx, g_all, precond, p_got, q_x, docs)
+    groups = [[i * ns + 2 * j + c for i in range(nt) for j in range(nx)] for c in (0, 1)]
+    pieces = lax.all_to_all(pieces, AXES, split_axis=0, concat_axis=0, tiled=True, axis_index_groups=groups)
+    token, *q_late = lax.optimization_barrier((token, *q_x[1:]))
+    tokens.append(token)
+    q_far = [send(q, 0, 1) for q in q_late]
+    q_all = [q for pair in zip(q_x, [q_near, *q_far]) for q in pair]
+    scores, token = score_rows(q_all, range(ns), store_rows, plan, None, tokens)
+    precond_docs, doc_scores = assemble(pieces, nt, docs, queries.shape[0], 2 * precond.shape[0], [token])
     return scores, precond_docs, doc_scores.T
 
 

time: 60 us -> 59.4 us (0.990)
  blocking collectives: 10.9 us -> 0 us
  waiting for transfers between devices: 16.2 us -> 21.6 us
  starting transfers between devices: 25.2 us -> 28.4 us
  Pallas kernels: 5.95 us -> 7.55 us
    all_to_all x1 -> x0, blocking collectives: 10.9 us -> none  [tiled(): lax.all_to_all(pieces, AXES, split_axis=0, concat_axis=0, tiled=True)]
    all_to_all x0 -> x1, waiting for transfers between devices: none -> 4.35 us  [tiled(): lax.all_to_all(pieces, AXES, split_axis=0, concat_axis=0, tiled=True, axi...]
    all_to_all x0 -> x1, starting transfers between devices: none -> 3.63 us  [tiled(): lax.all_to_all(pieces, AXES, split_axis=0, concat_axis=0, tiled=True, axi...]
    pallas_call x8, Pallas kernels: 5.95 us -> 7.55 us  [call(): pl.pallas_call(run, name=name, out_shape=out, in_specs=specs + [pl.BlockS...]
    ppermute x23, waiting for transfers between devices: 16.2 us -> 17.2 us  [send(): return lax.ppermute(value, AXES, perm)]
  transfers between devices with their start and end apart: 23 -> 24, of which waited for: 11 -> 12; matrix products, arithmetic and copies ran while one was open for 1% -> 1% of each run, Pallas kernels for 6% -> 10%
where the time goes in v6:
time: 59.4 us; the launch traced here: 59.2 us
  starting transfers between devices  28.4 us (48%)
  waiting for transfers between devices  21.6 us (36%)
  Pallas kernels  7.55 us (13%)
  between operations  0.83 us (1%)
  local copies, waits for them, and re-layouts  0.77 us (1%)
    ppermute x23, starting transfers between devices, send(): return lax.ppermute(value, AXES, perm)  24.8 us
    ppermute x23, waiting for transfers between devices, send(): return lax.ppermute(value, AXES, perm)  17.2 us
    pallas_call x8, Pallas kernels, call(): pl.pallas_call(run, name=name, out_shape=out, in_specs=specs + [pl.BlockS...  7.55 us
    all_to_all x1, waiting for transfers between devices, tiled(): lax.all_to_all(pieces, AXES, split_axis=0, concat_axis=0, tiled=True, axi...  4.35 us
    all_to_all x1, starting transfers between devices, tiled(): lax.all_to_all(pieces, AXES, split_axis=0, concat_axis=0, tiled=True, axi...  3.63 us
  transfers between devices with their start and end apart: 24, of which 12 were waited for; matrix products, arithmetic and copies ran while one was open for 1% of the time, Pallas kernels for 10%

profile of v6, /device:TPU:0, one launch (start us, length us, event | category | flops | bytes accessed | tf_op | source)
XLA Modules:
  0.0 59.2 jit_solution(11646738264845560111)
XLA Ops:
  0.7 0.5 collective-permute-start
  1.3 0.7 %dynamic-slice_bitcast_fusion.1 = bf16[32,256]{1,0:T(8,128)(2,1)S(1)} fusion(bf16[512,64]{0,1:T(8,128)(2,1)} %param.13, s32[]{:T(128)S(6)} %select_n.25, s32[]{:T(128)S(6)} %select_n.24), kind=kLoop, calls=%fused_computation.3 | loop fusion | bytes 32776 | tf_op jit(solution)/shard_map/dynamic_slice | solution.py:171
  2.0 3.1 %collective-permute-start.2 = (bf16[32,1152]{1,0:T(8,128)(2,1)S(1)}, bf16[32,1152]{1,0:T(8,128)(2,1)S(1)}, u32[]{:S(2)}, u32[]{:S(2)}) collective-permute-start(bf16[32,1152]{1,0:T(8,128)(2,1)S(1)} %pad_maximum_fusion.refs_0_), channel_id=1, source_target_pairs={{0,8},{1,9},{2,10},{3,11},{4,12},{5,13},{6,14},{7,15},{8,0},{9,1},... | collective-permute-start | bytes 221192 | tf_op jit(solution)/shard_map/ppermute | solution.py:439
  5.1 2.6 %collective-permute-start.3 = (bf16[32,1152]{1,0:T(8,128)(2,1)S(1)}, bf16[32,1152]{1,0:T(8,128)(2,1)S(1)}, u32[]{:S(2)}, u32[]{:S(2)}) collective-permute-start(bf16[32,1152]{1,0:T(8,128)(2,1)S(1)} %pad_maximum_fusion.refs_0_), channel_id=1, source_target_pairs={{0,16},{1,17},{2,18},{3,19},{4,20},{5,21},{6,22},{7,23},{8,24},{9,... | collective-permute-start | bytes 221192 | tf_op jit(solution)/shard_map/ppermute | solution.py:439
  7.7 2.7 %collective-permute-start.5 = (bf16[32,1152]{1,0:T(8,128)(2,1)S(1)}, bf16[32,1152]{1,0:T(8,128)(2,1)S(1)}, u32[]{:S(2)}, u32[]{:S(2)}) collective-permute-start(bf16[32,1152]{1,0:T(8,128)(2,1)S(1)} %pad_maximum_fusion.refs_0_), channel_id=1, source_target_pairs={{0,6},{1,7},{2,4},{3,5},{4,2},{5,3},{6,0},{7,1},{8,14},{9,15},{10,... | collective-permute-start | bytes 221192 | tf_op jit(solution)/shard_map/ppermute | solution.py:439
  10.3 2.8 %collective-permute-done.3.refs_2_ = bf16[32,1152]{1,0:T(8,128)(2,1)S(1)} collective-permute-done((bf16[32,1152]{1,0:T(8,128)(2,1)S(1)}, bf16[32,1152]{1,0:T(8,128)(2,1)S(1)}, u32[]{:S(2)}, u32[]{:S(2)}) %collective-permute-start.3) | collective-permute-done | bytes 73760 | tf_op jit(solution)/shard_map/ppermute | solution.py:439
  13.1 0.8 %collective-permute-done.4.refs_3_ = bf16[32,1152]{1,0:T(8,128)(2,1)S(1)} collective-permute-done((bf16[32,1152]{1,0:T(8,128)(2,1)S(1)}, bf16[32,1152]{1,0:T(8,128)(2,1)S(1)}, u32[]{:S(2)}, u32[]{:S(2)}) %collective-permute-start.4) | collective-permute-done | bytes 73760 | tf_op jit(solution)/shard_map/ppermute | solution.py:439
  14.0 1.6 %collective-permute-start.6 = (bf16[4,32,1152]{2,1,0:T(8,128)(2,1)S(1)}, bf16[4,32,1152]{2,1,0:T(8,128)(2,1)S(1)}, u32[]{:S(2)}, u32[]{:S(2)}) collective-permute-start(bf16[4,32,1152]{2,1,0:T(8,128)(2,1)S(1)} %stack.1.refs_4_), channel_id=1, source_target_pairs={{0,2},{1,3},{2,0},{3,1},{4,6},{5,7},{6,4},{7,5},{8,10},{9,11},{10,... | collective-permute-start | bytes 884744 | tf_op jit(solution)/shard_map/ppermute | solution.py:439
  15.5 1.5 %collective-permute-start.7 = (bf16[4,32,1152]{2,1,0:T(8,128)(2,1)S(1)}, bf16[4,32,1152]{2,1,0:T(8,128)(2,1)S(1)}, u32[]{:S(2)}, u32[]{:S(2)}) collective-permute-start(bf16[4,32,1152]{2,1,0:T(8,128)(2,1)S(1)} %stack.1.refs_4_), channel_id=1, source_target_pairs={{0,4},{1,5},{2,6},{3,7},{4,0},{5,1},{6,2},{7,3},{8,12},{9,13},{10,... | collective-permute-start | bytes 884744 | tf_op jit(solution)/shard_map/ppermute | solution.py:439
  17.0 3.6 %collective-permute-start.10 = (bf16[32,1152]{1,0:T(8,128)(2,1)S(1)}, bf16[32,1152]{1,0:T(8,128)(2,1)S(1)}, u32[]{:S(2)}, u32[]{:S(2)}) collective-permute-start(bf16[32,1152]{1,0:T(8,128)(2,1)S(1)} %collective-permute-done.5.refs_6_.refs_4_), channel_id=1, source_target_pairs={{0,24},{1,25},{2,26},{3,27},{4,28},{5,29},{6,30},{7,31},{8,16},{9,... | collective-permute-start | bytes 221192 | tf_op jit(solution)/shard_map/ppermute | solution.py:439
  20.6 0.8 %collective-permute-start.9 = (bf16[32,1152]{1,0:T(8,128)(2,1)S(1)}, bf16[32,1152]{1,0:T(8,128)(2,1)S(1)}, u32[]{:S(2)}, u32[]{:S(2)}) collective-permute-start(bf16[32,1152]{1,0:T(8,128)(2,1)S(1)} %collective-permute-done.5.refs_6_.refs_4_), channel_id=1, source_target_pairs={{0,16},{1,17},{2,18},{3,19},{4,20},{5,21},{6,22},{7,23},{8,24},{9,... | collective-permute-start | bytes 221192 | tf_op jit(solution)/shard_map/ppermute | solution.py:439
  21.4 1.3 %project_near.1 = (f32[128,64]{1,0:T(8,128)S(1)}, f32[64,128]{1,0:T(8,128)S(1)}, bf16[4,128,1152]{2,1,0:T(8,128)(2,1)S(1)}) custom-call(bf16[64,14336]{1,0:T(8,128)(2,1)S(1)} %bitcast.9, bf16[64,4096]{1,0:T(8,128)(2,1)S(1)} %bitcast.11, bf16[64,14336]{1,0:T(8,128)(2,1)S(1)} %collective-permute-done.refs_4_.refs_2_, ...), custom_call_target="tpu_custom_call" | custom-call | bytes 5308416 | tf_op jit(solution)/shard_map/project_near/pallas_call | solution.py:150
  22.8 0.9 %collective-permute-done.10.refs_7_ = bf16[32,1152]{1,0:T(8,128)(2,1)S(1)} collective-permute-done((bf16[32,1152]{1,0:T(8,128)(2,1)S(1)}, bf16[32,1152]{1,0:T(8,128)(2,1)S(1)}, u32[]{:S(2)}, u32[]{:S(2)}) %collective-permute-start.10) | collective-permute-done | bytes 73760 | tf_op jit(solution)/shard_map/ppermute | solution.py:439
  23.8 1.2 %collective-permute-done.8.refs_5_ = bf16[32,1152]{1,0:T(8,128)(2,1)S(1)} collective-permute-done((bf16[32,1152]{1,0:T(8,128)(2,1)S(1)}, bf16[32,1152]{1,0:T(8,128)(2,1)S(1)}, u32[]{:S(2)}, u32[]{:S(2)}) %collective-permute-start.8) | collective-permute-done | bytes 73760 | tf_op jit(solution)/shard_map/ppermute | solution.py:439
  25.0 0.9 %collective-permute-done.9.refs_6_ = bf16[32,1152]{1,0:T(8,128)(2,1)S(1)} collective-permute-done((bf16[32,1152]{1,0:T(8,128)(2,1)S(1)}, bf16[32,1152]{1,0:T(8,128)(2,1)S(1)}, u32[]{:S(2)}, u32[]{:S(2)}) %collective-permute-start.9) | collective-permute-done | bytes 73760 | tf_op jit(solution)/shard_map/ppermute | solution.py:439
  25.9 0.6 project_rest.1
  26.6 1.2 %collective-permute-done.11.refs_1_ = f32[64,128]{1,0:T(8,128)S(1)} collective-permute-done((f32[64,128]{1,0:T(8,128)S(1)}, f32[64,128]{1,0:T(8,128)S(1)}, u32[]{:S(2)}, u32[]{:S(2)}) %collective-permute-start.11) | collective-permute-done | bytes 32800 | tf_op jit(solution)/shard_map/ppermute | solution.py:439
  28.3 0.5 collective-permute-start.16
  28.8 2.0 %collective-permute-start.12 = (f32[64,128]{1,0:T(8,128)S(1)}, f32[64,128]{1,0:T(8,128)S(1)}, u32[]{:S(2)}, u32[]{:S(2)}) collective-permute-start(f32[64,128]{1,0:T(8,128)S(1)} %get-tuple-element.32.refs_0_), channel_id=1, source_target_pairs={{0,8},{1,9},{2,10},{3,11},{4,12},{5,13},{6,14},{7,15},{8,0},{9,1},... | collective-permute-start | bytes 98312 | tf_op jit(solution)/shard_map/ppermute | solution.py:439
  31.0 2.1 %collective-permute-start.14 = (f32[64,128]{1,0:T(8,128)S(1)}, f32[64,128]{1,0:T(8,128)S(1)}, u32[]{:S(2)}, u32[]{:S(2)}) collective-permute-start(f32[64,128]{1,0:T(8,128)S(1)} %get-tuple-element.32.refs_0_), channel_id=1, source_target_pairs={{0,24},{1,25},{2,26},{3,27},{4,28},{5,29},{6,30},{7,31},{8,16},{9,... | collective-permute-start | bytes 98312 | tf_op jit(solution)/shard_map/ppermute | solution.py:439
  33.2 2.7 %collective-permute-done.13.refs_2_ = f32[64,128]{1,0:T(8,128)S(1)} collective-permute-done((f32[64,128]{1,0:T(8,128)S(1)}, f32[64,128]{1,0:T(8,128)S(1)}, u32[]{:S(2)}, u32[]{:S(2)}) %collective-permute-start.13) | collective-permute-done | bytes 32800 | tf_op jit(solution)/shard_map/ppermute | solution.py:439
  35.9 0.8 %collective-permute-done.14.refs_3_ = f32[64,128]{1,0:T(8,128)S(1)} collective-permute-done((f32[64,128]{1,0:T(8,128)S(1)}, f32[64,128]{1,0:T(8,128)S(1)}, u32[]{:S(2)}, u32[]{:S(2)}) %collective-permute-start.14) | collective-permute-done | bytes 32800 | tf_op jit(solution)/shard_map/ppermute | solution.py:439
  36.8 0.7 %collective-permute-start.17 = (f32[64,128]{1,0:T(8,128)S(1)}, f32[64,128]{1,0:T(8,128)S(1)}, u32[]{:S(2)}, u32[]{:S(2)}) collective-permute-start(f32[64,128]{1,0:T(8,128)S(1)} %get-tuple-element.37), channel_id=1, source_target_pairs={{0,4},{1,5},{2,6},{3,7},{4,0},{5,1},{6,2},{7,3},{8,12},{9,13},{10,... | collective-permute-start | bytes 98312 | tf_op jit(solution)/shard_map/ppermute | solution.py:439
  37.5 3.3 %collective-permute-done.17 = f32[64,128]{1,0:T(8,128)S(1)} collective-permute-done((f32[64,128]{1,0:T(8,128)S(1)}, f32[64,128]{1,0:T(8,128)S(1)}, u32[]{:S(2)}, u32[]{:S(2)}) %collective-permute-start.17) | collective-permute-done | bytes 32800 | tf_op jit(solution)/shard_map/ppermute | solution.py:439
  40.8 1.6 %collective-permute-start.19 = (bf16[64,128]{1,0:T(8,128)(2,1)S(1)}, bf16[64,128]{1,0:T(8,128)(2,1)S(1)}, u32[]{:S(2)}, u32[]{:S(2)}) collective-permute-start(bf16[64,128]{1,0:T(8,128)(2,1)S(1)} %multiply_convert_fusion.refs_0_), channel_id=1, source_target_pairs={{0,2},{1,3},{2,0},{3,1},{4,6},{5,7},{6,4},{7,5},{8,10},{9,11},{10,... | collective-permute-start | bytes 49160 | tf_op jit(solution)/shard_map/ppermute | solution.py:439
  43.1 1.6 %collective-permute-done.19.refs_2_ = bf16[64,128]{1,0:T(8,128)(2,1)S(1)} collective-permute-done((bf16[64,128]{1,0:T(8,128)(2,1)S(1)}, bf16[64,128]{1,0:T(8,128)(2,1)S(1)}, u32[]{:S(2)}, u32[]{:S(2)}) %collective-permute-start.19) | collective-permute-done | bytes 16416 | tf_op jit(solution)/shard_map/ppermute | solution.py:439
  44.7 0.9 %collective-permute-done.20.refs_3_ = bf16[64,128]{1,0:T(8,128)(2,1)S(1)} collective-permute-done((bf16[64,128]{1,0:T(8,128)(2,1)S(1)}, bf16[64,128]{1,0:T(8,128)(2,1)S(1)}, u32[]{:S(2)}, u32[]{:S(2)}) %collective-permute-start.20) | collective-permute-done | bytes 16416 | tf_op jit(solution)/shard_map/ppermute | solution.py:439
  45.6 1.5 %finish.1 = (f32[16,8,128]{2,1,0:T(8,128)}, f32[8,128]{1,0:T(8,128)S(1)}) custom-call(bf16[64,128]{1,0:T(8,128)(2,1)S(1)} %multiply_convert_fusion.refs_0_, bf16[64,128]{1,0:T(8,128)(2,1)S(1)} %collective-permute-done.18.refs_1_, bf16[64,128]{1,0:T(8,128)(2,1)S(1)} %collective-permute-done.19.refs_2_, bf16[64,128]{1,0:T(8,128)(2,1)S(1)} %collective-permute-done.20.refs_3_, ...), custom_call_target="tpu_custom_call" | custom-call | bytes 3211264 | tf_op jit(solution)/shard_map/finish/pallas_call | solution.py:150
  47.3 3.6 %all-to-all-start = ((f32[16,8,128]{2,1,0:T(8,128)}), f32[16,8,128]{2,1,0:T(8,128)S(1)}, u32[]{:S(2)}, u32[]{:S(2)}) async-start(f32[16,8,128]{2,1,0:T(8,128)} %get-tuple-element.47), calls=%async_computation | async-start | bytes 131072 | tf_op jit(solution)/shard_map/all_to_all | solution.py:473
  51.0 3.1 %score_rows.1 = (f32[256,128]{1,0:T(8,128)}, f32[8,128]{1,0:T(8,128)S(1)}) custom-call(bf16[64,4096]{1,0:T(8,128)(2,1)S(1)} %copy-done.1, bf16[64,4096]{1,0:T(8,128)(2,1)} %collective-permute-done.15.refs_1_, bf16[64,4096]{1,0:T(8,128)(2,1)S(1)} %collective-permute-done.16.refs_7_.refs_2_, bf16[64,4096]{1,0:T(8,128)(2,1)} %collective-permute-done.22.refs_3_, ...), custom_call_target="tpu_custom_call" | custom-call | bytes 4194320 | tf_op jit(solution)/shard_map/score_rows/pallas_call | solution.py:150
  54.1 4.3 %all-to-all-done.refs_0_ = f32[16,8,128]{2,1,0:T(8,128)S(1)} async-done(((f32[16,8,128]{2,1,0:T(8,128)}), f32[16,8,128]{2,1,0:T(8,128)S(1)}, u32[]{:S(2)}, u32[]{:S(2)}) %all-to-all-start) | async-done | bytes 65568 | tf_op jit(solution)/shard_map/all_to_all | solution.py:473
  58.5 0.7 %assemble.1 = (f32[2,512]{1,0:T(2,128)}, f32[8,64]{1,0:T(8,128)}) custom-call(f32[16,8,128]{2,1,0:T(8,128)S(1)} %all-to-all-done.refs_0_, f32[8,128]{1,0:T(8,128)S(1)} %get-tuple-element.48.refs_1_), custom_call_target="tpu_custom_call" | custom-call | bytes 65536 | tf_op jit(solution)/shard_map/assemble/pallas_call | solution.py:150
  (44 shorter events, 2.0 us)
Async XLA Ops:
  0.6 1.3 %copy-start = (bf16[1792,64]{0,1:T(8,128)(2,1)S(1)}, bf16[1792,64]{0,1:T(8,128)(2,1)}, u32[]{:S(2)}) copy-start(bf16[1792,64]{0,1:T(8,128)(2,1)} %param.12) | copy-start | bytes 688132
  0.6 20.8 %copy-start.5 = (bf16[2,32,4096]{2,1,0:T(8,128)(2,1)S(1)}, bf16[2,32,4096]{2,1,0:T(8,128)(2,1)}, u32[]{:S(2)}) copy-start(bf16[2,32,4096]{2,1,0:T(8,128)(2,1)} %param.10) | copy-start | bytes 1572868
  0.7 13.3 %collective-permute-start = (bf16[64,14336]{1,0:T(8,128)(2,1)}, bf16[64,14336]{1,0:T(8,128)(2,1)S(1)}, u32[]{:S(2)}, u32[]{:S(2)}) collective-permute-start(bf16[64,14336]{1,0:T(8,128)(2,1)} %bitcast.8), channel_id=1, source_target_pairs={{0,1},{1,0},{2,3},{3,2},{4,5},{5,4},{6,7},{7,6},{8,9},{9,8},{10,11... | collective-permute-start | bytes 5505032 | tf_op jit(solution)/shard_map/ppermute | solution.py:439
  1.2 12.7 %collective-permute-start.1 = (bf16[64,4096]{1,0:T(8,128)(2,1)}, bf16[64,4096]{1,0:T(8,128)(2,1)S(1)}, u32[]{:S(2)}, u32[]{:S(2)}) collective-permute-start(bf16[64,4096]{1,0:T(8,128)(2,1)} %bitcast.10), channel_id=1, source_target_pairs={{0,1},{1,0},{2,3},{3,2},{4,5},{5,4},{6,7},{7,6},{8,9},{9,8},{10,11... | collective-permute-start | bytes 1572872 | tf_op jit(solution)/shard_map/ppermute | solution.py:439
  2.0 19.5 %copy-start.3 = (bf16[2,32,14336]{2,1,0:T(8,128)(2,1)S(1)}, bf16[2,32,14336]{2,1,0:T(8,128)(2,1)}, u32[]{:S(2)}) copy-start(bf16[2,32,14336]{2,1,0:T(8,128)(2,1)} %param.9) | copy-start | bytes 5505028
  2.0 5.7 %collective-permute-start.2 = (bf16[32,1152]{1,0:T(8,128)(2,1)S(1)}, bf16[32,1152]{1,0:T(8,128)(2,1)S(1)}, u32[]{:S(2)}, u32[]{:S(2)}) collective-permute-start(bf16[32,1152]{1,0:T(8,128)(2,1)S(1)} %pad_maximum_fusion.refs_0_), channel_id=1, source_target_pairs={{0,8},{1,9},{2,10},{3,11},{4,12},{5,13},{6,14},{7,15},{8,0},{9,1},... | collective-permute-start | bytes 221192 | tf_op jit(solution)/shard_map/ppermute | solution.py:439
  5.1 8.0 %collective-permute-start.3 = (bf16[32,1152]{1,0:T(8,128)(2,1)S(1)}, bf16[32,1152]{1,0:T(8,128)(2,1)S(1)}, u32[]{:S(2)}, u32[]{:S(2)}) collective-permute-start(bf16[32,1152]{1,0:T(8,128)(2,1)S(1)} %pad_maximum_fusion.refs_0_), channel_id=1, source_target_pairs={{0,16},{1,17},{2,18},{3,19},{4,20},{5,21},{6,22},{7,23},{8,24},{9,... | collective-permute-start | bytes 221192 | tf_op jit(solution)/shard_map/ppermute | solution.py:439
  7.7 6.3 %collective-permute-start.4 = (bf16[32,1152]{1,0:T(8,128)(2,1)S(1)}, bf16[32,1152]{1,0:T(8,128)(2,1)S(1)}, u32[]{:S(2)}, u32[]{:S(2)}) collective-permute-start(bf16[32,1152]{1,0:T(8,128)(2,1)S(1)} %pad_maximum_fusion.refs_0_), channel_id=1, source_target_pairs={{0,24},{1,25},{2,26},{3,27},{4,28},{5,29},{6,30},{7,31},{8,16},{9,... | collective-permute-start | bytes 221192 | tf_op jit(solution)/shard_map/ppermute | solution.py:439
  7.7 6.3 %collective-permute-start.5 = (bf16[32,1152]{1,0:T(8,128)(2,1)S(1)}, bf16[32,1152]{1,0:T(8,128)(2,1)S(1)}, u32[]{:S(2)}, u32[]{:S(2)}) collective-permute-start(bf16[32,1152]{1,0:T(8,128)(2,1)S(1)} %pad_maximum_fusion.refs_0_), channel_id=1, source_target_pairs={{0,6},{1,7},{2,4},{3,5},{4,2},{5,3},{6,0},{7,1},{8,14},{9,15},{10,... | collective-permute-start | bytes 221192 | tf_op jit(solution)/shard_map/ppermute | solution.py:439
  14.0 7.5 %collective-permute-start.6 = (bf16[4,32,1152]{2,1,0:T(8,128)(2,1)S(1)}, bf16[4,32,1152]{2,1,0:T(8,128)(2,1)S(1)}, u32[]{:S(2)}, u32[]{:S(2)}) collective-permute-start(bf16[4,32,1152]{2,1,0:T(8,128)(2,1)S(1)} %stack.1.refs_4_), channel_id=1, source_target_pairs={{0,2},{1,3},{2,0},{3,1},{4,6},{5,7},{6,4},{7,5},{8,10},{9,11},{10,... | collective-permute-start | bytes 884744 | tf_op jit(solution)/shard_map/ppermute | solution.py:439
  15.5 10.3 %collective-permute-start.7 = (bf16[4,32,1152]{2,1,0:T(8,128)(2,1)S(1)}, bf16[4,32,1152]{2,1,0:T(8,128)(2,1)S(1)}, u32[]{:S(2)}, u32[]{:S(2)}) collective-permute-start(bf16[4,32,1152]{2,1,0:T(8,128)(2,1)S(1)} %stack.1.refs_4_), channel_id=1, source_target_pairs={{0,4},{1,5},{2,6},{3,7},{4,0},{5,1},{6,2},{7,3},{8,12},{9,13},{10,... | collective-permute-start | bytes 884744 | tf_op jit(solution)/shard_map/ppermute | solution.py:439
  17.0 6.7 %collective-permute-start.10 = (bf16[32,1152]{1,0:T(8,128)(2,1)S(1)}, bf16[32,1152]{1,0:T(8,128)(2,1)S(1)}, u32[]{:S(2)}, u32[]{:S(2)}) collective-permute-start(bf16[32,1152]{1,0:T(8,128)(2,1)S(1)} %collective-permute-done.5.refs_6_.refs_4_), channel_id=1, source_target_pairs={{0,24},{1,25},{2,26},{3,27},{4,28},{5,29},{6,30},{7,31},{8,16},{9,... | collective-permute-start | bytes 221192 | tf_op jit(solution)/shard_map/ppermute | solution.py:439
  20.6 4.4 %collective-permute-start.8 = (bf16[32,1152]{1,0:T(8,128)(2,1)S(1)}, bf16[32,1152]{1,0:T(8,128)(2,1)S(1)}, u32[]{:S(2)}, u32[]{:S(2)}) collective-permute-start(bf16[32,1152]{1,0:T(8,128)(2,1)S(1)} %collective-permute-done.5.refs_6_.refs_4_), channel_id=1, source_target_pairs={{0,8},{1,9},{2,10},{3,11},{4,12},{5,13},{6,14},{7,15},{8,0},{9,1},... | collective-permute-start | bytes 221192 | tf_op jit(solution)/shard_map/ppermute | solution.py:439
  20.6 5.3 %collective-permute-start.9 = (bf16[32,1152]{1,0:T(8,128)(2,1)S(1)}, bf16[32,1152]{1,0:T(8,128)(2,1)S(1)}, u32[]{:S(2)}, u32[]{:S(2)}) collective-permute-start(bf16[32,1152]{1,0:T(8,128)(2,1)S(1)} %collective-permute-done.5.refs_6_.refs_4_), channel_id=1, source_target_pairs={{0,16},{1,17},{2,18},{3,19},{4,20},{5,21},{6,22},{7,23},{8,24},{9,... | collective-permute-start | bytes 221192 | tf_op jit(solution)/shard_map/ppermute | solution.py:439
  22.8 5.0 %copy-start.6 = (s32[2,32]{1,0:T(2,128)S(1)}, s32[2,32]{1,0:T(2,128)}, u32[]{:S(2)}) copy-start(s32[2,32]{1,0:T(2,128)} %refs_2_.1) | copy-start | bytes 772
  22.8 5.3 %copy-start.4 = (bf16[128,4096]{1,0:T(8,128)(2,1)S(1)}, bf16[128,4096]{1,0:T(8,128)(2,1)}, u32[]{:S(2)}) copy-start(bf16[128,4096]{1,0:T(8,128)(2,1)} %refs_4_.2) | copy-start | bytes 3145732
  22.8 5.5 %copy-start.1 = (bf16[64,4096]{1,0:T(8,128)(2,1)S(1)}, bf16[64,4096]{1,0:T(8,128)(2,1)}, u32[]{:S(2)}) copy-start(bf16[64,4096]{1,0:T(8,128)(2,1)} %refs_0_.1) | copy-start | bytes 1572868
  26.5 24.5 %copy-start.2 = (f32[128,4096]{1,0:T(8,128)S(1)}, f32[128,4096]{1,0:T(8,128)}, u32[]{:S(2)}) copy-start(f32[128,4096]{1,0:T(8,128)} %refs_4_.3) | copy-start | bytes 6291460
  26.5 24.5 %copy-start.7 = (s32[4,1]{0,1:T(1,128)S(1)}, s32[4,1]{0,1:T(1,128)}, u32[]{:S(2)}) copy-start(s32[4,1]{0,1:T(1,128)} %param.17) | copy-start | bytes 52
  26.5 1.3 %collective-permute-start.11 = (f32[64,128]{1,0:T(8,128)S(1)}, f32[64,128]{1,0:T(8,128)S(1)}, u32[]{:S(2)}, u32[]{:S(2)}) collective-permute-start(f32[64,128]{1,0:T(8,128)S(1)} %get-tuple-element.31), channel_id=1, source_target_pairs={{0,1},{1,0},{2,3},{3,2},{4,5},{5,4},{6,7},{7,6},{8,9},{9,8},{10,11... | collective-permute-start | bytes 98312 | tf_op jit(solution)/shard_map/ppermute | solution.py:439
  28.1 17.5 %collective-permute-start.21 = (bf16[128,4096]{1,0:T(8,128)(2,1)S(1)}, bf16[128,4096]{1,0:T(8,128)(2,1)S(1)}, u32[]{:S(2)}, u32[]{:S(2)}) collective-permute-start(bf16[128,4096]{1,0:T(8,128)(2,1)S(1)} %copy-done.4), channel_id=1, source_target_pairs={{0,1},{1,0},{2,3},{3,2},{4,5},{5,4},{6,7},{7,6},{8,9},{9,8},{10,11... | collective-permute-start | bytes 3145736 | tf_op jit(solution)/shard_map/ppermute | solution.py:439
  28.3 17.3 %collective-permute-start.16 = (bf16[64,4096]{1,0:T(8,128)(2,1)S(1)}, bf16[64,4096]{1,0:T(8,128)(2,1)S(1)}, u32[]{:S(2)}, u32[]{:S(2)}) collective-permute-start(bf16[64,4096]{1,0:T(8,128)(2,1)S(1)} %copy-done.1), channel_id=1, source_target_pairs={{0,2},{1,3},{2,0},{3,1},{4,6},{5,7},{6,4},{7,5},{8,10},{9,11},{10,... | collective-permute-start | bytes 1572872 | tf_op jit(solution)/shard_map/ppermute | solution.py:439
  28.8 4.4 %collective-permute-start.12 = (f32[64,128]{1,0:T(8,128)S(1)}, f32[64,128]{1,0:T(8,128)S(1)}, u32[]{:S(2)}, u32[]{:S(2)}) collective-permute-start(f32[64,128]{1,0:T(8,128)S(1)} %get-tuple-element.32.refs_0_), channel_id=1, source_target_pairs={{0,8},{1,9},{2,10},{3,11},{4,12},{5,13},{6,14},{7,15},{8,0},{9,1},... | collective-permute-start | bytes 98312 | tf_op jit(solution)/shard_map/ppermute | solution.py:439
  30.8 5.1 %collective-permute-start.13 = (f32[64,128]{1,0:T(8,128)S(1)}, f32[64,128]{1,0:T(8,128)S(1)}, u32[]{:S(2)}, u32[]{:S(2)}) collective-permute-start(f32[64,128]{1,0:T(8,128)S(1)} %get-tuple-element.32.refs_0_), channel_id=1, source_target_pairs={{0,16},{1,17},{2,18},{3,19},{4,20},{5,21},{6,22},{7,23},{8,24},{9,... | collective-permute-start | bytes 98312 | tf_op jit(solution)/shard_map/ppermute | solution.py:439
  31.0 5.7 %collective-permute-start.14 = (f32[64,128]{1,0:T(8,128)S(1)}, f32[64,128]{1,0:T(8,128)S(1)}, u32[]{:S(2)}, u32[]{:S(2)}) collective-permute-start(f32[64,128]{1,0:T(8,128)S(1)} %get-tuple-element.32.refs_0_), channel_id=1, source_target_pairs={{0,24},{1,25},{2,26},{3,27},{4,28},{5,29},{6,30},{7,31},{8,16},{9,... | collective-permute-start | bytes 98312 | tf_op jit(solution)/shard_map/ppermute | solution.py:439
  36.8 4.0 %collective-permute-start.17 = (f32[64,128]{1,0:T(8,128)S(1)}, f32[64,128]{1,0:T(8,128)S(1)}, u32[]{:S(2)}, u32[]{:S(2)}) collective-permute-start(f32[64,128]{1,0:T(8,128)S(1)} %get-tuple-element.37), channel_id=1, source_target_pairs={{0,4},{1,5},{2,6},{3,7},{4,0},{5,1},{6,2},{7,3},{8,12},{9,13},{10,... | collective-permute-start | bytes 98312 | tf_op jit(solution)/shard_map/ppermute | solution.py:439
  40.8 1.9 %collective-permute-start.18 = (bf16[64,128]{1,0:T(8,128)(2,1)S(1)}, bf16[64,128]{1,0:T(8,128)(2,1)S(1)}, u32[]{:S(2)}, u32[]{:S(2)}) collective-permute-start(bf16[64,128]{1,0:T(8,128)(2,1)S(1)} %multiply_convert_fusion.refs_0_), channel_id=1, source_target_pairs={{0,1},{1,0},{2,3},{3,2},{4,5},{5,4},{6,7},{7,6},{8,9},{9,8},{10,11... | collective-permute-start | bytes 49160 | tf_op jit(solution)/shard_map/ppermute | solution.py:439
  40.8 3.8 %collective-permute-start.19 = (bf16[64,128]{1,0:T(8,128)(2,1)S(1)}, bf16[64,128]{1,0:T(8,128)(2,1)S(1)}, u32[]{:S(2)}, u32[]{:S(2)}) collective-permute-start(bf16[64,128]{1,0:T(8,128)(2,1)S(1)} %multiply_convert_fusion.refs_0_), channel_id=1, source_target_pairs={{0,2},{1,3},{2,0},{3,1},{4,6},{5,7},{6,4},{7,5},{8,10},{9,11},{10,... | collective-permute-start | bytes 49160 | tf_op jit(solution)/shard_map/ppermute | solution.py:439
  42.4 3.2 %collective-permute-start.20 = (bf16[64,128]{1,0:T(8,128)(2,1)S(1)}, bf16[64,128]{1,0:T(8,128)(2,1)S(1)}, u32[]{:S(2)}, u32[]{:S(2)}) collective-permute-start(bf16[64,128]{1,0:T(8,128)(2,1)S(1)} %multiply_convert_fusion.refs_0_), channel_id=1, source_target_pairs={{0,3},{1,2},{2,1},{3,0},{4,7},{5,6},{6,5},{7,4},{8,11},{9,10},{10,... | collective-permute-start | bytes 49160 | tf_op jit(solution)/shard_map/ppermute | solution.py:439
  42.7 8.2 %collective-permute-start.15 = (bf16[64,4096]{1,0:T(8,128)(2,1)S(1)}, bf16[64,4096]{1,0:T(8,128)(2,1)}, u32[]{:S(2)}, u32[]{:S(2)}) collective-permute-start(bf16[64,4096]{1,0:T(8,128)(2,1)S(1)} %copy-done.1), channel_id=1, source_target_pairs={{0,1},{1,0},{2,3},{3,2},{4,5},{5,4},{6,7},{7,6},{8,9},{9,8},{10,11... | collective-permute-start | bytes 1572872 | tf_op jit(solution)/shard_map/ppermute | solution.py:439
  47.1 3.9 %collective-permute-start.22 = (bf16[64,4096]{1,0:T(8,128)(2,1)S(1)}, bf16[64,4096]{1,0:T(8,128)(2,1)}, u32[]{:S(2)}, u32[]{:S(2)}) collective-permute-start(bf16[64,4096]{1,0:T(8,128)(2,1)S(1)} %collective-permute-done.16.refs_7_.refs_2_), channel_id=1, source_target_pairs={{0,1},{1,0},{2,3},{3,2},{4,5},{5,4},{6,7},{7,6},{8,9},{9,8},{10,11... | collective-permute-start | bytes 1572872 | tf_op jit(solution)/shard_map/ppermute | solution.py:439
  47.3 11.2 %all-to-all-start = ((f32[16,8,128]{2,1,0:T(8,128)}), f32[16,8,128]{2,1,0:T(8,128)S(1)}, u32[]{:S(2)}, u32[]{:S(2)}) async-start(f32[16,8,128]{2,1,0:T(8,128)} %get-tuple-element.47), calls=%async_computation | async-start | bytes 131072 | tf_op jit(solution)/shard_map/all_to_all | solution.py:473

commit v7 on v6

--- a/solution.py
+++ b/solution.py
@@ -290,8 +290,8 @@
 
 
 def finish(nt, nx, grads, p_own, p_got, queries, docs):
-    ns = len(grads)
-    high = grads[0].shape[0]
+    ns = 2 * nx
+    high = grads[0].shape[1]
     pairs = high // docs
     cols = p_own.shape[0]
     n_q = queries[0].shape[0]
@@ -300,7 +300,7 @@
     k_fold = 2 * cols // folds
 
     def body(*refs):
-        g_refs, p_refs, q_refs = refs[:ns], refs[ns : ns + 2], refs[ns + 2 : ns + 2 + nx]
+        g_refs, p_refs, q_refs = refs[:2], refs[2:4], refs[4 : 4 + nx]
         out_ref, token_ref, wide, pre, q_part, sems = refs[-6:]
         token_ref[...] = jnp.zeros_like(token_ref)
         t, s, x, core = place()
@@ -311,8 +311,8 @@
         for copy in copies:
             copy.start()
         for n in range(ns):
-            at = pl.multiple_of((s ^ n) * high, high)
-            wide[pl.ds(at, high), :] = g_refs[n][...].astype(F32)
+            at = pl.multiple_of((n // 2 * 2 + (core ^ (n % 2))) * high, high)
+            wide[pl.ds(at, high), :] = g_refs[n % 2][n // 2].astype(F32)
         rows = [wide[pl.ds(j, n_rows, stride=pairs), :] for j in range(pairs)]
         rows = jnp.concatenate(rows, axis=1).astype(BF16)
         for ref, c in zip(p_refs, (core, 1 - core)):
@@ -340,7 +340,7 @@
         p_own,
         p_got,
         *queries,
-        far=range(ns + 2, ns + 2 + nx),
+        far=range(4, 4 + nx),
         scratch=[
             pltpu.VMEM((ns * high, LANES), F32),
             pltpu.VMEM((n_rows, 2 * cols), F32),
@@ -380,6 +380,14 @@
         token_ref[...] = jnp.zeros_like(token_ref)
 
     return call("pair_sum", body, (shape(terms[0].shape, F32), shape(TOKEN, F32)), *terms)
+
+
+def round_sums(pieces, nx, scale):
+    def body(in_ref, out_ref):
+        for n in range(nx):
+            out_ref[n] = ((in_ref[n] + in_ref[nx + n]) * scale).astype(BF16)
+
+    return call("round_sums", body, shape((nx, *pieces.shape[1:]), BF16), pieces)
 
 
 def score_rows(queries, order, store_rows, plan, scores, after):
@@ -460,20 +468,21 @@
     tokens.append(token)
     p_got = send(p_late, 0, 1)
 
-    total, token = pair_sum([part] + [send(part, o, 0) for o in z_offs[1:]])
-    token, q_late = lax.optimization_barrier((token, queries))
-    tokens.append(token)
-    q_near = send(q_late, 0, 1)
-    total = total + send(total, 1, 0)
-    g_own = (total * (1.0 / math.sqrt(toks * nt))).astype(BF16)
-    g_all = [g_own] + [send(g_own, 0, o) for o in range(1, ns)]
+    total, _ = pair_sum([part] + [send(part, o, 0) for o in z_offs[1:]])
+    groups = [
+        [(i + y) * ns + 2 * j + c for y in (0, 1) for j in range(nx)] for i in range(0, nt, 2) for c in (0, 1)
+    ]
+    sums = jnp.broadcast_to(total, (2 * nx, *total.shape))
+    sums = lax.all_to_all(sums, AXES, split_axis=0, concat_axis=0, tiled=True, axis_index_groups=groups)
+    g_own = round_sums(sums, nx, 1.0 / math.sqrt(toks * nt))
+    g_all = [g_own, send(g_own, 0, 1)]
 
     pieces, token = finish(nt, nx, g_all, precond, p_got, q_x, docs)
     groups = [[i * ns + 2 * j + c for i in range(nt) for j in range(nx)] for c in (0, 1)]
     pieces = lax.all_to_all(pieces, AXES, split_axis=0, concat_axis=0, tiled=True, axis_index_groups=groups)
-    token, *q_late = lax.optimization_barrier((token, *q_x[1:]))
+    token, *q_late = lax.optimization_barrier((token, *q_x))
     tokens.append(token)
-    q_far = [send(q, 0, 1) for q in q_late]
+    q_near, *q_far = [send(q, 0, 1) for q in q_late]
     q_all = [q for pair in zip(q_x, [q_near, *q_far]) for q in pair]
     scores, token = score_rows(q_all, range(ns), store_rows, plan, None, tokens)
     precond_docs, doc_scores = assemble(pieces, nt, docs, queries.shape[0], 2 * precond.shape[0], [token])

time: 59.4 us -> 60.8 us (1.024)
  blocking collectives: 0 us -> 7.72 us
  waiting for transfers between devices: 21.6 us -> 17 us
  starting transfers between devices: 28.4 us -> 26.1 us
  Pallas kernels: 7.55 us -> 8.16 us
    all_to_all x0 -> x1, blocking collectives: none -> 7.72 us  [tiled(): lax.all_to_all(sums, AXES, split_axis=0, concat_axis=0, tiled=True, axis_...]
    ppermute x23 -> x20, waiting for transfers between devices: 17.2 us -> 12.6 us  [send(): return lax.ppermute(value, AXES, perm)]
    ppermute x23 -> x20, starting transfers between devices: 24.8 us -> 22.2 us  [send(): return lax.ppermute(value, AXES, perm)]
    pallas_call x8 -> x9, Pallas kernels: 7.55 us -> 8.16 us  [call(): pl.pallas_call(run, name=name, out_shape=out, in_specs=specs + [pl.BlockS...]
  transfers between devices with their start and end apart: 24 -> 21, of which waited for: 12 -> 10; matrix products, arithmetic and copies ran while one was open for 1% -> 1% of each run, Pallas kernels for 10% -> 8%
where the time goes in v7:
time: 60.8 us; the launch traced here: 60.6 us
  starting transfers between devices  26.1 us (43%)
  waiting for transfers between devices  17 us (28%)
  Pallas kernels  8.16 us (13%)
  blocking collectives  7.72 us (13%)
  between operations  0.83 us (1%)
  local copies, waits for them, and re-layouts  0.78 us (1%)
    ppermute x20, starting transfers between devices, send(): return lax.ppermute(value, AXES, perm)  22.2 us
    ppermute x20, waiting for transfers between devices, send(): return lax.ppermute(value, AXES, perm)  12.6 us
    pallas_call x9, Pallas kernels, call(): pl.pallas_call(run, name=name, out_shape=out, in_specs=specs + [pl.BlockS...  8.16 us
    all_to_all x1, blocking collectives, tiled(): lax.all_to_all(sums, AXES, split_axis=0, concat_axis=0, tiled=True, axis_...  7.72 us
    all_to_all x1, waiting for transfers between devices, tiled(): lax.all_to_all(pieces, AXES, split_axis=0, concat_axis=0, tiled=True, axi...  4.34 us
    all_to_all x1, starting transfers between devices, tiled(): lax.all_to_all(pieces, AXES, split_axis=0, concat_axis=0, tiled=True, axi...  3.88 us
  transfers between devices with their start and end apart: 21, of which 10 were waited for; matrix products, arithmetic and copies ran while one was open for 1% of the time, Pallas kernels for 8%

profile of v7, /device:TPU:0, one launch (start us, length us, event | category | flops | bytes accessed | tf_op | source)
XLA Modules:
  0.0 60.6 jit_solution(9822139371425183864)
XLA Ops:
  0.7 0.5 collective-permute-start
  1.3 0.7 %dynamic-slice_bitcast_fusion.1 = bf16[32,256]{1,0:T(8,128)(2,1)S(1)} fusion(bf16[512,64]{0,1:T(8,128)(2,1)} %param.13, s32[]{:T(128)S(6)} %select_n.25, s32[]{:T(128)S(6)} %select_n.24), kind=kLoop, calls=%fused_computation.2 | loop fusion | bytes 32776 | tf_op jit(solution)/shard_map/dynamic_slice | solution.py:171
  2.0 3.1 %collective-permute-start.2 = (bf16[32,1152]{1,0:T(8,128)(2,1)S(1)}, bf16[32,1152]{1,0:T(8,128)(2,1)S(1)}, u32[]{:S(2)}, u32[]{:S(2)}) collective-permute-start(bf16[32,1152]{1,0:T(8,128)(2,1)S(1)} %pad_maximum_fusion.refs_0_), channel_id=1, source_target_pairs={{0,8},{1,9},{2,10},{3,11},{4,12},{5,13},{6,14},{7,15},{8,0},{9,1},... | collective-permute-start | bytes 221192 | tf_op jit(solution)/shard_map/ppermute | solution.py:447
  5.1 2.6 %collective-permute-start.3 = (bf16[32,1152]{1,0:T(8,128)(2,1)S(1)}, bf16[32,1152]{1,0:T(8,128)(2,1)S(1)}, u32[]{:S(2)}, u32[]{:S(2)}) collective-permute-start(bf16[32,1152]{1,0:T(8,128)(2,1)S(1)} %pad_maximum_fusion.refs_0_), channel_id=1, source_target_pairs={{0,16},{1,17},{2,18},{3,19},{4,20},{5,21},{6,22},{7,23},{8,24},{9,... | collective-permute-start | bytes 221192 | tf_op jit(solution)/shard_map/ppermute | solution.py:447
  7.7 2.7 %collective-permute-start.5 = (bf16[32,1152]{1,0:T(8,128)(2,1)S(1)}, bf16[32,1152]{1,0:T(8,128)(2,1)S(1)}, u32[]{:S(2)}, u32[]{:S(2)}) collective-permute-start(bf16[32,1152]{1,0:T(8,128)(2,1)S(1)} %pad_maximum_fusion.refs_0_), channel_id=1, source_target_pairs={{0,6},{1,7},{2,4},{3,5},{4,2},{5,3},{6,0},{7,1},{8,14},{9,15},{10,... | collective-permute-start | bytes 221192 | tf_op jit(solution)/shard_map/ppermute | solution.py:447
  10.3 2.8 %collective-permute-done.3.refs_2_ = bf16[32,1152]{1,0:T(8,128)(2,1)S(1)} collective-permute-done((bf16[32,1152]{1,0:T(8,128)(2,1)S(1)}, bf16[32,1152]{1,0:T(8,128)(2,1)S(1)}, u32[]{:S(2)}, u32[]{:S(2)}) %collective-permute-start.3) | collective-permute-done | bytes 73760 | tf_op jit(solution)/shard_map/ppermute | solution.py:447
  13.1 0.8 %collective-permute-done.4.refs_3_ = bf16[32,1152]{1,0:T(8,128)(2,1)S(1)} collective-permute-done((bf16[32,1152]{1,0:T(8,128)(2,1)S(1)}, bf16[32,1152]{1,0:T(8,128)(2,1)S(1)}, u32[]{:S(2)}, u32[]{:S(2)}) %collective-permute-start.4) | collective-permute-done | bytes 73760 | tf_op jit(solution)/shard_map/ppermute | solution.py:447
  14.0 1.6 %collective-permute-start.6 = (bf16[4,32,1152]{2,1,0:T(8,128)(2,1)S(1)}, bf16[4,32,1152]{2,1,0:T(8,128)(2,1)S(1)}, u32[]{:S(2)}, u32[]{:S(2)}) collective-permute-start(bf16[4,32,1152]{2,1,0:T(8,128)(2,1)S(1)} %stack.1.refs_4_), channel_id=1, source_target_pairs={{0,2},{1,3},{2,0},{3,1},{4,6},{5,7},{6,4},{7,5},{8,10},{9,11},{10,... | collective-permute-start | bytes 884744 | tf_op jit(solution)/shard_map/ppermute | solution.py:447
  15.5 1.5 %collective-permute-start.7 = (bf16[4,32,1152]{2,1,0:T(8,128)(2,1)S(1)}, bf16[4,32,1152]{2,1,0:T(8,128)(2,1)S(1)}, u32[]{:S(2)}, u32[]{:S(2)}) collective-permute-start(bf16[4,32,1152]{2,1,0:T(8,128)(2,1)S(1)} %stack.1.refs_4_), channel_id=1, source_target_pairs={{0,4},{1,5},{2,6},{3,7},{4,0},{5,1},{6,2},{7,3},{8,12},{9,13},{10,... | collective-permute-start | bytes 884744 | tf_op jit(solution)/shard_map/ppermute | solution.py:447
  17.0 3.6 %collective-permute-start.10 = (bf16[32,1152]{1,0:T(8,128)(2,1)S(1)}, bf16[32,1152]{1,0:T(8,128)(2,1)S(1)}, u32[]{:S(2)}, u32[]{:S(2)}) collective-permute-start(bf16[32,1152]{1,0:T(8,128)(2,1)S(1)} %collective-permute-done.5.refs_6_.refs_4_), channel_id=1, source_target_pairs={{0,24},{1,25},{2,26},{3,27},{4,28},{5,29},{6,30},{7,31},{8,16},{9,... | collective-permute-start | bytes 221192 | tf_op jit(solution)/shard_map/ppermute | solution.py:447
  20.6 0.8 %collective-permute-start.9 = (bf16[32,1152]{1,0:T(8,128)(2,1)S(1)}, bf16[32,1152]{1,0:T(8,128)(2,1)S(1)}, u32[]{:S(2)}, u32[]{:S(2)}) collective-permute-start(bf16[32,1152]{1,0:T(8,128)(2,1)S(1)} %collective-permute-done.5.refs_6_.refs_4_), channel_id=1, source_target_pairs={{0,16},{1,17},{2,18},{3,19},{4,20},{5,21},{6,22},{7,23},{8,24},{9,... | collective-permute-start | bytes 221192 | tf_op jit(solution)/shard_map/ppermute | solution.py:447
  21.4 1.3 %project_near.1 = (f32[128,64]{1,0:T(8,128)S(1)}, f32[64,128]{1,0:T(8,128)S(1)}, bf16[4,128,1152]{2,1,0:T(8,128)(2,1)S(1)}) custom-call(bf16[64,14336]{1,0:T(8,128)(2,1)S(1)} %bitcast.9, bf16[64,4096]{1,0:T(8,128)(2,1)S(1)} %bitcast.11, bf16[64,14336]{1,0:T(8,128)(2,1)S(1)} %collective-permute-done.refs_4_.refs_2_, ...), custom_call_target="tpu_custom_call" | custom-call | bytes 5308416 | tf_op jit(solution)/shard_map/project_near/pallas_call | solution.py:150
  22.8 0.9 %collective-permute-done.10.refs_7_ = bf16[32,1152]{1,0:T(8,128)(2,1)S(1)} collective-permute-done((bf16[32,1152]{1,0:T(8,128)(2,1)S(1)}, bf16[32,1152]{1,0:T(8,128)(2,1)S(1)}, u32[]{:S(2)}, u32[]{:S(2)}) %collective-permute-start.10) | collective-permute-done | bytes 73760 | tf_op jit(solution)/shard_map/ppermute | solution.py:447
  23.8 1.2 %collective-permute-done.8.refs_5_ = bf16[32,1152]{1,0:T(8,128)(2,1)S(1)} collective-permute-done((bf16[32,1152]{1,0:T(8,128)(2,1)S(1)}, bf16[32,1152]{1,0:T(8,128)(2,1)S(1)}, u32[]{:S(2)}, u32[]{:S(2)}) %collective-permute-start.8) | collective-permute-done | bytes 73760 | tf_op jit(solution)/shard_map/ppermute | solution.py:447
  25.0 0.9 %collective-permute-done.9.refs_6_ = bf16[32,1152]{1,0:T(8,128)(2,1)S(1)} collective-permute-done((bf16[32,1152]{1,0:T(8,128)(2,1)S(1)}, bf16[32,1152]{1,0:T(8,128)(2,1)S(1)}, u32[]{:S(2)}, u32[]{:S(2)}) %collective-permute-start.9) | collective-permute-done | bytes 73760 | tf_op jit(solution)/shard_map/ppermute | solution.py:447
  25.9 0.6 project_rest.1
  26.5 1.2 %collective-permute-done.11.refs_1_ = f32[64,128]{1,0:T(8,128)S(1)} collective-permute-done((f32[64,128]{1,0:T(8,128)S(1)}, f32[64,128]{1,0:T(8,128)S(1)}, u32[]{:S(2)}, u32[]{:S(2)}) %collective-permute-start.11) | collective-permute-done | bytes 32800 | tf_op jit(solution)/shard_map/ppermute | solution.py:447
  27.7 0.3 outer.1
  28.3 0.5 collective-permute-start.17
  28.8 2.0 %collective-permute-start.12 = (f32[64,128]{1,0:T(8,128)S(1)}, f32[64,128]{1,0:T(8,128)S(1)}, u32[]{:S(2)}, u32[]{:S(2)}) collective-permute-start(f32[64,128]{1,0:T(8,128)S(1)} %get-tuple-element.30.refs_0_), channel_id=1, source_target_pairs={{0,8},{1,9},{2,10},{3,11},{4,12},{5,13},{6,14},{7,15},{8,0},{9,1},... | collective-permute-start | bytes 98312 | tf_op jit(solution)/shard_map/ppermute | solution.py:447
  31.0 2.1 %collective-permute-start.14 = (f32[64,128]{1,0:T(8,128)S(1)}, f32[64,128]{1,0:T(8,128)S(1)}, u32[]{:S(2)}, u32[]{:S(2)}) collective-permute-start(f32[64,128]{1,0:T(8,128)S(1)} %get-tuple-element.30.refs_0_), channel_id=1, source_target_pairs={{0,24},{1,25},{2,26},{3,27},{4,28},{5,29},{6,30},{7,31},{8,16},{9,... | collective-permute-start | bytes 98312 | tf_op jit(solution)/shard_map/ppermute | solution.py:447
  33.2 2.7 %collective-permute-done.13.refs_2_ = f32[64,128]{1,0:T(8,128)S(1)} collective-permute-done((f32[64,128]{1,0:T(8,128)S(1)}, f32[64,128]{1,0:T(8,128)S(1)}, u32[]{:S(2)}, u32[]{:S(2)}) %collective-permute-start.13) | collective-permute-done | bytes 32800 | tf_op jit(solution)/shard_map/ppermute | solution.py:447
  35.9 0.8 %collective-permute-done.14.refs_3_ = f32[64,128]{1,0:T(8,128)S(1)} collective-permute-done((f32[64,128]{1,0:T(8,128)S(1)}, f32[64,128]{1,0:T(8,128)S(1)}, u32[]{:S(2)}, u32[]{:S(2)}) %collective-permute-start.14) | collective-permute-done | bytes 32800 | tf_op jit(solution)/shard_map/ppermute | solution.py:447
  36.7 0.6 pair_sum.1
  37.4 7.7 %all_to_all.10.refs_0_ = f32[4,64,128]{2,1,0:T(8,128)S(1)} all-to-all(f32[4,64,128]{2,1,0:T(8,128)S(1)} %broadcast_in_dim.3), channel_id=1, replica_groups={{0,2,4,6},{1,3,5,7},{8,10,12,14},{9,11,13,15},{16,18,20,22},{17,19,21,2..., dimensions={0} | all-to-all | bytes 262144 | tf_op jit(solution)/shard_map/all_to_all | solution.py:476
  45.2 1.2 %collective-permute-done.15.refs_1_ = bf16[2,64,128]{2,1,0:T(8,128)(2,1)S(1)} collective-permute-done((bf16[2,64,128]{2,1,0:T(8,128)(2,1)S(1)}, bf16[2,64,128]{2,1,0:T(8,128)(2,1)S(1)}, u32[]{:S(2)}, u32[]{:S(2)}) %collective-permute-start.15) | collective-permute-done | bytes 32800 | tf_op jit(solution)/shard_map/ppermute | solution.py:447
  46.4 1.5 %finish.1 = (f32[16,8,128]{2,1,0:T(8,128)}, f32[8,128]{1,0:T(8,128)S(1)}) custom-call(bf16[2,64,128]{2,1,0:T(8,128)(2,1)S(1)} %round_sums.1.refs_0_, bf16[2,64,128]{2,1,0:T(8,128)(2,1)S(1)} %collective-permute-done.15.refs_1_, bf16[128,4096]{1,0:T(8,128)(2,1)S(1)} %copy-done.4, bf16[128,4096]{1,0:T(8,128)(2,1)S(1)} %collective-permute-done.16.refs_3_, ...), custom_call_target="tpu_custom_call" | custom-call | bytes 3211264 | tf_op jit(solution)/shard_map/finish/pallas_call | solution.py:150
  48.1 0.4 collective-permute-start.19
  48.5 3.9 %all-to-all-start.1 = ((f32[16,8,128]{2,1,0:T(8,128)}), f32[16,8,128]{2,1,0:T(8,128)S(1)}, u32[]{:S(2)}, u32[]{:S(2)}) async-start(f32[16,8,128]{2,1,0:T(8,128)} %get-tuple-element.43), calls=%async_computation.1 | async-start | bytes 131072 | tf_op jit(solution)/shard_map/all_to_all | solution.py:482
  52.4 3.1 %score_rows.1 = (f32[256,128]{1,0:T(8,128)}, f32[8,128]{1,0:T(8,128)S(1)}) custom-call(bf16[64,4096]{1,0:T(8,128)(2,1)S(1)} %copy-done.1, bf16[64,4096]{1,0:T(8,128)(2,1)} %collective-permute-done.18.refs_1_, bf16[64,4096]{1,0:T(8,128)(2,1)S(1)} %collective-permute-done.17.refs_5_.refs_2_, bf16[64,4096]{1,0:T(8,128)(2,1)} %collective-permute-done.19.refs_3_, ...), custom_call_target="tpu_custom_call" | custom-call | bytes 4194320 | tf_op jit(solution)/shard_map/score_rows/pallas_call | solution.py:150
  55.5 4.3 %all-to-all-done.1.refs_0_ = f32[16,8,128]{2,1,0:T(8,128)S(1)} async-done(((f32[16,8,128]{2,1,0:T(8,128)}), f32[16,8,128]{2,1,0:T(8,128)S(1)}, u32[]{:S(2)}, u32[]{:S(2)}) %all-to-all-start.1) | async-done | bytes 65568 | tf_op jit(solution)/shard_map/all_to_all | solution.py:482
  59.9 0.7 %assemble.1 = (f32[2,512]{1,0:T(2,128)}, f32[8,64]{1,0:T(8,128)}) custom-call(f32[16,8,128]{2,1,0:T(8,128)S(1)} %all-to-all-done.1.refs_0_, f32[8,128]{1,0:T(8,128)S(1)} %get-tuple-element.44.refs_1_), custom_call_target="tpu_custom_call" | custom-call | bytes 65536 | tf_op jit(solution)/shard_map/assemble/pallas_call | solution.py:150
  (40 shorter events, 1.0 us)
Async XLA Ops:
  0.6 1.3 %copy-start = (bf16[1792,64]{0,1:T(8,128)(2,1)S(1)}, bf16[1792,64]{0,1:T(8,128)(2,1)}, u32[]{:S(2)}) copy-start(bf16[1792,64]{0,1:T(8,128)(2,1)} %param.12) | copy-start | bytes 688132
  0.6 20.8 %copy-start.5 = (bf16[2,32,4096]{2,1,0:T(8,128)(2,1)S(1)}, bf16[2,32,4096]{2,1,0:T(8,128)(2,1)}, u32[]{:S(2)}) copy-start(bf16[2,32,4096]{2,1,0:T(8,128)(2,1)} %param.10) | copy-start | bytes 1572868
  0.7 13.3 %collective-permute-start = (bf16[64,14336]{1,0:T(8,128)(2,1)}, bf16[64,14336]{1,0:T(8,128)(2,1)S(1)}, u32[]{:S(2)}, u32[]{:S(2)}) collective-permute-start(bf16[64,14336]{1,0:T(8,128)(2,1)} %bitcast.8), channel_id=1, source_target_pairs={{0,1},{1,0},{2,3},{3,2},{4,5},{5,4},{6,7},{7,6},{8,9},{9,8},{10,11... | collective-permute-start | bytes 5505032 | tf_op jit(solution)/shard_map/ppermute | solution.py:447
  1.2 12.7 %collective-permute-start.1 = (bf16[64,4096]{1,0:T(8,128)(2,1)}, bf16[64,4096]{1,0:T(8,128)(2,1)S(1)}, u32[]{:S(2)}, u32[]{:S(2)}) collective-permute-start(bf16[64,4096]{1,0:T(8,128)(2,1)} %bitcast.10), channel_id=1, source_target_pairs={{0,1},{1,0},{2,3},{3,2},{4,5},{5,4},{6,7},{7,6},{8,9},{9,8},{10,11... | collective-permute-start | bytes 1572872 | tf_op jit(solution)/shard_map/ppermute | solution.py:447
  2.0 19.5 %copy-start.3 = (bf16[2,32,14336]{2,1,0:T(8,128)(2,1)S(1)}, bf16[2,32,14336]{2,1,0:T(8,128)(2,1)}, u32[]{:S(2)}) copy-start(bf16[2,32,14336]{2,1,0:T(8,128)(2,1)} %param.9) | copy-start | bytes 5505028
  2.0 5.7 %collective-permute-start.2 = (bf16[32,1152]{1,0:T(8,128)(2,1)S(1)}, bf16[32,1152]{1,0:T(8,128)(2,1)S(1)}, u32[]{:S(2)}, u32[]{:S(2)}) collective-permute-start(bf16[32,1152]{1,0:T(8,128)(2,1)S(1)} %pad_maximum_fusion.refs_0_), channel_id=1, source_target_pairs={{0,8},{1,9},{2,10},{3,11},{4,12},{5,13},{6,14},{7,15},{8,0},{9,1},... | collective-permute-start | bytes 221192 | tf_op jit(solution)/shard_map/ppermute | solution.py:447
  5.1 8.0 %collective-permute-start.3 = (bf16[32,1152]{1,0:T(8,128)(2,1)S(1)}, bf16[32,1152]{1,0:T(8,128)(2,1)S(1)}, u32[]{:S(2)}, u32[]{:S(2)}) collective-permute-start(bf16[32,1152]{1,0:T(8,128)(2,1)S(1)} %pad_maximum_fusion.refs_0_), channel_id=1, source_target_pairs={{0,16},{1,17},{2,18},{3,19},{4,20},{5,21},{6,22},{7,23},{8,24},{9,... | collective-permute-start | bytes 221192 | tf_op jit(solution)/shard_map/ppermute | solution.py:447
  7.7 6.3 %collective-permute-start.4 = (bf16[32,1152]{1,0:T(8,128)(2,1)S(1)}, bf16[32,1152]{1,0:T(8,128)(2,1)S(1)}, u32[]{:S(2)}, u32[]{:S(2)}) collective-permute-start(bf16[32,1152]{1,0:T(8,128)(2,1)S(1)} %pad_maximum_fusion.refs_0_), channel_id=1, source_target_pairs={{0,24},{1,25},{2,26},{3,27},{4,28},{5,29},{6,30},{7,31},{8,16},{9,... | collective-permute-start | bytes 221192 | tf_op jit(solution)/shard_map/ppermute | solution.py:447
  7.7 6.3 %collective-permute-start.5 = (bf16[32,1152]{1,0:T(8,128)(2,1)S(1)}, bf16[32,1152]{1,0:T(8,128)(2,1)S(1)}, u32[]{:S(2)}, u32[]{:S(2)}) collective-permute-start(bf16[32,1152]{1,0:T(8,128)(2,1)S(1)} %pad_maximum_fusion.refs_0_), channel_id=1, source_target_pairs={{0,6},{1,7},{2,4},{3,5},{4,2},{5,3},{6,0},{7,1},{8,14},{9,15},{10,... | collective-permute-start | bytes 221192 | tf_op jit(solution)/shard_map/ppermute | solution.py:447
  14.0 7.5 %collective-permute-start.6 = (bf16[4,32,1152]{2,1,0:T(8,128)(2,1)S(1)}, bf16[4,32,1152]{2,1,0:T(8,128)(2,1)S(1)}, u32[]{:S(2)}, u32[]{:S(2)}) collective-permute-start(bf16[4,32,1152]{2,1,0:T(8,128)(2,1)S(1)} %stack.1.refs_4_), channel_id=1, source_target_pairs={{0,2},{1,3},{2,0},{3,1},{4,6},{5,7},{6,4},{7,5},{8,10},{9,11},{10,... | collective-permute-start | bytes 884744 | tf_op jit(solution)/shard_map/ppermute | solution.py:447
  15.5 10.3 %collective-permute-start.7 = (bf16[4,32,1152]{2,1,0:T(8,128)(2,1)S(1)}, bf16[4,32,1152]{2,1,0:T(8,128)(2,1)S(1)}, u32[]{:S(2)}, u32[]{:S(2)}) collective-permute-start(bf16[4,32,1152]{2,1,0:T(8,128)(2,1)S(1)} %stack.1.refs_4_), channel_id=1, source_target_pairs={{0,4},{1,5},{2,6},{3,7},{4,0},{5,1},{6,2},{7,3},{8,12},{9,13},{10,... | collective-permute-start | bytes 884744 | tf_op jit(solution)/shard_map/ppermute | solution.py:447
  17.0 6.7 %collective-permute-start.10 = (bf16[32,1152]{1,0:T(8,128)(2,1)S(1)}, bf16[32,1152]{1,0:T(8,128)(2,1)S(1)}, u32[]{:S(2)}, u32[]{:S(2)}) collective-permute-start(bf16[32,1152]{1,0:T(8,128)(2,1)S(1)} %collective-permute-done.5.refs_6_.refs_4_), channel_id=1, source_target_pairs={{0,24},{1,25},{2,26},{3,27},{4,28},{5,29},{6,30},{7,31},{8,16},{9,... | collective-permute-start | bytes 221192 | tf_op jit(solution)/shard_map/ppermute | solution.py:447
  20.6 4.4 %collective-permute-start.8 = (bf16[32,1152]{1,0:T(8,128)(2,1)S(1)}, bf16[32,1152]{1,0:T(8,128)(2,1)S(1)}, u32[]{:S(2)}, u32[]{:S(2)}) collective-permute-start(bf16[32,1152]{1,0:T(8,128)(2,1)S(1)} %collective-permute-done.5.refs_6_.refs_4_), channel_id=1, source_target_pairs={{0,8},{1,9},{2,10},{3,11},{4,12},{5,13},{6,14},{7,15},{8,0},{9,1},... | collective-permute-start | bytes 221192 | tf_op jit(solution)/shard_map/ppermute | solution.py:447
  20.6 5.3 %collective-permute-start.9 = (bf16[32,1152]{1,0:T(8,128)(2,1)S(1)}, bf16[32,1152]{1,0:T(8,128)(2,1)S(1)}, u32[]{:S(2)}, u32[]{:S(2)}) collective-permute-start(bf16[32,1152]{1,0:T(8,128)(2,1)S(1)} %collective-permute-done.5.refs_6_.refs_4_), channel_id=1, source_target_pairs={{0,16},{1,17},{2,18},{3,19},{4,20},{5,21},{6,22},{7,23},{8,24},{9,... | collective-permute-start | bytes 221192 | tf_op jit(solution)/shard_map/ppermute | solution.py:447
  22.8 5.0 %copy-start.6 = (s32[2,32]{1,0:T(2,128)S(1)}, s32[2,32]{1,0:T(2,128)}, u32[]{:S(2)}) copy-start(s32[2,32]{1,0:T(2,128)} %refs_2_.2) | copy-start | bytes 772
  22.8 5.3 %copy-start.4 = (bf16[128,4096]{1,0:T(8,128)(2,1)S(1)}, bf16[128,4096]{1,0:T(8,128)(2,1)}, u32[]{:S(2)}) copy-start(bf16[128,4096]{1,0:T(8,128)(2,1)} %refs_2_.3) | copy-start | bytes 3145732
  22.8 5.5 %copy-start.1 = (bf16[64,4096]{1,0:T(8,128)(2,1)S(1)}, bf16[64,4096]{1,0:T(8,128)(2,1)}, u32[]{:S(2)}) copy-start(bf16[64,4096]{1,0:T(8,128)(2,1)} %refs_0_.1) | copy-start | bytes 1572868
  26.5 1.3 %collective-permute-start.11 = (f32[64,128]{1,0:T(8,128)S(1)}, f32[64,128]{1,0:T(8,128)S(1)}, u32[]{:S(2)}, u32[]{:S(2)}) collective-permute-start(f32[64,128]{1,0:T(8,128)S(1)} %get-tuple-element.29), channel_id=1, source_target_pairs={{0,1},{1,0},{2,3},{3,2},{4,5},{5,4},{6,7},{7,6},{8,9},{9,8},{10,11... | collective-permute-start | bytes 98312 | tf_op jit(solution)/shard_map/ppermute | solution.py:447
  28.1 18.3 %collective-permute-start.16 = (bf16[128,4096]{1,0:T(8,128)(2,1)S(1)}, bf16[128,4096]{1,0:T(8,128)(2,1)S(1)}, u32[]{:S(2)}, u32[]{:S(2)}) collective-permute-start(bf16[128,4096]{1,0:T(8,128)(2,1)S(1)} %copy-done.4), channel_id=1, source_target_pairs={{0,1},{1,0},{2,3},{3,2},{4,5},{5,4},{6,7},{7,6},{8,9},{9,8},{10,11... | collective-permute-start | bytes 3145736 | tf_op jit(solution)/shard_map/ppermute | solution.py:447
  28.3 18.1 %collective-permute-start.17 = (bf16[64,4096]{1,0:T(8,128)(2,1)S(1)}, bf16[64,4096]{1,0:T(8,128)(2,1)S(1)}, u32[]{:S(2)}, u32[]{:S(2)}) collective-permute-start(bf16[64,4096]{1,0:T(8,128)(2,1)S(1)} %copy-done.1), channel_id=1, source_target_pairs={{0,2},{1,3},{2,0},{3,1},{4,6},{5,7},{6,4},{7,5},{8,10},{9,11},{10,... | collective-permute-start | bytes 1572872 | tf_op jit(solution)/shard_map/ppermute | solution.py:447
  28.8 4.4 %collective-permute-start.12 = (f32[64,128]{1,0:T(8,128)S(1)}, f32[64,128]{1,0:T(8,128)S(1)}, u32[]{:S(2)}, u32[]{:S(2)}) collective-permute-start(f32[64,128]{1,0:T(8,128)S(1)} %get-tuple-element.30.refs_0_), channel_id=1, source_target_pairs={{0,8},{1,9},{2,10},{3,11},{4,12},{5,13},{6,14},{7,15},{8,0},{9,1},... | collective-permute-start | bytes 98312 | tf_op jit(solution)/shard_map/ppermute | solution.py:447
  30.8 5.1 %collective-permute-start.13 = (f32[64,128]{1,0:T(8,128)S(1)}, f32[64,128]{1,0:T(8,128)S(1)}, u32[]{:S(2)}, u32[]{:S(2)}) collective-permute-start(f32[64,128]{1,0:T(8,128)S(1)} %get-tuple-element.30.refs_0_), channel_id=1, source_target_pairs={{0,16},{1,17},{2,18},{3,19},{4,20},{5,21},{6,22},{7,23},{8,24},{9,... | collective-permute-start | bytes 98312 | tf_op jit(solution)/shard_map/ppermute | solution.py:447
  31.0 5.7 %collective-permute-start.14 = (f32[64,128]{1,0:T(8,128)S(1)}, f32[64,128]{1,0:T(8,128)S(1)}, u32[]{:S(2)}, u32[]{:S(2)}) collective-permute-start(f32[64,128]{1,0:T(8,128)S(1)} %get-tuple-element.30.refs_0_), channel_id=1, source_target_pairs={{0,24},{1,25},{2,26},{3,27},{4,28},{5,29},{6,30},{7,31},{8,16},{9,... | collective-permute-start | bytes 98312 | tf_op jit(solution)/shard_map/ppermute | solution.py:447
  37.4 15.0 %copy-start.2 = (f32[128,4096]{1,0:T(8,128)S(1)}, f32[128,4096]{1,0:T(8,128)}, u32[]{:S(2)}) copy-start(f32[128,4096]{1,0:T(8,128)} %refs_4_.3) | copy-start | bytes 6291460
  37.4 15.0 %copy-start.7 = (s32[4,1]{0,1:T(1,128)S(1)}, s32[4,1]{0,1:T(1,128)}, u32[]{:S(2)}) copy-start(s32[4,1]{0,1:T(1,128)} %param.17) | copy-start | bytes 52
  45.1 1.3 %collective-permute-start.15 = (bf16[2,64,128]{2,1,0:T(8,128)(2,1)S(1)}, bf16[2,64,128]{2,1,0:T(8,128)(2,1)S(1)}, u32[]{:S(2)}, u32[]{:S(2)}) collective-permute-start(bf16[2,64,128]{2,1,0:T(8,128)(2,1)S(1)} %round_sums.1.refs_0_), channel_id=1, source_target_pairs={{0,1},{1,0},{2,3},{3,2},{4,5},{5,4},{6,7},{7,6},{8,9},{9,8},{10,11... | collective-permute-start | bytes 98312 | tf_op jit(solution)/shard_map/ppermute | solution.py:447
  47.9 4.5 %collective-permute-start.18 = (bf16[64,4096]{1,0:T(8,128)(2,1)S(1)}, bf16[64,4096]{1,0:T(8,128)(2,1)}, u32[]{:S(2)}, u32[]{:S(2)}) collective-permute-start(bf16[64,4096]{1,0:T(8,128)(2,1)S(1)} %copy-done.1), channel_id=1, source_target_pairs={{0,1},{1,0},{2,3},{3,2},{4,5},{5,4},{6,7},{7,6},{8,9},{9,8},{10,11... | collective-permute-start | bytes 1572872 | tf_op jit(solution)/shard_map/ppermute | solution.py:447
  48.1 4.3 %collective-permute-start.19 = (bf16[64,4096]{1,0:T(8,128)(2,1)S(1)}, bf16[64,4096]{1,0:T(8,128)(2,1)}, u32[]{:S(2)}, u32[]{:S(2)}) collective-permute-start(bf16[64,4096]{1,0:T(8,128)(2,1)S(1)} %collective-permute-done.17.refs_5_.refs_2_), channel_id=1, source_target_pairs={{0,1},{1,0},{2,3},{3,2},{4,5},{5,4},{6,7},{7,6},{8,9},{9,8},{10,11... | collective-permute-start | bytes 1572872 | tf_op jit(solution)/shard_map/ppermute | solution.py:447
  48.5 11.4 %all-to-all-start.1 = ((f32[16,8,128]{2,1,0:T(8,128)}), f32[16,8,128]{2,1,0:T(8,128)S(1)}, u32[]{:S(2)}, u32[]{:S(2)}) async-start(f32[16,8,128]{2,1,0:T(8,128)} %get-tuple-element.43), calls=%async_computation.1 | async-start | bytes 131072 | tf_op jit(solution)/shard_map/all_to_all | solution.py:482

commit v8 on v6

--- a/solution.py
+++ b/solution.py
@@ -460,10 +460,7 @@
     tokens.append(token)
     p_got = send(p_late, 0, 1)
 
-    total, token = pair_sum([part] + [send(part, o, 0) for o in z_offs[1:]])
-    token, q_late = lax.optimization_barrier((token, queries))
-    tokens.append(token)
-    q_near = send(q_late, 0, 1)
+    total, _ = pair_sum([part] + [send(part, o, 0) for o in z_offs[1:]])
     total = total + send(total, 1, 0)
     g_own = (total * (1.0 / math.sqrt(toks * nt))).astype(BF16)
     g_all = [g_own] + [send(g_own, 0, o) for o in range(1, ns)]
@@ -471,9 +468,9 @@
     pieces, token = finish(nt, nx, g_all, precond, p_got, q_x, docs)
     groups = [[i * ns + 2 * j + c for i in range(nt) for j in range(nx)] for c in (0, 1)]
     pieces = lax.all_to_all(pieces, AXES, split_axis=0, concat_axis=0, tiled=True, axis_index_groups=groups)
-    token, *q_late = lax.optimization_barrier((token, *q_x[1:]))
+    token, *q_late = lax.optimization_barrier((token, *q_x))
     tokens.append(token)
-    q_far = [send(q, 0, 1) for q in q_late]
+    q_near, *q_far = [send(q, 0, 1) for q in q_late]
     q_all = [q for pair in zip(q_x, [q_near, *q_far]) for q in pair]
     scores, token = score_rows(q_all, range(ns), store_rows, plan, None, tokens)
     precond_docs, doc_scores = assemble(pieces, nt, docs, queries.shape[0], 2 * precond.shape[0], [token])

time: 59.4 us -> 60.3 us (1.015)
  transfers between devices with their start and end apart: 24 -> 24, of which waited for: 12 -> 12; matrix products, arithmetic and copies ran while one was open for 1% -> 1% of each run, Pallas kernels for 10% -> 8%
where the time goes in v8:
time: 60.3 us; the launch traced here: 60.1 us
  starting transfers between devices  28.4 us (47%)
  waiting for transfers between devices  21.9 us (36%)
  Pallas kernels  8.15 us (14%)
  between operations  0.83 us (1%)
  local copies, waits for them, and re-layouts  0.77 us (1%)
    ppermute x23, starting transfers between devices, send(): return lax.ppermute(value, AXES, perm)  24.7 us
    ppermute x23, waiting for transfers between devices, send(): return lax.ppermute(value, AXES, perm)  17.6 us
    pallas_call x8, Pallas kernels, call(): pl.pallas_call(run, name=name, out_shape=out, in_specs=specs + [pl.BlockS...  8.15 us
    all_to_all x1, waiting for transfers between devices, tiled(): lax.all_to_all(pieces, AXES, split_axis=0, concat_axis=0, tiled=True, axi...  4.34 us
    all_to_all x1, starting transfers between devices, tiled(): lax.all_to_all(pieces, AXES, split_axis=0, concat_axis=0, tiled=True, axi...  3.7 us
  transfers between devices with their start and end apart: 24, of which 12 were waited for; matrix products, arithmetic and copies ran while one was open for 1% of the time, Pallas kernels for 8%

profile of v8, /device:TPU:0, one launch (start us, length us, event | category | flops | bytes accessed | tf_op | source)
XLA Modules:
  0.0 60.1 jit_solution(893047316784769354)
XLA Ops:
  1.3 0.7 %dynamic-slice_bitcast_fusion.1 = bf16[32,256]{1,0:T(8,128)(2,1)S(1)} fusion(bf16[512,64]{0,1:T(8,128)(2,1)} %param.13, s32[]{:T(128)S(6)} %select_n.25, s32[]{:T(128)S(6)} %select_n.24), kind=kLoop, calls=%fused_computation.3 | loop fusion | bytes 32776 | tf_op jit(solution)/shard_map/dynamic_slice | solution.py:171
  2.0 3.1 %collective-permute-start.2 = (bf16[32,1152]{1,0:T(8,128)(2,1)S(1)}, bf16[32,1152]{1,0:T(8,128)(2,1)S(1)}, u32[]{:S(2)}, u32[]{:S(2)}) collective-permute-start(bf16[32,1152]{1,0:T(8,128)(2,1)S(1)} %pad_maximum_fusion.refs_0_), channel_id=1, source_target_pairs={{0,8},{1,9},{2,10},{3,11},{4,12},{5,13},{6,14},{7,15},{8,0},{9,1},... | collective-permute-start | bytes 221192 | tf_op jit(solution)/shard_map/ppermute | solution.py:439
  5.1 2.6 %collective-permute-start.3 = (bf16[32,1152]{1,0:T(8,128)(2,1)S(1)}, bf16[32,1152]{1,0:T(8,128)(2,1)S(1)}, u32[]{:S(2)}, u32[]{:S(2)}) collective-permute-start(bf16[32,1152]{1,0:T(8,128)(2,1)S(1)} %pad_maximum_fusion.refs_0_), channel_id=1, source_target_pairs={{0,16},{1,17},{2,18},{3,19},{4,20},{5,21},{6,22},{7,23},{8,24},{9,... | collective-permute-start | bytes 221192 | tf_op jit(solution)/shard_map/ppermute | solution.py:439
  7.7 2.7 %collective-permute-start.5 = (bf16[32,1152]{1,0:T(8,128)(2,1)S(1)}, bf16[32,1152]{1,0:T(8,128)(2,1)S(1)}, u32[]{:S(2)}, u32[]{:S(2)}) collective-permute-start(bf16[32,1152]{1,0:T(8,128)(2,1)S(1)} %pad_maximum_fusion.refs_0_), channel_id=1, source_target_pairs={{0,6},{1,7},{2,4},{3,5},{4,2},{5,3},{6,0},{7,1},{8,14},{9,15},{10,... | collective-permute-start | bytes 221192 | tf_op jit(solution)/shard_map/ppermute | solution.py:439
  10.3 2.8 %collective-permute-done.3.refs_2_ = bf16[32,1152]{1,0:T(8,128)(2,1)S(1)} collective-permute-done((bf16[32,1152]{1,0:T(8,128)(2,1)S(1)}, bf16[32,1152]{1,0:T(8,128)(2,1)S(1)}, u32[]{:S(2)}, u32[]{:S(2)}) %collective-permute-start.3) | collective-permute-done | bytes 73760 | tf_op jit(solution)/shard_map/ppermute | solution.py:439
  13.1 0.8 %collective-permute-done.4.refs_3_ = bf16[32,1152]{1,0:T(8,128)(2,1)S(1)} collective-permute-done((bf16[32,1152]{1,0:T(8,128)(2,1)S(1)}, bf16[32,1152]{1,0:T(8,128)(2,1)S(1)}, u32[]{:S(2)}, u32[]{:S(2)}) %collective-permute-start.4) | collective-permute-done | bytes 73760 | tf_op jit(solution)/shard_map/ppermute | solution.py:439
  14.0 1.6 %collective-permute-start.6 = (bf16[4,32,1152]{2,1,0:T(8,128)(2,1)S(1)}, bf16[4,32,1152]{2,1,0:T(8,128)(2,1)S(1)}, u32[]{:S(2)}, u32[]{:S(2)}) collective-permute-start(bf16[4,32,1152]{2,1,0:T(8,128)(2,1)S(1)} %stack.1.refs_4_), channel_id=1, source_target_pairs={{0,2},{1,3},{2,0},{3,1},{4,6},{5,7},{6,4},{7,5},{8,10},{9,11},{10,... | collective-permute-start | bytes 884744 | tf_op jit(solution)/shard_map/ppermute | solution.py:439
  15.5 1.5 %collective-permute-start.7 = (bf16[4,32,1152]{2,1,0:T(8,128)(2,1)S(1)}, bf16[4,32,1152]{2,1,0:T(8,128)(2,1)S(1)}, u32[]{:S(2)}, u32[]{:S(2)}) collective-permute-start(bf16[4,32,1152]{2,1,0:T(8,128)(2,1)S(1)} %stack.1.refs_4_), channel_id=1, source_target_pairs={{0,4},{1,5},{2,6},{3,7},{4,0},{5,1},{6,2},{7,3},{8,12},{9,13},{10,... | collective-permute-start | bytes 884744 | tf_op jit(solution)/shard_map/ppermute | solution.py:439
  17.0 3.6 %collective-permute-start.10 = (bf16[32,1152]{1,0:T(8,128)(2,1)S(1)}, bf16[32,1152]{1,0:T(8,128)(2,1)S(1)}, u32[]{:S(2)}, u32[]{:S(2)}) collective-permute-start(bf16[32,1152]{1,0:T(8,128)(2,1)S(1)} %collective-permute-done.5.refs_6_.refs_4_), channel_id=1, source_target_pairs={{0,24},{1,25},{2,26},{3,27},{4,28},{5,29},{6,30},{7,31},{8,16},{9,... | collective-permute-start | bytes 221192 | tf_op jit(solution)/shard_map/ppermute | solution.py:439
  20.6 0.8 %collective-permute-start.9 = (bf16[32,1152]{1,0:T(8,128)(2,1)S(1)}, bf16[32,1152]{1,0:T(8,128)(2,1)S(1)}, u32[]{:S(2)}, u32[]{:S(2)}) collective-permute-start(bf16[32,1152]{1,0:T(8,128)(2,1)S(1)} %collective-permute-done.5.refs_6_.refs_4_), channel_id=1, source_target_pairs={{0,16},{1,17},{2,18},{3,19},{4,20},{5,21},{6,22},{7,23},{8,24},{9,... | collective-permute-start | bytes 221192 | tf_op jit(solution)/shard_map/ppermute | solution.py:439
  21.4 1.3 %project_near.1 = (f32[128,64]{1,0:T(8,128)S(1)}, f32[64,128]{1,0:T(8,128)S(1)}, bf16[4,128,1152]{2,1,0:T(8,128)(2,1)S(1)}) custom-call(bf16[64,14336]{1,0:T(8,128)(2,1)S(1)} %bitcast.9, bf16[64,4096]{1,0:T(8,128)(2,1)S(1)} %bitcast.11, bf16[64,14336]{1,0:T(8,128)(2,1)S(1)} %collective-permute-done.refs_4_.refs_2_, ...), custom_call_target="tpu_custom_call" | custom-call | bytes 5308416 | tf_op jit(solution)/shard_map/project_near/pallas_call | solution.py:150
  22.8 0.9 %collective-permute-done.10.refs_7_ = bf16[32,1152]{1,0:T(8,128)(2,1)S(1)} collective-permute-done((bf16[32,1152]{1,0:T(8,128)(2,1)S(1)}, bf16[32,1152]{1,0:T(8,128)(2,1)S(1)}, u32[]{:S(2)}, u32[]{:S(2)}) %collective-permute-start.10) | collective-permute-done | bytes 73760 | tf_op jit(solution)/shard_map/ppermute | solution.py:439
  23.8 1.2 %collective-permute-done.8.refs_5_ = bf16[32,1152]{1,0:T(8,128)(2,1)S(1)} collective-permute-done((bf16[32,1152]{1,0:T(8,128)(2,1)S(1)}, bf16[32,1152]{1,0:T(8,128)(2,1)S(1)}, u32[]{:S(2)}, u32[]{:S(2)}) %collective-permute-start.8) | collective-permute-done | bytes 73760 | tf_op jit(solution)/shard_map/ppermute | solution.py:439
  25.0 0.9 %collective-permute-done.9.refs_6_ = bf16[32,1152]{1,0:T(8,128)(2,1)S(1)} collective-permute-done((bf16[32,1152]{1,0:T(8,128)(2,1)S(1)}, bf16[32,1152]{1,0:T(8,128)(2,1)S(1)}, u32[]{:S(2)}, u32[]{:S(2)}) %collective-permute-start.9) | collective-permute-done | bytes 73760 | tf_op jit(solution)/shard_map/ppermute | solution.py:439
  25.9 0.6 project_rest.1
  26.6 1.2 %collective-permute-done.11.refs_1_ = f32[64,128]{1,0:T(8,128)S(1)} collective-permute-done((f32[64,128]{1,0:T(8,128)S(1)}, f32[64,128]{1,0:T(8,128)S(1)}, u32[]{:S(2)}, u32[]{:S(2)}) %collective-permute-start.11) | collective-permute-done | bytes 32800 | tf_op jit(solution)/shard_map/ppermute | solution.py:439
  28.3 0.5 collective-permute-start.20
  28.8 2.0 %collective-permute-start.12 = (f32[64,128]{1,0:T(8,128)S(1)}, f32[64,128]{1,0:T(8,128)S(1)}, u32[]{:S(2)}, u32[]{:S(2)}) collective-permute-start(f32[64,128]{1,0:T(8,128)S(1)} %get-tuple-element.30.refs_0_), channel_id=1, source_target_pairs={{0,8},{1,9},{2,10},{3,11},{4,12},{5,13},{6,14},{7,15},{8,0},{9,1},... | collective-permute-start | bytes 98312 | tf_op jit(solution)/shard_map/ppermute | solution.py:439
  31.0 2.1 %collective-permute-start.14 = (f32[64,128]{1,0:T(8,128)S(1)}, f32[64,128]{1,0:T(8,128)S(1)}, u32[]{:S(2)}, u32[]{:S(2)}) collective-permute-start(f32[64,128]{1,0:T(8,128)S(1)} %get-tuple-element.30.refs_0_), channel_id=1, source_target_pairs={{0,24},{1,25},{2,26},{3,27},{4,28},{5,29},{6,30},{7,31},{8,16},{9,... | collective-permute-start | bytes 98312 | tf_op jit(solution)/shard_map/ppermute | solution.py:439
  33.2 2.7 %collective-permute-done.13.refs_2_ = f32[64,128]{1,0:T(8,128)S(1)} collective-permute-done((f32[64,128]{1,0:T(8,128)S(1)}, f32[64,128]{1,0:T(8,128)S(1)}, u32[]{:S(2)}, u32[]{:S(2)}) %collective-permute-start.13) | collective-permute-done | bytes 32800 | tf_op jit(solution)/shard_map/ppermute | solution.py:439
  35.9 0.8 %collective-permute-done.14.refs_3_ = f32[64,128]{1,0:T(8,128)S(1)} collective-permute-done((f32[64,128]{1,0:T(8,128)S(1)}, f32[64,128]{1,0:T(8,128)S(1)}, u32[]{:S(2)}, u32[]{:S(2)}) %collective-permute-start.14) | collective-permute-done | bytes 32800 | tf_op jit(solution)/shard_map/ppermute | solution.py:439
  36.8 0.6 pair_sum.1
  37.4 0.6 %collective-permute-start.15 = (f32[64,128]{1,0:T(8,128)S(1)}, f32[64,128]{1,0:T(8,128)S(1)}, u32[]{:S(2)}, u32[]{:S(2)}) collective-permute-start(f32[64,128]{1,0:T(8,128)S(1)} %get-tuple-element.31), channel_id=1, source_target_pairs={{0,4},{1,5},{2,6},{3,7},{4,0},{5,1},{6,2},{7,3},{8,12},{9,13},{10,... | collective-permute-start | bytes 98312 | tf_op jit(solution)/shard_map/ppermute | solution.py:439
  38.0 3.3 %collective-permute-done.15 = f32[64,128]{1,0:T(8,128)S(1)} collective-permute-done((f32[64,128]{1,0:T(8,128)S(1)}, f32[64,128]{1,0:T(8,128)S(1)}, u32[]{:S(2)}, u32[]{:S(2)}) %collective-permute-start.15) | collective-permute-done | bytes 32800 | tf_op jit(solution)/shard_map/ppermute | solution.py:439
  41.4 1.6 %collective-permute-start.17 = (bf16[64,128]{1,0:T(8,128)(2,1)S(1)}, bf16[64,128]{1,0:T(8,128)(2,1)S(1)}, u32[]{:S(2)}, u32[]{:S(2)}) collective-permute-start(bf16[64,128]{1,0:T(8,128)(2,1)S(1)} %multiply_convert_fusion.refs_0_), channel_id=1, source_target_pairs={{0,2},{1,3},{2,0},{3,1},{4,6},{5,7},{6,4},{7,5},{8,10},{9,11},{10,... | collective-permute-start | bytes 49160 | tf_op jit(solution)/shard_map/ppermute | solution.py:439
  43.2 1.9 %collective-permute-done.17.refs_2_ = bf16[64,128]{1,0:T(8,128)(2,1)S(1)} collective-permute-done((bf16[64,128]{1,0:T(8,128)(2,1)S(1)}, bf16[64,128]{1,0:T(8,128)(2,1)S(1)}, u32[]{:S(2)}, u32[]{:S(2)}) %collective-permute-start.17) | collective-permute-done | bytes 16416 | tf_op jit(solution)/shard_map/ppermute | solution.py:439
  45.2 0.9 %collective-permute-done.18.refs_3_ = bf16[64,128]{1,0:T(8,128)(2,1)S(1)} collective-permute-done((bf16[64,128]{1,0:T(8,128)(2,1)S(1)}, bf16[64,128]{1,0:T(8,128)(2,1)S(1)}, u32[]{:S(2)}, u32[]{:S(2)}) %collective-permute-start.18) | collective-permute-done | bytes 16416 | tf_op jit(solution)/shard_map/ppermute | solution.py:439
  46.1 1.5 %finish.1 = (f32[16,8,128]{2,1,0:T(8,128)}, f32[8,128]{1,0:T(8,128)S(1)}) custom-call(bf16[64,128]{1,0:T(8,128)(2,1)S(1)} %multiply_convert_fusion.refs_0_, bf16[64,128]{1,0:T(8,128)(2,1)S(1)} %collective-permute-done.16.refs_1_, bf16[64,128]{1,0:T(8,128)(2,1)S(1)} %collective-permute-done.17.refs_2_, bf16[64,128]{1,0:T(8,128)(2,1)S(1)} %collective-permute-done.18.refs_3_, ...), custom_call_target="tpu_custom_call" | custom-call | bytes 3211264 | tf_op jit(solution)/shard_map/finish/pallas_call | solution.py:150
  48.2 3.7 %all-to-all-start = ((f32[16,8,128]{2,1,0:T(8,128)}), f32[16,8,128]{2,1,0:T(8,128)S(1)}, u32[]{:S(2)}, u32[]{:S(2)}) async-start(f32[16,8,128]{2,1,0:T(8,128)} %get-tuple-element.43), calls=%async_computation | async-start | bytes 131072 | tf_op jit(solution)/shard_map/all_to_all | solution.py:470
  51.9 3.1 %score_rows.1 = (f32[256,128]{1,0:T(8,128)}, f32[8,128]{1,0:T(8,128)S(1)}) custom-call(bf16[64,4096]{1,0:T(8,128)(2,1)S(1)} %copy-done.1, bf16[64,4096]{1,0:T(8,128)(2,1)} %collective-permute-done.21.refs_1_, bf16[64,4096]{1,0:T(8,128)(2,1)S(1)} %collective-permute-done.20.refs_7_.refs_2_, bf16[64,4096]{1,0:T(8,128)(2,1)} %collective-permute-done.22.refs_3_, ...), custom_call_target="tpu_custom_call" | custom-call | bytes 4194320 | tf_op jit(solution)/shard_map/score_rows/pallas_call | solution.py:150
  55.1 4.3 %all-to-all-done.refs_0_ = f32[16,8,128]{2,1,0:T(8,128)S(1)} async-done(((f32[16,8,128]{2,1,0:T(8,128)}), f32[16,8,128]{2,1,0:T(8,128)S(1)}, u32[]{:S(2)}, u32[]{:S(2)}) %all-to-all-start) | async-done | bytes 65568 | tf_op jit(solution)/shard_map/all_to_all | solution.py:470
  59.4 0.7 %assemble.1 = (f32[2,512]{1,0:T(2,128)}, f32[8,64]{1,0:T(8,128)}) custom-call(f32[16,8,128]{2,1,0:T(8,128)S(1)} %all-to-all-done.refs_0_, f32[8,128]{1,0:T(8,128)S(1)} %get-tuple-element.44.refs_1_), custom_call_target="tpu_custom_call" | custom-call | bytes 65536 | tf_op jit(solution)/shard_map/assemble/pallas_call | solution.py:150
  (44 shorter events, 2.5 us)
Async XLA Ops:
  0.6 1.3 %copy-start = (bf16[1792,64]{0,1:T(8,128)(2,1)S(1)}, bf16[1792,64]{0,1:T(8,128)(2,1)}, u32[]{:S(2)}) copy-start(bf16[1792,64]{0,1:T(8,128)(2,1)} %param.12) | copy-start | bytes 688132
  0.6 20.8 %copy-start.5 = (bf16[2,32,4096]{2,1,0:T(8,128)(2,1)S(1)}, bf16[2,32,4096]{2,1,0:T(8,128)(2,1)}, u32[]{:S(2)}) copy-start(bf16[2,32,4096]{2,1,0:T(8,128)(2,1)} %param.10) | copy-start | bytes 1572868
  0.7 13.3 %collective-permute-start = (bf16[64,14336]{1,0:T(8,128)(2,1)}, bf16[64,14336]{1,0:T(8,128)(2,1)S(1)}, u32[]{:S(2)}, u32[]{:S(2)}) collective-permute-start(bf16[64,14336]{1,0:T(8,128)(2,1)} %bitcast.8), channel_id=1, source_target_pairs={{0,1},{1,0},{2,3},{3,2},{4,5},{5,4},{6,7},{7,6},{8,9},{9,8},{10,11... | collective-permute-start | bytes 5505032 | tf_op jit(solution)/shard_map/ppermute | solution.py:439
  1.2 12.7 %collective-permute-start.1 = (bf16[64,4096]{1,0:T(8,128)(2,1)}, bf16[64,4096]{1,0:T(8,128)(2,1)S(1)}, u32[]{:S(2)}, u32[]{:S(2)}) collective-permute-start(bf16[64,4096]{1,0:T(8,128)(2,1)} %bitcast.10), channel_id=1, source_target_pairs={{0,1},{1,0},{2,3},{3,2},{4,5},{5,4},{6,7},{7,6},{8,9},{9,8},{10,11... | collective-permute-start | bytes 1572872 | tf_op jit(solution)/shard_map/ppermute | solution.py:439
  2.0 19.5 %copy-start.3 = (bf16[2,32,14336]{2,1,0:T(8,128)(2,1)S(1)}, bf16[2,32,14336]{2,1,0:T(8,128)(2,1)}, u32[]{:S(2)}) copy-start(bf16[2,32,14336]{2,1,0:T(8,128)(2,1)} %param.9) | copy-start | bytes 5505028
  2.0 5.7 %collective-permute-start.2 = (bf16[32,1152]{1,0:T(8,128)(2,1)S(1)}, bf16[32,1152]{1,0:T(8,128)(2,1)S(1)}, u32[]{:S(2)}, u32[]{:S(2)}) collective-permute-start(bf16[32,1152]{1,0:T(8,128)(2,1)S(1)} %pad_maximum_fusion.refs_0_), channel_id=1, source_target_pairs={{0,8},{1,9},{2,10},{3,11},{4,12},{5,13},{6,14},{7,15},{8,0},{9,1},... | collective-permute-start | bytes 221192 | tf_op jit(solution)/shard_map/ppermute | solution.py:439
  5.1 8.0 %collective-permute-start.3 = (bf16[32,1152]{1,0:T(8,128)(2,1)S(1)}, bf16[32,1152]{1,0:T(8,128)(2,1)S(1)}, u32[]{:S(2)}, u32[]{:S(2)}) collective-permute-start(bf16[32,1152]{1,0:T(8,128)(2,1)S(1)} %pad_maximum_fusion.refs_0_), channel_id=1, source_target_pairs={{0,16},{1,17},{2,18},{3,19},{4,20},{5,21},{6,22},{7,23},{8,24},{9,... | collective-permute-start | bytes 221192 | tf_op jit(solution)/shard_map/ppermute | solution.py:439
  7.7 6.3 %collective-permute-start.4 = (bf16[32,1152]{1,0:T(8,128)(2,1)S(1)}, bf16[32,1152]{1,0:T(8,128)(2,1)S(1)}, u32[]{:S(2)}, u32[]{:S(2)}) collective-permute-start(bf16[32,1152]{1,0:T(8,128)(2,1)S(1)} %pad_maximum_fusion.refs_0_), channel_id=1, source_target_pairs={{0,24},{1,25},{2,26},{3,27},{4,28},{5,29},{6,30},{7,31},{8,16},{9,... | collective-permute-start | bytes 221192 | tf_op jit(solution)/shard_map/ppermute | solution.py:439
  7.7 6.3 %collective-permute-start.5 = (bf16[32,1152]{1,0:T(8,128)(2,1)S(1)}, bf16[32,1152]{1,0:T(8,128)(2,1)S(1)}, u32[]{:S(2)}, u32[]{:S(2)}) collective-permute-start(bf16[32,1152]{1,0:T(8,128)(2,1)S(1)} %pad_maximum_fusion.refs_0_), channel_id=1, source_target_pairs={{0,6},{1,7},{2,4},{3,5},{4,2},{5,3},{6,0},{7,1},{8,14},{9,15},{10,... | collective-permute-start | bytes 221192 | tf_op jit(solution)/shard_map/ppermute | solution.py:439
  14.0 7.5 %collective-permute-start.6 = (bf16[4,32,1152]{2,1,0:T(8,128)(2,1)S(1)}, bf16[4,32,1152]{2,1,0:T(8,128)(2,1)S(1)}, u32[]{:S(2)}, u32[]{:S(2)}) collective-permute-start(bf16[4,32,1152]{2,1,0:T(8,128)(2,1)S(1)} %stack.1.refs_4_), channel_id=1, source_target_pairs={{0,2},{1,3},{2,0},{3,1},{4,6},{5,7},{6,4},{7,5},{8,10},{9,11},{10,... | collective-permute-start | bytes 884744 | tf_op jit(solution)/shard_map/ppermute | solution.py:439
  15.5 10.3 %collective-permute-start.7 = (bf16[4,32,1152]{2,1,0:T(8,128)(2,1)S(1)}, bf16[4,32,1152]{2,1,0:T(8,128)(2,1)S(1)}, u32[]{:S(2)}, u32[]{:S(2)}) collective-permute-start(bf16[4,32,1152]{2,1,0:T(8,128)(2,1)S(1)} %stack.1.refs_4_), channel_id=1, source_target_pairs={{0,4},{1,5},{2,6},{3,7},{4,0},{5,1},{6,2},{7,3},{8,12},{9,13},{10,... | collective-permute-start | bytes 884744 | tf_op jit(solution)/shard_map/ppermute | solution.py:439
  17.0 6.7 %collective-permute-start.10 = (bf16[32,1152]{1,0:T(8,128)(2,1)S(1)}, bf16[32,1152]{1,0:T(8,128)(2,1)S(1)}, u32[]{:S(2)}, u32[]{:S(2)}) collective-permute-start(bf16[32,1152]{1,0:T(8,128)(2,1)S(1)} %collective-permute-done.5.refs_6_.refs_4_), channel_id=1, source_target_pairs={{0,24},{1,25},{2,26},{3,27},{4,28},{5,29},{6,30},{7,31},{8,16},{9,... | collective-permute-start | bytes 221192 | tf_op jit(solution)/shard_map/ppermute | solution.py:439
  20.6 4.4 %collective-permute-start.8 = (bf16[32,1152]{1,0:T(8,128)(2,1)S(1)}, bf16[32,1152]{1,0:T(8,128)(2,1)S(1)}, u32[]{:S(2)}, u32[]{:S(2)}) collective-permute-start(bf16[32,1152]{1,0:T(8,128)(2,1)S(1)} %collective-permute-done.5.refs_6_.refs_4_), channel_id=1, source_target_pairs={{0,8},{1,9},{2,10},{3,11},{4,12},{5,13},{6,14},{7,15},{8,0},{9,1},... | collective-permute-start | bytes 221192 | tf_op jit(solution)/shard_map/ppermute | solution.py:439
  20.6 5.3 %collective-permute-start.9 = (bf16[32,1152]{1,0:T(8,128)(2,1)S(1)}, bf16[32,1152]{1,0:T(8,128)(2,1)S(1)}, u32[]{:S(2)}, u32[]{:S(2)}) collective-permute-start(bf16[32,1152]{1,0:T(8,128)(2,1)S(1)} %collective-permute-done.5.refs_6_.refs_4_), channel_id=1, source_target_pairs={{0,16},{1,17},{2,18},{3,19},{4,20},{5,21},{6,22},{7,23},{8,24},{9,... | collective-permute-start | bytes 221192 | tf_op jit(solution)/shard_map/ppermute | solution.py:439
  22.8 5.0 %copy-start.6 = (s32[2,32]{1,0:T(2,128)S(1)}, s32[2,32]{1,0:T(2,128)}, u32[]{:S(2)}) copy-start(s32[2,32]{1,0:T(2,128)} %refs_2_.1) | copy-start | bytes 772
  22.8 5.3 %copy-start.4 = (bf16[128,4096]{1,0:T(8,128)(2,1)S(1)}, bf16[128,4096]{1,0:T(8,128)(2,1)}, u32[]{:S(2)}) copy-start(bf16[128,4096]{1,0:T(8,128)(2,1)} %refs_4_.2) | copy-start | bytes 3145732
  22.8 5.5 %copy-start.1 = (bf16[64,4096]{1,0:T(8,128)(2,1)S(1)}, bf16[64,4096]{1,0:T(8,128)(2,1)}, u32[]{:S(2)}) copy-start(bf16[64,4096]{1,0:T(8,128)(2,1)} %refs_0_.1) | copy-start | bytes 1572868
  26.5 25.4 %copy-start.2 = (f32[128,4096]{1,0:T(8,128)S(1)}, f32[128,4096]{1,0:T(8,128)}, u32[]{:S(2)}) copy-start(f32[128,4096]{1,0:T(8,128)} %refs_4_.3) | copy-start | bytes 6291460
  26.5 25.4 %copy-start.7 = (s32[4,1]{0,1:T(1,128)S(1)}, s32[4,1]{0,1:T(1,128)}, u32[]{:S(2)}) copy-start(s32[4,1]{0,1:T(1,128)} %param.17) | copy-start | bytes 52
  26.5 1.3 %collective-permute-start.11 = (f32[64,128]{1,0:T(8,128)S(1)}, f32[64,128]{1,0:T(8,128)S(1)}, u32[]{:S(2)}, u32[]{:S(2)}) collective-permute-start(f32[64,128]{1,0:T(8,128)S(1)} %get-tuple-element.29), channel_id=1, source_target_pairs={{0,1},{1,0},{2,3},{3,2},{4,5},{5,4},{6,7},{7,6},{8,9},{9,8},{10,11... | collective-permute-start | bytes 98312 | tf_op jit(solution)/shard_map/ppermute | solution.py:439
  28.1 18.0 %collective-permute-start.19 = (bf16[128,4096]{1,0:T(8,128)(2,1)S(1)}, bf16[128,4096]{1,0:T(8,128)(2,1)S(1)}, u32[]{:S(2)}, u32[]{:S(2)}) collective-permute-start(bf16[128,4096]{1,0:T(8,128)(2,1)S(1)} %copy-done.4), channel_id=1, source_target_pairs={{0,1},{1,0},{2,3},{3,2},{4,5},{5,4},{6,7},{7,6},{8,9},{9,8},{10,11... | collective-permute-start | bytes 3145736 | tf_op jit(solution)/shard_map/ppermute | solution.py:439
  28.3 17.8 %collective-permute-start.20 = (bf16[64,4096]{1,0:T(8,128)(2,1)S(1)}, bf16[64,4096]{1,0:T(8,128)(2,1)S(1)}, u32[]{:S(2)}, u32[]{:S(2)}) collective-permute-start(bf16[64,4096]{1,0:T(8,128)(2,1)S(1)} %copy-done.1), channel_id=1, source_target_pairs={{0,2},{1,3},{2,0},{3,1},{4,6},{5,7},{6,4},{7,5},{8,10},{9,11},{10,... | collective-permute-start | bytes 1572872 | tf_op jit(solution)/shard_map/ppermute | solution.py:439
  28.8 4.4 %collective-permute-start.12 = (f32[64,128]{1,0:T(8,128)S(1)}, f32[64,128]{1,0:T(8,128)S(1)}, u32[]{:S(2)}, u32[]{:S(2)}) collective-permute-start(f32[64,128]{1,0:T(8,128)S(1)} %get-tuple-element.30.refs_0_), channel_id=1, source_target_pairs={{0,8},{1,9},{2,10},{3,11},{4,12},{5,13},{6,14},{7,15},{8,0},{9,1},... | collective-permute-start | bytes 98312 | tf_op jit(solution)/shard_map/ppermute | solution.py:439
  30.8 5.1 %collective-permute-start.13 = (f32[64,128]{1,0:T(8,128)S(1)}, f32[64,128]{1,0:T(8,128)S(1)}, u32[]{:S(2)}, u32[]{:S(2)}) collective-permute-start(f32[64,128]{1,0:T(8,128)S(1)} %get-tuple-element.30.refs_0_), channel_id=1, source_target_pairs={{0,16},{1,17},{2,18},{3,19},{4,20},{5,21},{6,22},{7,23},{8,24},{9,... | collective-permute-start | bytes 98312 | tf_op jit(solution)/shard_map/ppermute | solution.py:439
  31.0 5.7 %collective-permute-start.14 = (f32[64,128]{1,0:T(8,128)S(1)}, f32[64,128]{1,0:T(8,128)S(1)}, u32[]{:S(2)}, u32[]{:S(2)}) collective-permute-start(f32[64,128]{1,0:T(8,128)S(1)} %get-tuple-element.30.refs_0_), channel_id=1, source_target_pairs={{0,24},{1,25},{2,26},{3,27},{4,28},{5,29},{6,30},{7,31},{8,16},{9,... | collective-permute-start | bytes 98312 | tf_op jit(solution)/shard_map/ppermute | solution.py:439
  37.4 3.9 %collective-permute-start.15 = (f32[64,128]{1,0:T(8,128)S(1)}, f32[64,128]{1,0:T(8,128)S(1)}, u32[]{:S(2)}, u32[]{:S(2)}) collective-permute-start(f32[64,128]{1,0:T(8,128)S(1)} %get-tuple-element.31), channel_id=1, source_target_pairs={{0,4},{1,5},{2,6},{3,7},{4,0},{5,1},{6,2},{7,3},{8,12},{9,13},{10,... | collective-permute-start | bytes 98312 | tf_op jit(solution)/shard_map/ppermute | solution.py:439
  41.3 1.9 %collective-permute-start.16 = (bf16[64,128]{1,0:T(8,128)(2,1)S(1)}, bf16[64,128]{1,0:T(8,128)(2,1)S(1)}, u32[]{:S(2)}, u32[]{:S(2)}) collective-permute-start(bf16[64,128]{1,0:T(8,128)(2,1)S(1)} %multiply_convert_fusion.refs_0_), channel_id=1, source_target_pairs={{0,1},{1,0},{2,3},{3,2},{4,5},{5,4},{6,7},{7,6},{8,9},{9,8},{10,11... | collective-permute-start | bytes 49160 | tf_op jit(solution)/shard_map/ppermute | solution.py:439
  41.4 3.8 %collective-permute-start.17 = (bf16[64,128]{1,0:T(8,128)(2,1)S(1)}, bf16[64,128]{1,0:T(8,128)(2,1)S(1)}, u32[]{:S(2)}, u32[]{:S(2)}) collective-permute-start(bf16[64,128]{1,0:T(8,128)(2,1)S(1)} %multiply_convert_fusion.refs_0_), channel_id=1, source_target_pairs={{0,2},{1,3},{2,0},{3,1},{4,6},{5,7},{6,4},{7,5},{8,10},{9,11},{10,... | collective-permute-start | bytes 49160 | tf_op jit(solution)/shard_map/ppermute | solution.py:439
  42.9 3.2 %collective-permute-start.18 = (bf16[64,128]{1,0:T(8,128)(2,1)S(1)}, bf16[64,128]{1,0:T(8,128)(2,1)S(1)}, u32[]{:S(2)}, u32[]{:S(2)}) collective-permute-start(bf16[64,128]{1,0:T(8,128)(2,1)S(1)} %multiply_convert_fusion.refs_0_), channel_id=1, source_target_pairs={{0,3},{1,2},{2,1},{3,0},{4,7},{5,6},{6,5},{7,4},{8,11},{9,10},{10,... | collective-permute-start | bytes 49160 | tf_op jit(solution)/shard_map/ppermute | solution.py:439
  47.6 4.3 %collective-permute-start.21 = (bf16[64,4096]{1,0:T(8,128)(2,1)S(1)}, bf16[64,4096]{1,0:T(8,128)(2,1)}, u32[]{:S(2)}, u32[]{:S(2)}) collective-permute-start(bf16[64,4096]{1,0:T(8,128)(2,1)S(1)} %copy-done.1), channel_id=1, source_target_pairs={{0,1},{1,0},{2,3},{3,2},{4,5},{5,4},{6,7},{7,6},{8,9},{9,8},{10,11... | collective-permute-start | bytes 1572872 | tf_op jit(solution)/shard_map/ppermute | solution.py:439
  47.8 4.1 %collective-permute-start.22 = (bf16[64,4096]{1,0:T(8,128)(2,1)S(1)}, bf16[64,4096]{1,0:T(8,128)(2,1)}, u32[]{:S(2)}, u32[]{:S(2)}) collective-permute-start(bf16[64,4096]{1,0:T(8,128)(2,1)S(1)} %collective-permute-done.20.refs_7_.refs_2_), channel_id=1, source_target_pairs={{0,1},{1,0},{2,3},{3,2},{4,5},{5,4},{6,7},{7,6},{8,9},{9,8},{10,11... | collective-permute-start | bytes 1572872 | tf_op jit(solution)/shard_map/ppermute | solution.py:439
  48.2 11.2 %all-to-all-start = ((f32[16,8,128]{2,1,0:T(8,128)}), f32[16,8,128]{2,1,0:T(8,128)S(1)}, u32[]{:S(2)}, u32[]{:S(2)}) async-start(f32[16,8,128]{2,1,0:T(8,128)} %get-tuple-element.43), calls=%async_computation | async-start | bytes 131072 | tf_op jit(solution)/shard_map/all_to_all | solution.py:470
